TPU v7x, 32 devices: a whole 2x2x4 slice. The times are simulated.
32 devices in a mesh: seq: 8 (over z, core), mp: 4 (over y, x).
Axes of the slice: x: 2, y: 2, z: 4, core: 2. Of those that a mesh axis runs over, the one named last changes fastest.
Arguments:
- tokens: bfloat16 [2, 2, 2048, 2048], P(None, None, 'seq'), may hold values from -6 to 6
- query_weight: bfloat16 [2048, 2048], P('seq', 'mp'), may hold values from -0.125 to 0.125
- query_bias: bfloat16 [2048], P(('mp', 'seq')), may hold values from -1.75 to 1.75
- key_weight: bfloat16 [2048, 2048], P('seq', 'mp'), may hold values from -0.125 to 0.125
- value_weight: bfloat16 [2048, 2048], P('seq', 'mp'), may hold values from -0.125 to 0.125
- value_bias: bfloat16 [2048], P(('mp', 'seq')), may hold values from -0.125 to 0.125
- proj_weight: bfloat16 [2048, 2048], P('mp', 'seq'), may hold values from -3.5 to 3.5
- proj_bias: bfloat16 [2048], P('seq'), may hold values from -1.75 to 1.75
- gain_first: bfloat16 [2048], P('seq'), may hold values from 0.5 to 1.5
- shift_first: bfloat16 [2048], P('seq'), may hold values from -1.75 to 1.75
- inner_weight: bfloat16 [2048, 8192], P('seq', 'mp'), may hold values from -0.125 to 0.125
- inner_bias: bfloat16 [8192], P(('mp', 'seq')), may hold values from -1.75 to 1.75
- outer_weight: bfloat16 [8192, 2048], P('mp', 'seq'), may hold values from -0.0625 to 0.0625
- outer_bias: bfloat16 [2048], P('seq'), may hold values from -1.75 to 1.75
- gain_second: bfloat16 [2048], P('seq'), may hold values from 0.5 to 1.5
- shift_second: bfloat16 [2048], P('seq'), may hold values from -1.75 to 1.75
- cotangent: bfloat16 [2, 2, 2048, 2048], P(None, None, 'seq'), may hold values from -6 to 6
Outputs:
- layer_out: bfloat16 [2, 2, 2048, 2048], P(None, None, 'seq')
- input_grad: float32 [2, 2, 2048, 2048], P(None, None, 'seq')
- query_weight_grad: float32 [2048, 2048], P('seq', 'mp')
- query_bias_grad: float32 [2048], P(('mp', 'seq'))
- key_weight_grad: float32 [2048, 2048], P('seq', 'mp')
- value_weight_grad: float32 [2048, 2048], P('seq', 'mp')
- value_bias_grad: float32 [2048], P(('mp', 'seq'))
- proj_weight_grad: float32 [2048, 2048], P('mp', 'seq')
- proj_bias_grad: float32 [2048], P('seq')
- gain_first_grad: float32 [2048], P('seq')
- shift_first_grad: float32 [2048], P('seq')
- inner_weight_grad: float32 [2048, 8192], P('seq', 'mp')
- inner_bias_grad: float32 [8192], P(('mp', 'seq'))
- outer_weight_grad: float32 [8192, 2048], P('mp', 'seq')
- outer_bias_grad: float32 [2048], P('seq')
- second_gain_gradient: float32 [2048], P('seq')
- shift_second_grad: float32 [2048], P('seq')
All inputs are finite; a program needn't handle non-finite values.
Results may differ from a plain program's by a relative error of at most 0.024.
Values may be sent and summed in bfloat16 or wider, within the bound.
A program may use at most 256 MiB of HBM per device.

v0:
```python
import jax
import jax.numpy as jnp
from jax import lax
from jax.sharding import PartitionSpec as P

DH = 128


EPSILON = 1e-06


def layer_norm(values, gain, shift):
    centre = values - jnp.mean(values, axis=-1, keepdims=True)
    spread = jnp.mean(centre * centre, axis=-1, keepdims=True)
    return centre * lax.rsqrt(spread + EPSILON) * gain + shift


def gelu_tanh(values):
    return jax.nn.gelu(values, approximate=True)


def matmul(left, right):
    return jnp.dot(left, right, preferred_element_type=jnp.float32)


def over_rows(left, right):
    return lax.dot_general(
        left, right, (((0,), (0,)), ((), ())), preferred_element_type=jnp.float32
    )


def over_cols(left, right):
    return lax.dot_general(
        left, right, (((1,), (1,)), ((), ())), preferred_element_type=jnp.float32
    )


def add_trees(first_tree, second_tree):
    return tuple((left + right for left, right in zip(first_tree, second_tree)))


def gather_forward(shards):
    return (
        lax.all_gather(shards[0], "seq", axis=0, tiled=True),
        lax.all_gather(shards[1], "seq", axis=0, tiled=True),
        lax.all_gather(shards[2], "seq", axis=0, tiled=True),
        lax.all_gather(shards[3], "seq", axis=0, tiled=True),
        lax.all_gather(shards[4], "seq", axis=0, tiled=True),
        lax.all_gather(shards[5], "seq", axis=1, tiled=True),
        lax.all_gather(shards[6], "seq", axis=0, tiled=True),
        lax.all_gather(shards[7], "seq", axis=0, tiled=True),
        lax.all_gather(shards[8], "seq", axis=0, tiled=True),
        lax.all_gather(shards[9], "seq", axis=0, tiled=True),
        lax.all_gather(shards[10], "seq", axis=0, tiled=True),
        lax.all_gather(shards[11], "seq", axis=1, tiled=True),
        lax.all_gather(shards[12], "seq", axis=0, tiled=True),
        lax.all_gather(shards[13], "seq", axis=0, tiled=True),
        lax.all_gather(shards[14], "seq", axis=0, tiled=True),
    )


def gather_backward(shards):
    return (
        lax.all_gather(shards[0], "seq", axis=0, tiled=True),
        lax.all_gather(shards[2], "seq", axis=0, tiled=True),
        lax.all_gather(shards[3], "seq", axis=0, tiled=True),
        lax.all_gather(shards[5], "seq", axis=1, tiled=True),
        lax.all_gather(shards[9], "seq", axis=0, tiled=True),
        lax.all_gather(shards[11], "seq", axis=1, tiled=True),
        lax.all_gather(shards[7], "seq", axis=0, tiled=True),
        lax.all_gather(shards[13], "seq", axis=0, tiled=True),
    )


def reduce_end(gradients):
    return (
        lax.psum_scatter(
            gradients[0].astype(jnp.bfloat16), "seq", scatter_dimension=0, tiled=True
        ).astype(jnp.float32),
        lax.psum_scatter(
            gradients[1].astype(jnp.bfloat16), "seq", scatter_dimension=0, tiled=True
        ).astype(jnp.float32),
        lax.psum_scatter(
            gradients[2].astype(jnp.bfloat16), "seq", scatter_dimension=0, tiled=True
        ).astype(jnp.float32),
        lax.psum_scatter(
            gradients[3].astype(jnp.bfloat16), "seq", scatter_dimension=0, tiled=True
        ).astype(jnp.float32),
        lax.psum_scatter(
            gradients[4].astype(jnp.bfloat16), "seq", scatter_dimension=0, tiled=True
        ).astype(jnp.float32),
        lax.psum_scatter(
            gradients[5].astype(jnp.bfloat16), "seq", scatter_dimension=1, tiled=True
        ).astype(jnp.float32),
        lax.psum_scatter(
            gradients[6].astype(jnp.bfloat16), "seq", scatter_dimension=0, tiled=True
        ).astype(jnp.float32),
        lax.psum_scatter(
            gradients[7].astype(jnp.bfloat16), "seq", scatter_dimension=0, tiled=True
        ).astype(jnp.float32),
        lax.psum_scatter(
            gradients[8].astype(jnp.bfloat16), "seq", scatter_dimension=0, tiled=True
        ).astype(jnp.float32),
        lax.psum_scatter(
            gradients[9].astype(jnp.bfloat16), "seq", scatter_dimension=0, tiled=True
        ).astype(jnp.float32),
        lax.psum_scatter(
            gradients[10].astype(jnp.bfloat16), "seq", scatter_dimension=0, tiled=True
        ).astype(jnp.float32),
        lax.psum_scatter(
            gradients[11].astype(jnp.bfloat16), "seq", scatter_dimension=1, tiled=True
        ).astype(jnp.float32),
        lax.psum_scatter(
            gradients[12].astype(jnp.bfloat16), "seq", scatter_dimension=0, tiled=True
        ).astype(jnp.float32),
        lax.psum_scatter(
            gradients[13].astype(jnp.bfloat16), "seq", scatter_dimension=0, tiled=True
        ).astype(jnp.float32),
        lax.psum_scatter(
            gradients[14].astype(jnp.bfloat16), "seq", scatter_dimension=0, tiled=True
        ).astype(jnp.float32),
    )


def attention_scores(query_low, gathered_key_rows, seq_count, head_count):
    query_matrix = query_low.reshape(seq_count, -1, head_count, DH)
    return jnp.einsum(
        "bcqa,buqa->bqcu", query_matrix, gathered_key_rows, preferred_element_type=jnp.float32
    ) * DH ** (-0.5)


def forward_pass(token_rows, gathered, seq_count):
    (
        w_query,
        b_query,
        w_key,
        w_value,
        b_value,
        w_proj,
        b_proj,
        gain_one,
        shift_one,
        w_inner,
        b_inner,
        w_outer,
        b_outer,
        gain_two,
        shift_two,
    ) = gathered
    head_count = w_query.shape[1] // DH
    local_len = token_rows.shape[0] // seq_count
    query_low = (matmul(token_rows, w_query) + b_query.astype(jnp.float32)).astype(jnp.bfloat16)
    key_local = (
        matmul(token_rows, w_key).astype(jnp.bfloat16).reshape(seq_count, local_len, head_count, DH)
    )
    value_local = (matmul(token_rows, w_value) + b_value.astype(jnp.float32)).astype(jnp.bfloat16)
    value_local = value_local.reshape(seq_count, local_len, head_count, DH)
    gathered_key_rows, gathered_value_rows = (
        lax.all_gather(key_local, "seq", axis=1, tiled=True),
        lax.all_gather(value_local, "seq", axis=1, tiled=True),
    )
    scores = attention_scores(query_low, gathered_key_rows, seq_count, head_count)
    row_max = jnp.max(scores, axis=-1, keepdims=True)
    exponent = jnp.exp(scores - row_max)
    row_total = jnp.sum(exponent, axis=-1, keepdims=True)
    log_total = row_max + jnp.log(row_total)
    probability_reduced = (exponent / row_total).astype(jnp.bfloat16)
    mixture = jnp.einsum(
        "tiaq,tqiz->taiz",
        probability_reduced,
        gathered_value_rows,
        preferred_element_type=jnp.float32,
    )
    mixture_low = mixture.astype(jnp.bfloat16).reshape(token_rows.shape[0], -1)
    attention = lax.psum(matmul(mixture_low, w_proj).astype(jnp.bfloat16), "mp").astype(
        jnp.float32
    ) + b_proj.astype(jnp.float32)
    first_in = token_rows.astype(jnp.float32) + attention
    first_out = layer_norm(first_in, gain_one.astype(jnp.float32), shift_one.astype(jnp.float32))
    first_low = first_out.astype(jnp.bfloat16)
    inner_pre = matmul(first_low, w_inner) + b_inner.astype(jnp.float32)
    active = gelu_tanh(inner_pre).astype(jnp.bfloat16)
    feed = lax.psum(matmul(active, w_outer).astype(jnp.bfloat16), "mp").astype(
        jnp.float32
    ) + b_outer.astype(jnp.float32)
    second_in = first_out + feed
    result = layer_norm(second_in, gain_two.astype(jnp.float32), shift_two.astype(jnp.float32))
    stored = (
        query_low,
        key_local,
        value_local,
        gathered_key_rows,
        gathered_value_rows,
        log_total,
        mixture,
        mixture_low,
        first_in,
        first_low,
        inner_pre,
        active,
        second_in,
    )
    return (result.astype(jnp.bfloat16), stored)


def backward_pass(token_rows, cotan_rows, gathered, stored, key_value, seq_count):
    w_query, w_key, w_value, w_proj, w_inner, w_outer, gain_one, gain_two = gathered
    (
        query_low,
        key_local,
        value_local,
        key_all_kept,
        value_all_kept,
        log_total,
        mixture,
        mixture_low,
        first_in,
        first_low,
        inner_pre,
        active,
        second_in,
    ) = stored
    gathered_key_rows, gathered_value_rows = key_value
    head_count = w_query.shape[1] // DH
    zero_shift = jnp.zeros((second_in.shape[-1],), jnp.float32)
    _, second_pullback = jax.vjp(layer_norm, second_in, gain_two.astype(jnp.float32), zero_shift)
    second_grad, gain_two_grad, shift_two_grad = second_pullback(cotan_rows.astype(jnp.float32))
    second_low = second_grad.astype(jnp.bfloat16)
    outer_w_grad = over_rows(active, second_low)
    outer_b_grad = jnp.sum(second_grad, axis=0)
    active_grad = over_cols(second_low, w_outer)
    _, pull_gelu = jax.vjp(gelu_tanh, inner_pre)
    inner_grad = pull_gelu(active_grad)[0].astype(jnp.bfloat16)
    inner_w_grad = over_rows(first_low, inner_grad)
    inner_b_grad = jnp.sum(inner_grad.astype(jnp.float32), axis=0)
    first_grad = (
        lax.psum(over_cols(inner_grad, w_inner).astype(jnp.bfloat16), "mp").astype(jnp.float32)
        + second_grad
    )
    _, pull_one = jax.vjp(layer_norm, first_in, gain_one.astype(jnp.float32), zero_shift)
    attn_grad, gain_one_grad, shift_one_grad = pull_one(first_grad)
    attn_low = attn_grad.astype(jnp.bfloat16)
    proj_w_grad = over_rows(mixture_low, attn_low)
    proj_b_grad = jnp.sum(attn_grad, axis=0)
    attention_mixture_gradient = (
        over_cols(attn_low, w_proj).astype(jnp.bfloat16).reshape(seq_count, -1, head_count, DH)
    )
    scores = attention_scores(query_low, gathered_key_rows, seq_count, head_count)
    probs = jnp.exp(scores - log_total)
    prob_grad = jnp.einsum(
        "bcqa,buqa->bqcu",
        attention_mixture_gradient,
        gathered_value_rows,
        preferred_element_type=jnp.float32,
    )
    row_terms = jnp.einsum(
        "srhd,srhd->shr", attention_mixture_gradient.astype(jnp.float32), mixture
    )
    score_gradient = (probs * (prob_grad - row_terms[..., None]) * DH ** (-0.5)).astype(
        jnp.bfloat16
    )
    query_matrix = query_low.reshape(seq_count, -1, head_count, DH)
    query_grad = jnp.einsum(
        "tiaq,tqiz->taiz", score_gradient, gathered_key_rows, preferred_element_type=jnp.float32
    )
    query_grad = query_grad.astype(jnp.bfloat16).reshape(token_rows.shape[0], -1)
    value_full_grad = jnp.einsum(
        "ejkp,ekjz->epjz",
        probs.astype(jnp.bfloat16),
        attention_mixture_gradient,
        preferred_element_type=jnp.float32,
    )
    key_full_grad = jnp.einsum(
        "ejkp,ekjz->epjz", score_gradient, query_matrix, preferred_element_type=jnp.float32
    )
    key_share, value_share = (
        lax.psum_scatter(
            key_full_grad.astype(jnp.bfloat16), "seq", scatter_dimension=1, tiled=True
        ).astype(jnp.float32),
        lax.psum_scatter(
            value_full_grad.astype(jnp.bfloat16), "seq", scatter_dimension=1, tiled=True
        ).astype(jnp.float32),
    )
    key_grad = key_share.astype(jnp.bfloat16).reshape(token_rows.shape[0], -1)
    value_grad = value_share.astype(jnp.bfloat16).reshape(token_rows.shape[0], -1)
    query_w_grad = over_rows(token_rows, query_grad)
    query_b_grad = jnp.sum(query_grad.astype(jnp.float32), axis=0)
    key_w_grad = over_rows(token_rows, key_grad)
    value_w_grad = over_rows(token_rows, value_grad)
    value_b_grad = jnp.sum(value_grad.astype(jnp.float32), axis=0)
    across_heads = (
        over_cols(query_grad, w_query) + over_cols(key_grad, w_key) + over_cols(value_grad, w_value)
    )
    input_rows = lax.psum(across_heads.astype(jnp.bfloat16), "mp").astype(jnp.float32) + attn_grad
    gradients = (
        query_w_grad,
        query_b_grad,
        key_w_grad,
        value_w_grad,
        value_b_grad,
        proj_w_grad,
        proj_b_grad,
        gain_one_grad,
        shift_one_grad,
        inner_w_grad,
        inner_b_grad,
        outer_w_grad,
        outer_b_grad,
        gain_two_grad,
        shift_two_grad,
    )
    return (input_rows, gradients)


def on_device(
    tokens,
    query_weight,
    query_bias,
    key_weight,
    value_weight,
    value_bias,
    proj_weight,
    proj_bias,
    gain_first,
    shift_first,
    inner_weight,
    inner_bias,
    outer_weight,
    outer_bias,
    gain_second,
    shift_second,
    cotangent,
):
    shards = (
        query_weight,
        query_bias,
        key_weight,
        value_weight,
        value_bias,
        proj_weight,
        proj_bias,
        gain_first,
        shift_first,
        inner_weight,
        inner_bias,
        outer_weight,
        outer_bias,
        gain_second,
        shift_second,
    )
    micro_count, seq_count, local_len, width = tokens.shape
    outputs = []
    input_grads = []
    summed = None
    for micro_index in range(micro_count):
        token_rows = tokens[micro_index].reshape(seq_count * local_len, width)
        cotan_rows = cotangent[micro_index].reshape(seq_count * local_len, width)
        gathered = gather_forward(shards)
        result, stored = forward_pass(token_rows, gathered, seq_count)
        back_weights = gather_backward(shards)
        key_value = (
            lax.all_gather(stored[1], "seq", axis=1, tiled=True),
            lax.all_gather(stored[2], "seq", axis=1, tiled=True),
        )
        input_rows, gradients = backward_pass(
            token_rows, cotan_rows, back_weights, stored, key_value, seq_count
        )
        outputs.append(result.reshape(seq_count, local_len, width))
        input_grads.append(input_rows.reshape(seq_count, local_len, width))
        summed = gradients if summed is None else add_trees(summed, gradients)
    summed = reduce_end(summed)
    return (
        jnp.stack(outputs),
        jnp.stack(input_grads),
        summed[0],
        summed[1],
        summed[2],
        summed[3],
        summed[4],
        summed[5],
        summed[6],
        summed[7],
        summed[8],
        summed[9],
        summed[10],
        summed[11],
        summed[12],
        summed[13],
        summed[14],
    )


def solution(mesh):
    placed = (
        P(None, None, "seq", None),
        P("seq", "mp"),
        P(("mp", "seq")),
        P("seq", "mp"),
        P("seq", "mp"),
        P(("mp", "seq")),
        P("mp", "seq"),
        P("seq"),
        P("seq"),
        P("seq"),
        P("seq", "mp"),
        P(("mp", "seq")),
        P("mp", "seq"),
        P("seq"),
        P("seq"),
        P("seq"),
        P(None, None, "seq", None),
    )
    return jax.shard_map(
        on_device,
        mesh=mesh,
        in_specs=placed,
        out_specs=(
            P(None, None, "seq", None),
            P(None, None, "seq", None),
            P("seq", "mp"),
            P(("mp", "seq")),
            P("seq", "mp"),
            P("seq", "mp"),
            P(("mp", "seq")),
            P("mp", "seq"),
            P("seq"),
            P("seq"),
            P("seq"),
            P("seq", "mp"),
            P(("mp", "seq")),
            P("mp", "seq"),
            P("seq"),
            P("seq"),
            P("seq"),
        ),
        check_vma=False,
    )
```

profile of v0, /device:TPU:9, one launch (start us, length us, event | category | flops | bytes accessed | tf_op | source)
XLA Modules:
  0.0 1564.0 jit_solution(6395384455976822307)
XLA Ops:
  13.4 26.9 %all-gather.24.cloned.1.call-done = bf16[2048,512]{1,0:T(8,128)(2,1)} async-done(((bf16[256,512]{1,0:T(8,128)(2,1)}), bf16[2048,512]{1,0:T(8,128)(2,1)}) %all-gather.24.cloned.1.call-update) | async-done | bytes 2097168 | tf_op jit(solution)/shard_map/all_gather | solution.py:46
  57.2 13.6 all-gather.18.cloned.1.call-done
  84.5 16.5 %all-gather.22.cloned.1.call-done = bf16[2048,512]{1,0:T(8,128)(2,1)} async-done(((bf16[256,512]{1,0:T(8,128)(2,1)}), bf16[2048,512]{1,0:T(8,128)(2,1)}) %all-gather.22.cloned.1.call-update) | async-done | bytes 2097168 | tf_op jit(solution)/shard_map/all_gather | solution.py:44
  110.2 38.0 %all-gather.36.cloned.1.call-done = bf16[2,2048,4,128]{3,1,2,0:T(8,128)(2,1)} async-done(((bf16[2,256,4,128]{3,1,2,0:T(8,128)(2,1)}), bf16[2,2048,4,128]{3,1,2,0:T(8,128)(2,1)}) %all-gather.36.cloned.1.call-update) | async-done | bytes 4194320 | tf_op jit(solution)/shard_map/all_gather | solution.py:159
  162.8 34.3 %all-gather.34.cloned.1.call-done = bf16[2,2048,4,128]{1,3,2,0:T(8,128)(2,1)} async-done(((bf16[2,256,4,128]{1,3,2,0:T(8,128)(2,1)}), bf16[2,2048,4,128]{1,3,2,0:T(8,128)(2,1)}) %all-gather.34.cloned.1.call-update) | async-done | bytes 4194320 | tf_op jit(solution)/shard_map/all_gather | solution.py:160
  207.1 37.0 %all-gather.26.cloned.1.call-done = bf16[2,2048,4,128]{3,1,2,0:T(8,128)(2,1)} async-done(((bf16[2,256,4,128]{3,1,2,0:T(8,128)(2,1)}), bf16[2,2048,4,128]{3,1,2,0:T(8,128)(2,1)}) %all-gather.26.cloned.1.call-update) | async-done | bytes 4194320 | tf_op jit(solution)/shard_map/all_gather | solution.py:159
  264.1 29.1 %all-gather.20.cloned.1.call-done = bf16[2,2048,4,128]{1,3,2,0:T(8,128)(2,1)} async-done(((bf16[2,256,4,128]{1,3,2,0:T(8,128)(2,1)}), bf16[2,2048,4,128]{1,3,2,0:T(8,128)(2,1)}) %all-gather.20.cloned.1.call-update) | async-done | bytes 4194320 | tf_op jit(solution)/shard_map/all_gather | solution.py:160
  304.6 22.3 %all-gather.28.cloned.1.call-done = bf16[512,2048]{1,0:T(8,128)(2,1)} async-done(((bf16[512,256]{1,0:T(8,128)(2,1)}), bf16[512,2048]{1,0:T(8,128)(2,1)}) %all-gather.28.cloned.1.call-update) | async-done | bytes 2097168 | tf_op jit(solution)/shard_map/all_gather | solution.py:49
  342.5 11.7 all-gather.2
  373.1 62.0 %all-reduce.28.cloned.1.call-done = (bf16[512,2048]{1,0:T(8,128)(2,1)}, bf16[512,2048]{1,0:T(8,128)(2,1)}) async-done(((bf16[512,2048]{1,0:T(8,128)(2,1)}, bf16[512,2048]{1,0:T(8,128)(2,1)}), (bf16[512,2048]{1,0:T(8,128)(2,1)}, bf16[512,2048]{1,0:T(8,128)(2,1)})) %all-reduce.28.cloned.1.call-update) | async-done | bytes 4194320 | tf_op jit(solution)/shard_map/psum | solution.py:175
  444.7 71.7 %all-gather.30.cloned.1.call-done = bf16[2048,2048]{1,0:T(8,128)(2,1)} async-done(((bf16[256,2048]{1,0:T(8,128)(2,1)}), bf16[2048,2048]{1,0:T(8,128)(2,1)}) %all-gather.30.cloned.1.call-update) | async-done | bytes 8388624 | tf_op jit(solution)/shard_map/all_gather | solution.py:53
  516.4 11.3 fusion.115
  534.0 64.8 %all-gather.32.cloned.1.call-done = bf16[2048,2048]{1,0:T(8,128)(2,1)} async-done(((bf16[2048,256]{1,0:T(8,128)(2,1)}), bf16[2048,2048]{1,0:T(8,128)(2,1)}) %all-gather.32.cloned.1.call-update) | async-done | bytes 8388624 | tf_op jit(solution)/shard_map/all_gather | solution.py:55
  617.3 12.0 all-gather.6
  648.2 73.6 %all-reduce.26.cloned.1.call-done = (bf16[512,2048]{1,0:T(8,128)(2,1)}, bf16[512,2048]{1,0:T(8,128)(2,1)}) async-done(((bf16[512,2048]{1,0:T(8,128)(2,1)}, bf16[512,2048]{1,0:T(8,128)(2,1)}), (bf16[512,2048]{1,0:T(8,128)(2,1)}, bf16[512,2048]{1,0:T(8,128)(2,1)})) %all-reduce.26.cloned.1.call-update) | async-done | bytes 4194320 | tf_op jit(solution)/shard_map/psum | solution.py:183
  738.3 14.9 convert_reduce_fusion.3
  759.0 12.4 convert_reduce_fusion.2
  779.2 103.6 %all-reduce.24.cloned.1.call-done = (bf16[512,2048]{1,0:T(8,128)(2,1)}, bf16[512,2048]{1,0:T(8,128)(2,1)}) async-done(((bf16[512,2048]{1,0:T(8,128)(2,1)}, bf16[512,2048]{1,0:T(8,128)(2,1)}), (bf16[512,2048]{1,0:T(8,128)(2,1)}, bf16[512,2048]{1,0:T(8,128)(2,1)})) %all-reduce.24.cloned.1.call-update) | async-done | bytes 4194320 | tf_op jit(solution)/shard_map/psum | solution.py:237
  905.6 11.2 convert_bitcast_fusion
  922.1 11.6 convert_bitcast_fusion.2
  1023.3 43.0 %reduce-scatter.15.cloned.1.call-done = bf16[2,256,4,128]{1,3,2,0:T(8,128)(2,1)} async-done(((bf16[2,2048,4,128]{1,3,2,0:T(8,128)(2,1)}), bf16[2,256,4,128]{1,3,2,0:T(8,128)(2,1)}) %reduce-scatter.15.cloned.1.call-update) | async-done | bytes 524304 | tf_op jit(solution)/shard_map/reduce_scatter | solution.py:277
  1067.6 49.1 %reduce-scatter.11.cloned.1.call-done = bf16[2,256,4,128]{1,3,2,0:T(8,128)(2,1)} async-done(((bf16[2,2048,4,128]{1,3,2,0:T(8,128)(2,1)}), bf16[2,256,4,128]{1,3,2,0:T(8,128)(2,1)}) %reduce-scatter.11.cloned.1.call-update) | async-done | bytes 524304 | tf_op jit(solution)/shard_map/reduce_scatter | solution.py:277
  1124.3 14.8 fusion.107
  1139.1 17.6 %add_convert_fusion = bf16[2048,2048]{1,0:T(8,128)(2,1)} fusion(f32[2048,2048]{1,0:T(8,128)} %fusion.107, f32[512,2048]{1,0:T(8,128)} %copy-done.17, f32[512]{0:T(512)S(1)} %negate_multiply_fusion.1, f32[512,2048]{1,0:T(8,128)} %fusion.111, f32[2048]{0:T(1024)S(1)} %bitcast.274), kind=kOutput, calls=%fused_computation | convolution fusion | flops 4315938816 | bytes 33564672 | tf_op jit(solution)/shard_map/dot_general | solution.py:27
  1170.3 13.5 fusion.113
  1183.8 11.1 add_convert_fusion.1
  1206.2 16.6 %reduce-scatter.23.cloned.1.call-done = bf16[256,512]{0,1:T(8,128)(2,1)} async-done(((bf16[2048,512]{0,1:T(8,128)(2,1)}), bf16[256,512]{0,1:T(8,128)(2,1)}) %reduce-scatter.23.cloned.1.call-update) | async-done | bytes 262160 | tf_op jit(solution)/shard_map/reduce_scatter | solution.py:86
  1224.7 35.5 %reduce-scatter.21.cloned.1.call-done = bf16[256,512]{0,1:T(8,128)(2,1)} async-done(((bf16[2048,512]{0,1:T(8,128)(2,1)}), bf16[256,512]{0,1:T(8,128)(2,1)}) %reduce-scatter.21.cloned.1.call-update) | async-done | bytes 262160 | tf_op jit(solution)/shard_map/reduce_scatter | solution.py:83
  1262.1 93.1 %reduce-scatter.29.cloned.1.call-done = bf16[2048,256]{1,0:T(8,128)(2,1)} async-done(((bf16[2048,2048]{1,0:T(8,128)(2,1)}), bf16[2048,256]{1,0:T(8,128)(2,1)}) %reduce-scatter.29.cloned.1.call-update) | async-done | bytes 1048592 | tf_op jit(solution)/shard_map/reduce_scatter | solution.py:110
  1358.0 105.3 %all-reduce.22.cloned.1.call-done = (bf16[512,2048]{1,0:T(8,128)(2,1)}, bf16[512,2048]{1,0:T(8,128)(2,1)}) async-done(((bf16[512,2048]{1,0:T(8,128)(2,1)}, bf16[512,2048]{1,0:T(8,128)(2,1)}), (bf16[512,2048]{1,0:T(8,128)(2,1)}, bf16[512,2048]{1,0:T(8,128)(2,1)})) %all-reduce.22.cloned.1.call-update) | async-done | bytes 4194320 | tf_op jit(solution)/shard_map/psum | solution.py:294
  1471.4 22.4 %all-reduce.11 = (bf16[512]{0:T(512)(128)(2,1)S(1)}, bf16[512]{0:T(512)(128)(2,1)S(1)}, bf16[2048]{0:T(1024)(128)(2,1)S(1)}, bf16[2048]{0:T(1024)(128)(2,1)S(1)}...) all-reduce(bf16[512]{0:T(512)(128)(2,1)S(1)} %fusion.101, ...), channel_id=7, replica_groups=mesh['seq'=8,'mp'=4] {'seq'}, use_global_device_ids=true, to_apply=%region_35.0.clone | all-reduce | flops 15360 | bytes 61440
  1507.5 46.7 %reduce-scatter.27.cloned.1.call-done = bf16[256,2048]{1,0:T(8,128)(2,1)} async-done(((bf16[2048,2048]{1,0:T(8,128)(2,1)}), bf16[256,2048]{1,0:T(8,128)(2,1)}) %reduce-scatter.27.cloned.1.call-update) | async-done | bytes 1048592 | tf_op jit(solution)/shard_map/reduce_scatter | solution.py:104
  (379 shorter events, 398.8 us)
Async XLA Ops:
  7.2 33.1 %all-gather.24.cloned.1.call-start = ((), (), s32[]{:S(2)}) async-start(), calls=%async_computation.13 | async-start | bytes 2359296 | tf_op jit(solution)/shard_map/all_gather | solution.py:46
  7.9 62.8 %all-gather.18.cloned.1.call-start = ((), (), s32[]{:S(2)}) async-start(), calls=%async_computation.10 | async-start | bytes 2359296 | tf_op jit(solution)/shard_map/all_gather | solution.py:47
  8.7 92.4 %all-gather.22.cloned.1.call-start = ((), (), s32[]{:S(2)}) async-start(), calls=%async_computation.12 | async-start | bytes 2359296 | tf_op jit(solution)/shard_map/all_gather | solution.py:44
  9.4 138.8 %all-gather.36.cloned.1.call-start = ((), (), s32[]{:S(2)}) async-start(), calls=%async_computation.19 | async-start | bytes 4718592 | tf_op jit(solution)/shard_map/all_gather | solution.py:159
  13.4 426.2 %copy-start.3 = (bf16[1,2,256,2048]{3,2,1,0:T(8,128)(2,1)}, bf16[1,2,256,2048]{3,2,1,0:T(8,128)(2,1)S(1)}, u32[]{:S(2)}) copy-start(bf16[1,2,256,2048]{3,2,1,0:T(8,128)(2,1)S(1)} %get-tuple-element.131) | copy-start | bytes 6291460
  44.9 152.2 %all-gather.34.cloned.1.call-start = ((), (), s32[]{:S(2)}) async-start(), calls=%async_computation.18 | async-start | bytes 4718592 | tf_op jit(solution)/shard_map/all_gather | solution.py:160
  75.5 168.7 %all-gather.26.cloned.1.call-start = ((), (), s32[]{:S(2)}) async-start(), calls=%async_computation.14 | async-start | bytes 4718592 | tf_op jit(solution)/shard_map/all_gather | solution.py:159
  79.4 213.8 %all-gather.20.cloned.1.call-start = ((), (), s32[]{:S(2)}) async-start(), calls=%async_computation.11 | async-start | bytes 4718592 | tf_op jit(solution)/shard_map/all_gather | solution.py:160
  83.7 243.2 %all-gather.28.cloned.1.call-start = ((), (), s32[]{:S(2)}) async-start(), calls=%async_computation.15 | async-start | bytes 2359296 | tf_op jit(solution)/shard_map/all_gather | solution.py:49
  84.4 350.6 %all-reduce.28.cloned.1.call-start = ((), (), s32[]{:S(2)}) async-start(), calls=%async_computation.33 | async-start | bytes 8388608 | tf_op jit(solution)/shard_map/psum | solution.py:175
  104.3 139.9 %copy-start.30 = (bf16[2,256,4,128]{1,3,2,0:T(8,128)(2,1)}, bf16[2,256,4,128]{1,3,2,0:T(8,128)(2,1)S(1)}, u32[]{:S(2)}) copy-start(bf16[2,256,4,128]{1,3,2,0:T(8,128)(2,1)S(1)} %copy.92) | copy-start | bytes 1572868
  110.2 42.7 %copy-start.32 = (bf16[2,256,4,128]{1,3,2,0:T(8,128)(2,1)}, bf16[2,256,4,128]{1,3,2,0:T(8,128)(2,1)S(1)}, u32[]{:S(2)}) copy-start(bf16[2,256,4,128]{1,3,2,0:T(8,128)(2,1)S(1)} %copy.100) | copy-start | bytes 1572868
  152.9 44.1 %copy-start.49 = (f32[2,4,256]{2,1,0:T(4,128)}, f32[2,4,256]{2,1,0:T(4,128)S(1)}, u32[]{:S(2)}) copy-start(f32[2,4,256]{2,1,0:T(4,128)S(1)} %get-tuple-element.148) | copy-start | bytes 24580
  162.8 44.4 %copy-start.53 = (f32[2,4,256]{2,1,0:T(4,128)}, f32[2,4,256]{2,1,0:T(4,128)S(1)}, u32[]{:S(2)}) copy-start(f32[2,4,256]{2,1,0:T(4,128)S(1)} %fusion.1) | copy-start | bytes 24580
  256.2 70.7 %copy-start.43 = (bf16[2,256,4,128]{3,2,1,0:T(4,128)(2,1)}, bf16[2,256,4,128]{3,2,1,0:T(4,128)(2,1)S(1)}, u32[]{:S(2)}) copy-start(bf16[2,256,4,128]{3,2,1,0:T(4,128)(2,1)S(1)} %copy.87) | copy-start | bytes 1572868
  264.0 39.2 %copy-start.51 = (f32[2,4,256]{2,1,0:T(4,128)}, f32[2,4,256]{2,1,0:T(4,128)S(1)}, u32[]{:S(2)}) copy-start(f32[2,4,256]{2,1,0:T(4,128)S(1)} %fusion) | copy-start | bytes 24580
  333.9 182.6 %all-gather.30.cloned.1.call-start = ((), (), s32[]{:S(2)}) async-start(), calls=%async_computation.16 | async-start | bytes 9437184 | tf_op jit(solution)/shard_map/all_gather | solution.py:53
  334.5 264.4 %all-gather.32.cloned.1.call-start = ((), (), s32[]{:S(2)}) async-start(), calls=%async_computation.17 | async-start | bytes 9437184 | tf_op jit(solution)/shard_map/all_gather | solution.py:55
  335.2 386.6 %all-reduce.26.cloned.1.call-start = ((), (), s32[]{:S(2)}) async-start(), calls=%async_computation.32 | async-start | bytes 8388608 | tf_op jit(solution)/shard_map/psum | solution.py:183
  354.2 367.6 %copy-start.55 = (f32[8,1,256]{2,1,0:T(1,128)}, f32[8,1,256]{2,1,0:T(1,128)S(1)}, u32[]{:S(2)}) copy-start(f32[8,1,256]{2,1,0:T(1,128)S(1)} %convert_element_type.487) | copy-start | bytes 24580
  616.7 266.2 %all-reduce.24.cloned.1.call-start = ((), (), s32[]{:S(2)}) async-start(), calls=%async_computation.31 | async-start | bytes 8388608 | tf_op jit(solution)/shard_map/psum | solution.py:237
  778.5 226.6 %reduce-scatter.17.cloned.1.call-start = ((), (), s32[]{:S(2)}) async-start(), calls=%async_computation.23 | async-start | bytes 4718592 | tf_op jit(solution)/shard_map/reduce_scatter | solution.py:280
  916.8 99.1 %reduce-scatter.13.cloned.1.call-start = ((), (), s32[]{:S(2)}) async-start(), calls=%async_computation.21 | async-start | bytes 4718592 | tf_op jit(solution)/shard_map/reduce_scatter | solution.py:280
  933.7 132.6 %reduce-scatter.15.cloned.1.call-start = ((), (), s32[]{:S(2)}) async-start(), calls=%async_computation.22 | async-start | bytes 4718592 | tf_op jit(solution)/shard_map/reduce_scatter | solution.py:277
  955.2 161.5 %reduce-scatter.11.cloned.1.call-start = ((), (), s32[]{:S(2)}) async-start(), calls=%async_computation.20 | async-start | bytes 4718592 | tf_op jit(solution)/shard_map/reduce_scatter | solution.py:277
  974.9 227.4 %reduce-scatter.25.cloned.1.call-start = ((), (), s32[]{:S(2)}) async-start(), calls=%async_computation.27 | async-start | bytes 2359296 | tf_op jit(solution)/shard_map/reduce_scatter | solution.py:92
  982.3 221.7 %reduce-scatter.19.cloned.1.call-start = ((), (), s32[]{:S(2)}) async-start(), calls=%async_computation.24 | async-start | bytes 2359296 | tf_op jit(solution)/shard_map/reduce_scatter | solution.py:77
  1005.1 217.7 %reduce-scatter.23.cloned.1.call-start = ((), (), s32[]{:S(2)}) async-start(), calls=%async_computation.26 | async-start | bytes 2359296 | tf_op jit(solution)/shard_map/reduce_scatter | solution.py:86
  1023.2 237.0 %reduce-scatter.21.cloned.1.call-start = ((), (), s32[]{:S(2)}) async-start(), calls=%async_computation.25 | async-start | bytes 2359296 | tf_op jit(solution)/shard_map/reduce_scatter | solution.py:83
  1124.0 231.2 %reduce-scatter.29.cloned.1.call-start = ((), (), s32[]{:S(2)}) async-start(), calls=%async_computation.29 | async-start | bytes 9437184 | tf_op jit(solution)/shard_map/reduce_scatter | solution.py:110
  1156.7 306.5 %all-reduce.22.cloned.1.call-start = ((), (), s32[]{:S(2)}) async-start(), calls=%async_computation.30 | async-start | bytes 8388608 | tf_op jit(solution)/shard_map/psum | solution.py:294
  1169.6 384.6 %reduce-scatter.27.cloned.1.call-start = ((), (), s32[]{:S(2)}) async-start(), calls=%async_computation.28 | async-start | bytes 9437184 | tf_op jit(solution)/shard_map/reduce_scatter | solution.py:104
  (77 other events, 485.1 us)
Sparse Core Ops, SparseCore 0:
  9.6 30.6 all-gather.23
  41.9 28.8 all-gather.17
  72.4 28.6 all-gather.21
  103.1 45.0 all-gather.35
  150.2 46.8 all-gather.33
  199.1 45.0 all-gather.25
  246.3 46.7 all-gather.19
  294.7 32.1 all-gather.27
  334.0 101.0 all-reduce.27
  436.6 79.8 all-gather.29
  518.1 80.6 all-gather.31
  616.8 104.9 all-reduce.25
  778.7 104.1 all-reduce.23
  916.9 48.4 reduce-scatter.16
  967.7 48.1 reduce-scatter.12
  1018.1 48.1 reduce-scatter.14
  1068.5 48.1 reduce-scatter.10
  1119.0 30.7 reduce-scatter.24
  1152.2 34.2 reduce-scatter.18
  1188.7 34.0 reduce-scatter.22
  1225.8 34.3 reduce-scatter.20
  1263.2 91.9 reduce-scatter.28
  1359.2 104.0 all-reduce.21
  1465.4 88.6 reduce-scatter.26
where the time goes:
time: 1580 us; the launch traced here: 1560 us
  waiting for transfers between devices  997 us (63%)
  matrix products  299 us (19%)
  blocking collectives  101 us (6%)
  other arithmetic  89.6 us (6%)
  local copies, waits for them, and re-layouts  57.2 us (4%)
  between operations  17.8 us (1%)
    psum x1, waiting for transfers between devices, backward_pass(): lax.psum(across_heads.astype(jnp.bfloat16), 'mp').astype(jnp.float32)  105 us
    psum x1, waiting for transfers between devices, backward_pass(): lax.psum(over_cols(inner_grad, w_inner).astype(jnp.bfloat16), 'mp')  104 us
    reduce_scatter x1, waiting for transfers between devices, reduce_end(): lax.psum_scatter(gradients[11].astype(jnp.bfloat16), 'seq', scatter_dimen...  93.1 us
    reduce_scatter x2, waiting for transfers between devices, backward_pass(): lax.psum_scatter(key_full_grad.astype(jnp.bfloat16), 'seq', scatter_dimen...  92.1 us
    dot_general x12, matrix products, over_rows(): lax.dot_general(left, right, (((0,), (0,)), ((), ())), preferred_element_...  77.9 us
    all_gather x2, waiting for transfers between devices, forward_pass(): lax.all_gather(key_local, 'seq', axis=1, tiled=True)  75 us
    psum x1, waiting for transfers between devices, forward_pass(): lax.psum(matmul(active, w_outer).astype(jnp.bfloat16), 'mp')  73.6 us
    all_gather x1, waiting for transfers between devices, gather_forward(): lax.all_gather(shards[9], 'seq', axis=0, tiled=True)  71.7 us
  transfers between devices with their start and end apart: 24, of which 21 were waited for; matrix products, arithmetic and copies ran while one was open for 20% of the time, Pallas kernels for 0%

commit v1 on v0

v1 whole, which is shorter than its diff:
```python
import functools

import jax
import jax.numpy as jnp
from jax import lax
from jax.experimental import pallas as pl
from jax.experimental.pallas import tpu as pltpu
from jax.sharding import PartitionSpec as P

DH = 128
EPSILON = 1e-06
BF = jnp.bfloat16
F32 = jnp.float32
MESH = pl.DeviceIdType.MESH
ANY = pl.BlockSpec(memory_space=pl.ANY)
VMEM = pl.BlockSpec(memory_space=pltpu.VMEM)
MIB = 1 << 20


def matmul(left, right):
    return jnp.dot(left, right, preferred_element_type=F32)


def over_rows(left, right):
    return lax.dot_general(left, right, (((0,), (0,)), ((), ())), preferred_element_type=F32)


def over_cols(left, right):
    return lax.dot_general(left, right, (((1,), (1,)), ((), ())), preferred_element_type=F32)


def gelu_tanh(values):
    return jax.nn.gelu(values, approximate=True)


def square():
    me = lax.axis_index("mp")
    return me, me + 1 - 2 * lax.rem(me, 2), lax.rem(me + 2, 4), 3 - me


def greet(devices):
    barrier = pltpu.get_barrier_semaphore()
    for device in devices:
        pl.semaphore_signal(barrier, inc=1, device_id=device, device_id_type=MESH)
    pl.semaphore_wait(barrier, len(devices))


def sender(send_sem, recv_sem):
    def send(source, target, slot, device):
        copy = pltpu.make_async_remote_copy(
            src_ref=source,
            dst_ref=target,
            send_sem=send_sem.at[slot],
            recv_sem=recv_sem.at[slot],
            device_id=device,
            device_id_type=MESH,
        )
        copy.start()
        return copy

    return send


def sum_kernel(part_ref, out_ref, landed, relay, send_sem, recv_sem):
    me, along_x, along_y, across = square()
    greet([{"mp": along_x}, {"mp": along_y}])
    send = sender(send_sem, recv_sem)
    half = out_ref.shape[0] // 2
    upper, lower = pl.ds(0, half), pl.ds(half, half)
    copies = [
        send(part_ref.at[across, upper], landed.at[0], 0, {"mp": along_x}),
        send(part_ref.at[across, lower], landed.at[1], 1, {"mp": along_y}),
        send(part_ref.at[along_x, upper], landed.at[2], 2, {"mp": along_x}),
        send(part_ref.at[along_y, lower], landed.at[3], 3, {"mp": along_y}),
    ]
    copies[0].wait_recv()
    relay[0] = (part_ref[along_y, upper].astype(F32) + landed[0].astype(F32)).astype(BF)
    copies.append(send(relay.at[0], landed.at[4], 4, {"mp": along_y}))
    copies[1].wait_recv()
    relay[1] = (part_ref[along_x, lower].astype(F32) + landed[1].astype(F32)).astype(BF)
    copies.append(send(relay.at[1], landed.at[5], 5, {"mp": along_x}))
    copies[2].wait_recv()
    out_ref[upper] = part_ref[me, upper].astype(F32) + landed[2].astype(F32)
    copies[3].wait_recv()
    out_ref[lower] = part_ref[me, lower].astype(F32) + landed[3].astype(F32)
    copies[4].wait_recv()
    out_ref[upper] += landed[4].astype(F32)
    copies[5].wait_recv()
    out_ref[lower] += landed[5].astype(F32)
    for copy in copies:
        copy.wait_send()


def sum_over_mp(part, parts, ident):
    rows, width = part.shape
    mine = rows // parts
    if parts != 4:
        return lax.psum_scatter(part, "mp", scatter_dimension=0, tiled=True).astype(F32)
    return pl.pallas_call(
        sum_kernel,
        out_shape=jax.ShapeDtypeStruct((mine, width), F32),
        in_specs=[VMEM],
        out_specs=VMEM,
        scratch_shapes=[
            pltpu.VMEM((6, mine // 2, width), BF),
            pltpu.VMEM((2, mine // 2, width), BF),
            pltpu.SemaphoreType.DMA((6,)),
            pltpu.SemaphoreType.DMA((6,)),
        ],
        compiler_params=pltpu.CompilerParams(
            collective_id=ident, has_side_effects=True, vmem_limit_bytes=48 * MIB
        ),
        cost_estimate=pl.CostEstimate(flops=0, bytes_accessed=100 * MIB, transcendentals=0),
        name=f"sum_over_mp_{ident}",
    )(part.reshape(parts, mine, width))


def share_kernel(own_ref, all_ref, send_sem, recv_sem, local_sem):
    me, along_x, along_y, _ = square()
    to_x, to_y = {"mp": along_x}, {"mp": along_y}
    greet([to_x, to_y])
    send = sender(send_sem, recv_sem)
    half = own_ref.shape[0] // 2
    upper, lower = pl.ds(0, half), pl.ds(half, half)
    copies = [
        send(own_ref.at[upper], all_ref.at[me, upper], 0, to_x),
        send(own_ref.at[lower], all_ref.at[me, lower], 1, to_y),
        send(own_ref.at[lower], all_ref.at[me, lower], 2, to_x),
        send(own_ref.at[upper], all_ref.at[me, upper], 3, to_y),
    ]
    local = pltpu.make_async_copy(own_ref, all_ref.at[me], local_sem)
    local.start()
    copies[0].wait_recv()
    copies.append(send(all_ref.at[along_x, upper], all_ref.at[along_x, upper], 4, to_y))
    copies[1].wait_recv()
    copies.append(send(all_ref.at[along_y, lower], all_ref.at[along_y, lower], 5, to_x))
    for copy in copies[2:]:
        copy.wait_recv()
    for copy in copies:
        copy.wait_send()
    local.wait()


def share_over_mp(own, parts, ident):
    if parts != 4:
        return lax.all_gather(own, "mp", axis=0)
    return pl.pallas_call(
        share_kernel,
        out_shape=jax.ShapeDtypeStruct((parts,) + own.shape, own.dtype),
        in_specs=[ANY],
        out_specs=ANY,
        scratch_shapes=[
            pltpu.SemaphoreType.DMA((6,)),
            pltpu.SemaphoreType.DMA((6,)),
            pltpu.SemaphoreType.DMA,
        ],
        compiler_params=pltpu.CompilerParams(collective_id=ident, has_side_effects=True),
        cost_estimate=pl.CostEstimate(flops=0, bytes_accessed=100 * MIB, transcendentals=0),
        name=f"share_over_mp_{ident}",
    )(own)


def swap_kernel(groups, per, block_ref, out_ref, send_sem, recv_sem, local_sem):
    index = lax.axis_index("seq")
    group, place = index // per, lax.rem(index, per)
    targets = [lax.rem(group + step, groups) for step in range(groups)]
    devices = [{"seq": target * per + place} for target in targets]
    greet(devices[1:])
    send = sender(send_sem, recv_sem)
    copies = [
        send(block_ref.at[targets[step]], out_ref.at[group], step, devices[step])
        for step in range(1, groups)
    ]
    local = pltpu.make_async_copy(block_ref.at[group], out_ref.at[group], local_sem)
    local.start()
    local.wait()
    for copy in copies:
        copy.wait()


def swap_groups(blocks, per, parts, ident):
    groups = blocks.shape[0]
    if parts != 4:
        members = [[group * per + place for group in range(groups)] for place in range(per)]
        return lax.all_to_all(blocks, "seq", 0, 0, axis_index_groups=members)
    return pl.pallas_call(
        functools.partial(swap_kernel, groups, per),
        out_shape=jax.ShapeDtypeStruct(blocks.shape, blocks.dtype),
        in_specs=[ANY],
        out_specs=ANY,
        scratch_shapes=[
            pltpu.SemaphoreType.DMA((groups,)),
            pltpu.SemaphoreType.DMA((groups,)),
            pltpu.SemaphoreType.DMA,
        ],
        compiler_params=pltpu.CompilerParams(collective_id=ident, has_side_effects=True),
        cost_estimate=pl.CostEstimate(flops=0, bytes_accessed=60 * MIB, transcendentals=0),
        name=f"swap_groups_{ident}",
    )(blocks)


def normed(values):
    centre = values - jnp.mean(values, axis=-1, keepdims=True)
    spread = jnp.mean(centre * centre, axis=-1, keepdims=True)
    inverse = lax.rsqrt(spread + EPSILON)
    return centre * inverse, inverse


def norm_back(grad, normal, inverse, gain):
    inner = grad * gain
    moved = inverse * (
        inner
        - jnp.mean(inner, axis=-1, keepdims=True)
        - normal * jnp.mean(inner * normal, axis=-1, keepdims=True)
    )
    return moved, jnp.sum(grad * normal, axis=0), jnp.sum(grad, axis=0)


def around_group(block, members, per):
    blocks = [block]
    for step in range(1, per):
        pairs = [
            (base + place, base + (place - step) % per)
            for base in range(0, members, per)
            for place in range(per)
        ]
        blocks.append(lax.ppermute(block, "seq", pairs))
    return blocks


def group_sum(blocks, members, per):
    total = blocks[0]
    for step in range(1, per):
        pairs = [
            (base + place, base + (place + step) % per)
            for base in range(0, members, per)
            for place in range(per)
        ]
        total = total + lax.ppermute(blocks[step].astype(BF), "seq", pairs).astype(F32)
    return total


def on_device(members, parts, *arrays):
    (
        tokens,
        query_weight,
        query_bias,
        key_weight,
        value_weight,
        value_bias,
        proj_weight,
        proj_bias,
        gain_first,
        shift_first,
        inner_weight,
        inner_bias,
        outer_weight,
        outer_bias,
        gain_second,
        shift_second,
        cotangent,
    ) = arrays
    micro, seqs, length, width = tokens.shape
    groups = micro * seqs
    per = members // groups
    assert per * groups == members
    piece = length // parts
    rows = groups * length
    quarter = groups * piece
    mine = lax.axis_index("mp")

    depth, cols = query_weight.shape
    heads = cols // DH
    proj_fold = proj_weight.reshape(-1, depth, width // members)
    folds = proj_fold.shape[0]
    vectors = [
        query_bias,
        value_bias,
        inner_bias,
        proj_bias,
        gain_first,
        shift_first,
        outer_bias,
        gain_second,
        shift_second,
    ]
    sizes = [vector.shape[0] for vector in vectors]
    first_cols = 3 * cols + folds * (width // members)
    flat = jnp.concatenate(vectors)
    extra = 16
    flat = jnp.pad(flat, (0, extra * first_cols - flat.shape[0])).reshape(extra, first_cols)
    first = jnp.concatenate(
        [
            jnp.concatenate(
                [query_weight, key_weight, value_weight] + [proj_fold[i] for i in range(folds)], axis=1
            ),
            flat,
        ],
        axis=0,
    )
    first = lax.all_gather(first, "seq", axis=0)
    w_inner = lax.all_gather(inner_weight, "seq", axis=0, tiled=True)
    w_outer = lax.all_gather(outer_weight, "seq", axis=1, tiled=True)
    w_qkv = first[:, :depth, : 3 * cols].reshape(members * depth, 3 * cols)
    w_proj = first[:, :depth, 3 * cols :].reshape(members, depth, folds, width // members)
    w_proj = w_proj.transpose(2, 1, 0, 3).reshape(folds * depth, width)
    flat = first[:, depth:, :].reshape(members, -1)
    full = []
    start = 0
    for size in sizes:
        full.append(flat[:, start : start + size].reshape(-1).astype(F32))
        start += size
    b_query, b_value, b_inner, b_proj, gain_one, shift_one, b_outer, gain_two, shift_two = full

    def to_group(array, ident):
        blocks = lax.dynamic_slice_in_dim(
            array.reshape(groups, length, width), mine * piece, piece, axis=1
        )
        return swap_groups(blocks, per, parts, ident).reshape(quarter, width)

    def from_group(array, swap_id, share_id):
        blocks = swap_groups(array.reshape(groups, piece, width), per, parts, swap_id)
        every = share_over_mp(blocks.reshape(quarter, width), parts, share_id)
        every = every.reshape(parts, groups, piece, width).transpose(1, 0, 2, 3)
        return every.reshape(micro, seqs, length, width)

    x_part = to_group(tokens, 1)
    x_rows = share_over_mp(x_part, parts, 2).reshape(rows, width)
    cotan = to_group(cotangent, 3).astype(F32)

    bias = jnp.concatenate([b_query, jnp.zeros_like(b_query), b_value])
    qkv = (matmul(x_rows, w_qkv) + bias).astype(BF)
    query = qkv[:, :cols].reshape(rows, heads, DH)
    kv = jnp.concatenate(around_group(qkv[:, cols:], members, per), axis=0)
    keys = kv[:, :cols].reshape(per * rows, heads, DH)
    values = kv[:, cols:].reshape(per * rows, heads, DH)
    scale = DH ** (-0.5)

    def scores_of():
        return jnp.einsum("qhd,khd->hqk", query, keys, preferred_element_type=F32) * scale

    scores = scores_of()
    row_max = jnp.max(scores, axis=-1, keepdims=True)
    exponent = jnp.exp(scores - row_max)
    row_total = jnp.sum(exponent, axis=-1, keepdims=True)
    log_total = row_max + jnp.log(row_total)
    probs_low = (exponent / row_total).astype(BF)
    mixture = jnp.einsum("hqk,khd->qhd", probs_low, values, preferred_element_type=F32)
    mixture_low = mixture.astype(BF).reshape(rows, cols)
    first_in = (
        x_part.astype(F32)
        + sum_over_mp(matmul(mixture_low, w_proj).astype(BF), parts, 4)
        + b_proj
    )
    normal_one, inverse_one = normed(first_in)
    first_out = normal_one * gain_one + shift_one
    first_low = share_over_mp(first_out.astype(BF), parts, 5).reshape(rows, width)

    inner_pre = matmul(first_low, w_inner) + b_inner
    active = gelu_tanh(inner_pre).astype(BF)
    second_in = first_out + sum_over_mp(matmul(active, w_outer).astype(BF), parts, 6) + b_outer
    normal_two, inverse_two = normed(second_in)
    layer_out = (normal_two * gain_two + shift_two).astype(BF)
    second_grad, gain_two_grad, shift_two_grad = norm_back(cotan, normal_two, inverse_two, gain_two)
    outer_b_grad = jnp.sum(second_grad, axis=0)
    second_low = share_over_mp(second_grad.astype(BF), parts, 7).reshape(rows, width)

    outer_w_grad = lax.psum_scatter(
        over_rows(active, second_low).astype(BF), "seq", scatter_dimension=1, tiled=True
    )
    _, pull_gelu = jax.vjp(gelu_tanh, inner_pre)
    inner_grad = pull_gelu(over_cols(second_low, w_outer))[0].astype(BF)
    inner_w_grad = lax.psum_scatter(
        over_rows(first_low, inner_grad).astype(BF), "seq", scatter_dimension=0, tiled=True
    )
    inner_b_grad = jnp.sum(inner_grad.astype(F32), axis=0)
    first_grad = sum_over_mp(over_cols(inner_grad, w_inner).astype(BF), parts, 8) + second_grad
    attn_grad, gain_one_grad, shift_one_grad = norm_back(
        first_grad, normal_one, inverse_one, gain_one
    )
    proj_b_grad = jnp.sum(attn_grad, axis=0)
    attn_low = share_over_mp(attn_grad.astype(BF), parts, 9).reshape(rows, width)

    proj_w_grad = lax.psum_scatter(
        over_rows(mixture_low, attn_low).astype(BF), "seq", scatter_dimension=1, tiled=True
    )
    mixture_grad = over_cols(attn_low, w_proj).astype(BF).reshape(rows, heads, DH)
    probs = jnp.exp(scores_of() - log_total)
    prob_grad = jnp.einsum("qhd,khd->hqk", mixture_grad, values, preferred_element_type=F32)
    row_terms = jnp.einsum("qhd,qhd->hq", mixture_grad.astype(F32), mixture)
    score_grad = (probs * (prob_grad - row_terms[..., None]) * scale).astype(BF)
    query_grad = jnp.einsum("hqk,khd->qhd", score_grad, keys, preferred_element_type=F32)
    key_part = jnp.einsum("hqk,qhd->khd", score_grad, query, preferred_element_type=F32)
    value_part = jnp.einsum(
        "hqk,qhd->khd", probs.astype(BF), mixture_grad, preferred_element_type=F32
    )
    kv_part = jnp.concatenate(
        [key_part.reshape(per, rows, cols), value_part.reshape(per, rows, cols)], axis=2
    )
    kv_grad = group_sum([kv_part[i] for i in range(per)], members, per)
    qkv_grad = jnp.concatenate([query_grad.reshape(rows, cols), kv_grad], axis=1).astype(BF)
    qkv_w_grad = over_rows(x_rows, qkv_grad)
    bias_grad = jnp.sum(qkv_grad.astype(F32), axis=0)

    whole_rows = jnp.stack(
        [proj_b_grad, gain_one_grad, shift_one_grad, outer_b_grad, gain_two_grad, shift_two_grad]
        + [jnp.zeros_like(proj_b_grad)] * 2
    )
    summed_rows = lax.psum(whole_rows, "mp")
    small = jnp.concatenate(
        [
            bias_grad[:cols].reshape(members, -1),
            bias_grad[2 * cols :].reshape(members, -1),
            inner_b_grad.reshape(members, -1),
        ]
        + [summed_rows[i].reshape(members, -1) for i in range(6)],
        axis=1,
    )
    small = jnp.pad(small, ((0, 0), (0, extra * 3 * cols - small.shape[1])))
    last = jnp.concatenate(
        [
            qkv_w_grad.astype(BF).reshape(members, depth, 3 * cols),
            small.astype(BF).reshape(members, extra, 3 * cols),
        ],
        axis=1,
    )
    last = lax.psum_scatter(last, "seq", scatter_dimension=0, tiled=True)[0].astype(F32)
    pieces = []
    start = 0
    flat = last[depth:].reshape(-1)
    for size in sizes:
        pieces.append(flat[start : start + size])
        start += size

    layer_out = from_group(layer_out, 10, 11)
    input_part = (
        sum_over_mp(
            over_cols(qkv_grad, w_qkv).astype(BF),
            parts,
            12,
        )
        + attn_grad
    )
    input_grad = from_group(input_part.astype(BF), 13, 14).astype(F32)
    return (
        layer_out,
        input_grad,
        last[:depth, :cols],
        pieces[0],
        last[:depth, cols : 2 * cols],
        last[:depth, 2 * cols :],
        pieces[1],
        proj_w_grad.astype(F32),
        pieces[3],
        pieces[4],
        pieces[5],
        inner_w_grad.astype(F32),
        pieces[2],
        outer_w_grad.astype(F32),
        pieces[6],
        pieces[7],
        pieces[8],
    )


def solution(mesh):
    tokens = P(None, None, "seq", None)
    rows_cols, cols_rows, both, seq = P("seq", "mp"), P("mp", "seq"), P(("mp", "seq")), P("seq")
    weights = (
        rows_cols,
        both,
        rows_cols,
        rows_cols,
        both,
        cols_rows,
        seq,
        seq,
        seq,
        rows_cols,
        both,
        cols_rows,
        seq,
        seq,
        seq,
    )
    return jax.shard_map(
        functools.partial(on_device, mesh.shape["seq"], mesh.shape["mp"]),
        mesh=mesh,
        in_specs=(tokens,) + weights + (tokens,),
        out_specs=(tokens, tokens) + weights,
        check_vma=False,
    )
```

time: 1580 us -> 1030 us (0.65)
  waiting for transfers between devices: 997 us -> 45.4 us
  Pallas kernels: 0 us -> 551 us
  blocking collectives: 101 us -> 13.4 us
  matrix products: 299 us -> 235 us
  local copies, waits for them, and re-layouts: 57.2 us -> 87.9 us
  other arithmetic: 89.6 us -> 62.1 us
    pallas_call x0 -> x14, Pallas kernels: none -> 551 us  [the longest x6 210 us: share_over_mp(): pl.pallas_call(share_kernel, out_shape=jax.ShapeDtypeStruct((parts,) + ow...]
    all_gather x10 -> x3, waiting for transfers between devices: 354 us -> 5.27 us  [the longest x1 5.25 us: on_device(): first = lax.all_gather(first, 'seq', axis=0)]
    psum x4 -> x0, waiting for transfers between devices: 345 us -> none  [the longest x1 105 us: backward_pass(): lax.psum(across_heads.astype(jnp.bfloat16), 'mp').astype(jnp.float32)]
    reduce_scatter x10 -> x4, waiting for transfers between devices: 293 us -> 39.3 us  [the longest x1 39.3 us: on_device(): lax.psum_scatter(over_rows(first_low, inner_grad).astype(BF), 'seq', scat...]
    all_gather x7 -> x0, blocking collectives: 68.5 us -> none  [the longest x1 12 us: gather_forward(): lax.all_gather(shards[14], 'seq', axis=0, tiled=True)]
    reduce_sum x16 -> x11, other arithmetic: 62.2 us -> 23.5 us  [the longest x1 14.6 us: on_device(): row_total = jnp.sum(exponent, axis=-1, keepdims=True)]
    unnamed x2 -> x0, blocking collectives: 32.8 us -> none
    dot_general x12 -> x4, matrix products: 77.9 us -> 47.2 us  [over_rows(): lax.dot_general(left, right, (((0,), (0,)), ((), ())), preferred_element_...]
  transfers between devices with their start and end apart: 24 -> 9, of which waited for: 21 -> 2; matrix products, arithmetic and copies ran while one was open for 20% -> 22% of each run, Pallas kernels for 0% -> 41%
where the time goes in v1:
time: 1030 us; the launch traced here: 1020 us
  Pallas kernels  551 us (53%)
  matrix products  235 us (23%)
  local copies, waits for them, and re-layouts  87.9 us (9%)
  other arithmetic  62.1 us (6%)
  waiting for transfers between devices  45.4 us (4%)
  between operations  15 us (1%)
  blocking collectives  13.4 us (1%)
    pallas_call x6, Pallas kernels, share_over_mp(): pl.pallas_call(share_kernel, out_shape=jax.ShapeDtypeStruct((parts,) + ow...  210 us
    pallas_call x4, Pallas kernels, swap_groups(): pl.pallas_call(functools.partial(swap_kernel, groups, per), out_shape=jax...  194 us
    pallas_call x4, Pallas kernels, sum_over_mp(): pl.pallas_call(sum_kernel, out_shape=jax.ShapeDtypeStruct((mine, width),...  147 us
    dot_general x4, matrix products, over_cols(): lax.dot_general(left, right, (((1,), (1,)), ((), ())), preferred_element_...  50.1 us
    dot_general x4, matrix products, over_rows(): lax.dot_general(left, right, (((0,), (0,)), ((), ())), preferred_element_...  47.2 us
    dot_general x4, matrix products, matmul(): return jnp.dot(left, right, preferred_element_type=F32)  46.3 us
    reduce_scatter x1, waiting for transfers between devices, on_device(): lax.psum_scatter(over_rows(first_low, inner_grad).astype(BF), 'seq', scat...  39.3 us
  transfers between devices with their start and end apart: 9, of which 2 were waited for; matrix products, arithmetic and copies ran while one was open for 22% of the time, Pallas kernels for 41%

profile of v1, /device:TPU:9, one launch (start us, length us, event | category | flops | bytes accessed | tf_op | source)
XLA Modules:
  0.0 1019.3 jit_solution(17448925850319459546)
XLA Ops:
  23.2 55.5 %swap_groups_1.1 = bf16[4,64,2048]{2,1,0:T(8,128)(2,1)} custom-call(bf16[4,64,2048]{2,1,0:T(8,128)(2,1)} %get-tuple-element.75.block_ref), custom_call_target="tpu_custom_call" | custom-call | bytes 62914560 | tf_op jit(solution)/shard_map/swap_groups_1/pallas_call | solution.py:186
  78.6 36.7 %share_over_mp_2.1 = bf16[4,256,2048]{2,1,0:T(8,128)(2,1)} custom-call(bf16[256,2048]{1,0:T(8,128)(2,1)} %bitcast.161), custom_call_target="tpu_custom_call" | custom-call | bytes 104857600 | tf_op jit(solution)/shard_map/share_over_mp_2/pallas_call | solution.py:147
  128.8 10.0 add_convert_fusion
  142.9 57.1 %swap_groups_3.1 = bf16[4,64,2048]{2,1,0:T(8,128)(2,1)} custom-call(bf16[4,64,2048]{2,1,0:T(8,128)(2,1)} %get-tuple-element.74.block_ref), custom_call_target="tpu_custom_call" | custom-call | bytes 62914560 | tf_op jit(solution)/shard_map/swap_groups_3/pallas_call | solution.py:186
  223.1 15.7 %multiply_reduce_fusion = (f32[4,1024]{1,0:T(4,128)S(1)}, f32[4,1024,2048]{2,1,0:T(8,128)}) fusion(bf16[1024,4,128]{0,2,1:T(8,128)(2,1)} %bitcast.162, bf16[2048,4,128]{0,2,1:T(8,128)(2,1)S(1)} %bitcast.157), kind=kOutput, calls=%fused_computation.6 | convolution fusion | flops 2164256768 | bytes 36716544 | tf_op jit(solution)/shard_map/qhd,khd->hqk/dot_general | solution.py:340
  238.8 14.6 %fusion = f32[4,1024]{1,0:T(4,128)S(1)} fusion(f32[4,1024,2048]{2,1,0:T(8,128)} %get-tuple-element.69, f32[4,1024]{1,0:T(4,128)S(1)} %get-tuple-element.68), kind=kLoop, calls=%fused_computation.4 | loop fusion | flops 25161728 | bytes 33587200 | tf_op jit(solution)/shard_map/reduce_sum | solution.py:345
  253.4 17.5 %bitcast_convert_fusion = (bf16[1024,4,128]{0,2,1:T(8,128)(2,1)}, f32[4,128,1024]{2,1,0:T(8,128)}) fusion(f32[4,1024,2048]{2,1,0:T(8,128)} %get-tuple-element.69, f32[4,1024]{1,0:T(4,128)S(1)} %fusion, f32[4,1024]{1,0:T(4,128)S(1)} %get-tuple-element.68, bf16[256,4,8,128]{3,2,1,0:T(8,128)(2,1)} %get-tuple-element.42), kind=kOutput, calls=%fused_computation.64 | convolution fusion | flops 2181562368 | bytes 38830080 | tf_op jit(solution)/shard_map/hqk,khd->qhd/dot_general | solution.py:348
  276.6 38.9 %sum_over_mp_4.1 = f32[256,2048]{1,0:T(8,128)S(1)} custom-call(bf16[4,256,2048]{2,1,0:T(8,128)(2,1)} %bitcast.187), custom_call_target="tpu_custom_call" | custom-call | bytes 104857600 | tf_op jit(solution)/shard_map/sum_over_mp_4/pallas_call | solution.py:99
  317.7 34.9 %share_over_mp_5.1 = bf16[4,256,2048]{2,1,0:T(8,128)(2,1)} custom-call(bf16[256,2048]{1,0:T(8,128)(2,1)} %fusion.35.own_ref), custom_call_target="tpu_custom_call" | custom-call | bytes 104857600 | tf_op jit(solution)/shard_map/share_over_mp_5/pallas_call | solution.py:147
  352.6 14.5 %fusion.54 = f32[1024,2048]{1,0:T(8,128)} fusion(bf16[1024,2048]{1,0:T(8,128)(2,1)} %bitcast.176, bf16[2048,2048]{1,0:T(8,128)(2,1)} %all-gather.5.cloned.1.call-done), kind=kOutput, calls=%fused_computation.133 | convolution fusion | flops 8589934592 | bytes 20971520 | tf_op jit(solution)/shard_map/dot_general | solution.py:21
  367.1 16.1 %convolution_convert_fusion.5 = bf16[1024,2048]{1,0:T(8,128)(2,1)} fusion(bf16[2048,2048]{1,0:T(8,128)(2,1)} %all-gather.7.cloned.1.call-done, f32[1024,2048]{1,0:T(8,128)} %fusion.54, f32[2048]{0:T(1024)S(1)} %bitcast.219), kind=kOutput, calls=%fused_computation.39 | convolution fusion | flops 8613003264 | bytes 20979712 | tf_op jit(solution)/shard_map/dot_general | solution.py:21
  383.2 36.0 %sum_over_mp_6.1 = f32[256,2048]{1,0:T(8,128)S(1)} custom-call(bf16[4,256,2048]{2,1,0:T(8,128)(2,1)} %bitcast.188), custom_call_target="tpu_custom_call" | custom-call | bytes 104857600 | tf_op jit(solution)/shard_map/sum_over_mp_6/pallas_call | solution.py:99
  425.5 33.3 %share_over_mp_7.1 = bf16[4,256,2048]{2,1,0:T(8,128)(2,1)} custom-call(bf16[256,2048]{1,0:T(8,128)(2,1)} %convert_element_type.235.own_ref), custom_call_target="tpu_custom_call" | custom-call | bytes 104857600 | tf_op jit(solution)/shard_map/share_over_mp_7/pallas_call | solution.py:147
  458.8 19.9 %fusion.46 = (bf16[2048]{0:T(1024)(128)(2,1)S(1)}, bf16[1024,2048]{1,0:T(8,128)(2,1)}) fusion(f32[1024,2048]{1,0:T(8,128)} %fusion.54, f32[2048]{0:T(1024)S(1)} %bitcast.220, bf16[1024,2048]{1,0:T(8,128)(2,1)} %bitcast.178, bf16[2048,2048]{1,0:T(8,128)(2,1)} %all-gather.7.cloned.1.call-done), kind=kOutput, calls=%fused_computation.126 | convolution fusion | flops 8636069888 | bytes 25178112 | tf_op jit(solution)/shard_map/dot_general | solution.py:29
  478.7 13.9 %convolution_convert_fusion.4 = bf16[1024,2048]{1,0:T(8,128)(2,1)} fusion(bf16[1024,2048]{1,0:T(8,128)(2,1)} %get-tuple-element.36, bf16[2048,2048]{1,0:T(8,128)(2,1)} %all-gather.5.cloned.1.call-done), kind=kOutput, calls=%fused_computation.38 | convolution fusion | flops 8592031744 | bytes 16777216 | tf_op jit(solution)/shard_map/dot_general | solution.py:29
  492.6 34.5 %sum_over_mp_8.1 = f32[256,2048]{1,0:T(8,128)S(1)} custom-call(bf16[4,256,2048]{2,1,0:T(8,128)(2,1)} %bitcast.186), custom_call_target="tpu_custom_call" | custom-call | bytes 104857600 | tf_op jit(solution)/shard_map/sum_over_mp_8/pallas_call | solution.py:99
  530.3 13.4 %psum.7 = bf16[8,2048]{1,0:T(8,128)(2,1)S(1)} all-reduce(f32[8,2048]{1,0:T(8,128)S(1)} %stack.31), channel_id=1, replica_groups=mesh['seq'=8,'mp'=4] {'mp'}, use_global_device_ids=true, to_apply=%region_18.19 | all-reduce | flops 16384 | bytes 98304 | tf_op jit(solution)/shard_map/psum | solution.py:409
  546.7 34.1 %share_over_mp_9.1 = bf16[4,256,2048]{2,1,0:T(8,128)(2,1)} custom-call(bf16[256,2048]{1,0:T(8,128)(2,1)} %convert_element_type.238.own_ref), custom_call_target="tpu_custom_call" | custom-call | bytes 104857600 | tf_op jit(solution)/shard_map/share_over_mp_9/pallas_call | solution.py:147
  586.1 16.0 %fusion.19 = f32[2048,4,128]{0,2,1:T(8,128)} fusion(bf16[1024,4,128]{0,2,1:T(8,128)(2,1)S(1)} %bitcast.195, f32[4,1024,2048]{2,1,0:T(8,128)} %get-tuple-element.69, f32[4,1024]{1,0:T(4,128)S(1)} %log_add_fusion), kind=kOutput, calls=%fused_computation.41 | convolution fusion | flops 2172649472 | bytes 38813696 | tf_op jit(solution)/shard_map/hqk,qhd->khd/dot_general | solution.py:394
  602.1 20.3 %multiply_convert_fusion = bf16[4,1024,2048]{2,1,0:T(8,128)(2,1)} fusion(f32[4,1024,2048]{2,1,0:T(8,128)} %get-tuple-element.69, bf16[1024,4,128]{0,2,1:T(8,128)(2,1)S(1)} %bitcast.196, f32[4,1024]{1,0:T(4,128)S(1)} %get-tuple-element.72, f32[4,1024]{1,0:T(4,128)S(1)} %log_add_fusion, bf16[256,4,8,128]{3,2,1,0:T(8,128)(2,1)S(1)} %copy-done.12), kind=kOutput, calls=%fused_computation | convolution fusion | flops 2197815296 | bytes 53510144 | tf_op jit(solution)/shard_map/qhd,khd->hqk/dot_general | solution.py:389
  622.4 10.1 convolution_bitcast_fusion
  680.6 11.6 %convolution_convert_fusion.8 = bf16[4,128,1024]{2,1,0:T(8,128)(2,1)S(1)} fusion(bf16[2048,4,128]{0,2,1:T(8,128)(2,1)S(1)} %bitcast.158, bf16[4,1024,2048]{2,1,0:T(8,128)(2,1)} %multiply_convert_fusion), kind=kOutput, calls=%fused_computation.81 | convolution fusion | flops 2148007936 | bytes 19922944 | tf_op jit(solution)/shard_map/hqk,khd->qhd/dot_general | solution.py:392
  698.4 11.2 %convolution_convert_fusion.2 = bf16[2048,1536]{1,0:T(8,128)(2,1)} fusion(bf16[1024,2048]{1,0:T(8,128)(2,1)} %bitcast.175, bf16[1024,1024]{1,0:T(8,128)(2,1)S(1)} %fusion.17, bf16[1024,512]{1,0:T(8,128)(2,1)S(1)} %copy-done.8), kind=kOutput, calls=%fused_computation.26 | convolution fusion | flops 6451888128 | bytes 13631488 | tf_op jit(solution)/shard_map/dot_general | solution.py:25
  715.9 15.9 %convolution_convert_fusion = bf16[2048,2048]{1,0:T(8,128)(2,1)} fusion(bf16[1024,2048]{1,0:T(8,128)(2,1)} %bitcast.179, f32[1024,2048]{1,0:T(8,128)} %fusion.54, f32[2048]{0:T(1024)S(1)} %bitcast.221), kind=kOutput, calls=%fused_computation.24 | convolution fusion | flops 8615100416 | bytes 20979712 | tf_op jit(solution)/shard_map/dot_general | solution.py:25
  731.9 14.3 %convolution_convert_fusion.1 = bf16[2048,2048]{1,0:T(8,128)(2,1)} fusion(bf16[1024,2048]{1,0:T(8,128)(2,1)} %bitcast.177, bf16[1024,2048]{1,0:T(8,128)(2,1)} %get-tuple-element.36), kind=kOutput, calls=%fused_computation.25 | convolution fusion | flops 8594128896 | bytes 16777216 | tf_op jit(solution)/shard_map/dot_general | solution.py:25
  746.2 42.5 %swap_groups_10.1 = bf16[4,64,2048]{2,1,0:T(8,128)(2,1)} custom-call(bf16[4,64,2048]{2,1,0:T(8,128)(2,1)} %bitcast.190), custom_call_target="tpu_custom_call" | custom-call | bytes 62914560 | tf_op jit(solution)/shard_map/swap_groups_10/pallas_call | solution.py:186
  788.6 35.8 %share_over_mp_11.1 = bf16[4,256,2048]{2,1,0:T(8,128)(2,1)} custom-call(bf16[256,2048]{1,0:T(8,128)(2,1)} %bitcast.183), custom_call_target="tpu_custom_call" | custom-call | bytes 104857600 | tf_op jit(solution)/shard_map/share_over_mp_11/pallas_call | solution.py:147
  829.3 11.1 %convolution_convert_fusion.3 = bf16[1024,2048]{1,0:T(8,128)(2,1)} fusion(bf16[2048,1536]{1,0:T(8,128)(2,1)} %bitcast.172, bf16[1024,1024]{1,0:T(8,128)(2,1)S(1)} %fusion.17, bf16[1024,512]{1,0:T(8,128)(2,1)S(1)} %copy-done.8), kind=kOutput, calls=%fused_computation.37 | convolution fusion | flops 6450839552 | bytes 13631488 | tf_op jit(solution)/shard_map/dot_general | solution.py:29
  840.4 37.2 %sum_over_mp_12.1 = f32[256,2048]{1,0:T(8,128)S(1)} custom-call(bf16[4,256,2048]{2,1,0:T(8,128)(2,1)} %bitcast.185), custom_call_target="tpu_custom_call" | custom-call | bytes 104857600 | tf_op jit(solution)/shard_map/sum_over_mp_12/pallas_call | solution.py:99
  878.8 39.4 %swap_groups_13.1 = bf16[4,64,2048]{2,1,0:T(8,128)(2,1)} custom-call(bf16[4,64,2048]{2,1,0:T(8,128)(2,1)} %bitcast.182), custom_call_target="tpu_custom_call" | custom-call | bytes 62914560 | tf_op jit(solution)/shard_map/swap_groups_13/pallas_call | solution.py:186
  918.2 35.6 %share_over_mp_14.1 = bf16[4,256,2048]{2,1,0:T(8,128)(2,1)} custom-call(bf16[256,2048]{1,0:T(8,128)(2,1)} %bitcast.184), custom_call_target="tpu_custom_call" | custom-call | bytes 104857600 | tf_op jit(solution)/shard_map/share_over_mp_14/pallas_call | solution.py:147
  970.1 39.3 %reduce-scatter.9.cloned.1.call-done = bf16[256,2048]{1,0:T(8,128)(2,1)} async-done(((bf16[2048,2048]{1,0:T(8,128)(2,1)}), bf16[256,2048]{1,0:T(8,128)(2,1)}) %reduce-scatter.9.cloned.1.call-update) | async-done | bytes 1048592 | tf_op jit(solution)/shard_map/reduce_scatter | solution.py:373
  (154 shorter events, 167.5 us)
Async XLA Ops:
  7.2 113.4 %all-gather.9.cloned.1.call-start = ((), (), s32[]{:S(2)}) async-start(), calls=%async_computation.10 | async-start | bytes 10027008 | tf_op jit(solution)/shard_map/all_gather | solution.py:301
  19.2 333.3 %all-gather.5.cloned.1.call-start = ((), (), s32[]{:S(2)}) async-start(), calls=%async_computation.4 | async-start | bytes 9437184 | tf_op jit(solution)/shard_map/all_gather | solution.py:302
  20.0 347.1 %all-gather.7.cloned.1.call-start = ((), (), s32[]{:S(2)}) async-start(), calls=%async_computation.5 | async-start | bytes 9437184 | tf_op jit(solution)/shard_map/all_gather | solution.py:303
  127.8 0.8 copy-start.13
  138.9 1.7 copy-start.9
  142.2 74.0 %collective-permute-start = (bf16[1024,1024]{1,0:T(8,128)(2,1)}, bf16[1024,1024]{1,0:T(8,128)(2,1)}, u32[]{:S(2)}, u32[]{:S(2)}) collective-permute-start(bf16[1024,1024]{1,0:T(8,128)(2,1)} %slice.196), channel_id=1, source_target_pairs={{0,4},{4,0},{8,12},{12,8},{16,20},{20,16},{24,28},{28,24},{1,5},{5... | collective-permute-start | bytes 6291464 | tf_op jit(solution)/shard_map/ppermute | solution.py:227
  142.6 818.4 %reduce-scatter.7.cloned.1.call-start = ((), (), s32[]{:S(2)}) async-start(), calls=%async_computation.7 | async-start | bytes 2359296 | tf_op jit(solution)/shard_map/reduce_scatter | solution.py:384
  200.0 5.1 copy-start.5
  223.1 15.7 %copy-start = (bf16[2048,512]{0,1:T(8,128)(2,1)}, bf16[2048,512]{0,1:T(8,128)(2,1)S(1)}, u32[]{:S(2)}) copy-start(bf16[2048,512]{0,1:T(8,128)(2,1)S(1)} %copy.92) | copy-start | bytes 6291460
  253.4 17.6 %copy-start.10 = (bf16[64,8,8,256]{3,1,2,0:T(8,128)(2,1)S(1)}, bf16[64,8,8,256]{3,1,2,0:T(8,128)(2,1)}, u32[]{:S(2)}) copy-start(bf16[64,8,8,256]{3,1,2,0:T(8,128)(2,1)} %copy.95) | copy-start | bytes 6291460
  276.6 38.9 %copy-start.6 = (bf16[4,64,2048]{2,1,0:T(8,128)(2,1)S(1)}, bf16[4,64,2048]{2,1,0:T(8,128)(2,1)}, u32[]{:S(2)}) copy-start(bf16[4,64,2048]{2,1,0:T(8,128)(2,1)} %swap_groups_1.1) | copy-start | bytes 3145732
  423.1 1.3 copy-start.2
  492.6 34.5 %copy-start.3 = (f32[256,2048]{1,0:T(8,128)S(1)}, f32[256,2048]{1,0:T(8,128)}, u32[]{:S(2)}) copy-start(f32[256,2048]{1,0:T(8,128)} %copy-done.2) | copy-start | bytes 6291460
  528.2 2.1 copy-start.14
  543.7 37.1 %copy-start.11 = (bf16[64,8,8,256]{3,1,2,0:T(8,128)(2,1)S(1)}, bf16[64,8,8,256]{3,1,2,0:T(8,128)(2,1)}, u32[]{:S(2)}) copy-start(bf16[64,8,8,256]{3,1,2,0:T(8,128)(2,1)} %copy.95) | copy-start | bytes 6291460
  586.0 16.0 %copy-start.12 = (bf16[256,4,8,128]{3,2,1,0:T(8,128)(2,1)S(1)}, bf16[256,4,8,128]{3,2,1,0:T(8,128)(2,1)}, u32[]{:S(2)}) copy-start(bf16[256,4,8,128]{3,2,1,0:T(8,128)(2,1)} %get-tuple-element.42) | copy-start | bytes 6291460
  602.1 20.3 %copy-start.7 = (bf16[1024,512]{0,1:T(8,128)(2,1)S(1)}, bf16[1024,512]{0,1:T(8,128)(2,1)}, u32[]{:S(2)}) copy-start(bf16[1024,512]{0,1:T(8,128)(2,1)} %copy.91) | copy-start | bytes 3145732
  660.6 12.6 %copy-start.15 = (bf16[1024,4,128]{0,2,1:T(8,128)(2,1)S(1)}, bf16[1024,4,128]{0,2,1:T(8,128)(2,1)}, u32[]{:S(2)}) copy-start(bf16[1024,4,128]{0,2,1:T(8,128)(2,1)} %get-tuple-element.70) | copy-start | bytes 3145732
  664.5 29.3 %collective-permute-start.1 = (bf16[1024,1024]{1,0:T(8,128)(2,1)}, bf16[1024,1024]{1,0:T(8,128)(2,1)}, u32[]{:S(2)}, u32[]{:S(2)}) collective-permute-start(bf16[1024,1024]{1,0:T(8,128)(2,1)} %fusion.24), channel_id=1, source_target_pairs={{0,4},{4,0},{8,12},{12,8},{16,20},{20,16},{24,28},{28,24},{1,5},{5... | collective-permute-start | bytes 6291464 | tf_op jit(solution)/shard_map/ppermute | solution.py:239
  679.0 1.6 copy-start.1
  679.0 283.8 %reduce-scatter.5.cloned.1.call-start = ((), (), s32[]{:S(2)}) async-start(), calls=%async_computation.6 | async-start | bytes 7520256 | tf_op jit(solution)/shard_map/reduce_scatter | solution.py:427
  693.7 3.8 copy-start.8
  715.9 251.5 %reduce-scatter.11.cloned.1.call-start = ((), (), s32[]{:S(2)}) async-start(), calls=%async_computation.9 | async-start | bytes 9437184 | tf_op jit(solution)/shard_map/reduce_scatter | solution.py:368
  731.8 277.6 %reduce-scatter.9.cloned.1.call-start = ((), (), s32[]{:S(2)}) async-start(), calls=%async_computation.8 | async-start | bytes 9437184 | tf_op jit(solution)/shard_map/reduce_scatter | solution.py:373
  840.4 37.2 %copy-start.4 = (f32[256,2048]{1,0:T(8,128)S(1)}, f32[256,2048]{1,0:T(8,128)}, u32[]{:S(2)}) copy-start(f32[256,2048]{1,0:T(8,128)} %get-tuple-element.34) | copy-start | bytes 6291460
Sparse Core Ops, SparseCore 0:
  19.4 101.2 all-gather.8
  122.2 102.5 all-gather.4
  226.4 83.3 all-gather.6
  679.1 27.8 reduce-scatter.6
  716.0 92.6 reduce-scatter.4
  810.9 109.4 reduce-scatter.10
  922.8 86.6 reduce-scatter.8

commit v2 on v1

v2 whole, which is shorter than its diff:
```python
import functools

import jax
import jax.numpy as jnp
from jax import lax
from jax.experimental import pallas as pl
from jax.experimental.pallas import tpu as pltpu
from jax.sharding import PartitionSpec as P

DH = 128
EPSILON = 1e-06
BF = jnp.bfloat16
F32 = jnp.float32
MESH = pl.DeviceIdType.MESH
ANY = pl.BlockSpec(memory_space=pl.ANY)
VMEM = pl.BlockSpec(memory_space=pltpu.VMEM)
MIB = 1 << 20


def matmul(left, right):
    return jnp.dot(left, right, preferred_element_type=F32)


def over_rows(left, right):
    return lax.dot_general(left, right, (((0,), (0,)), ((), ())), preferred_element_type=F32)


def over_cols(left, right):
    return lax.dot_general(left, right, (((1,), (1,)), ((), ())), preferred_element_type=F32)


def gelu_tanh(values):
    return jax.nn.gelu(values, approximate=True)


def square():
    me = lax.axis_index("mp")
    return me, me + 1 - 2 * lax.rem(me, 2), lax.rem(me + 2, 4), 3 - me


def greet(devices):
    barrier = pltpu.get_barrier_semaphore()
    for device in devices:
        pl.semaphore_signal(barrier, inc=1, device_id=device, device_id_type=MESH)
    pl.semaphore_wait(barrier, len(devices))


def sender(send_sem, recv_sem):
    def send(source, target, slot, device):
        copy = pltpu.make_async_remote_copy(
            src_ref=source,
            dst_ref=target,
            send_sem=send_sem.at[slot],
            recv_sem=recv_sem.at[slot],
            device_id=device,
            device_id_type=MESH,
        )
        copy.start()
        return copy

    return send


class Exchange:
    def __init__(self, part_ref, landed, relay, send_sem, recv_sem):
        self.me, self.along_x, self.along_y, self.across = square()
        self.part, self.landed, self.relay = part_ref, landed, relay
        self.send = sender(send_sem, recv_sem)
        self.copies = {}

    def ways(self, index):
        pair = (self.along_x, self.along_y)
        return pair if index % 2 == 0 else pair[::-1]

    def start(self, index, piece):
        near, _ = self.ways(index)
        for kind, owner in enumerate((self.across, near)):
            self.copies[index, kind] = self.send(
                self.part.at[owner, piece], self.landed.at[index, kind], 6 * index + kind, {"mp": near}
            )

    def pass_on(self, index, piece):
        _, far = self.ways(index)
        self.copies[index, 0].wait_recv()
        self.relay[index] = (
            self.part[far, piece].astype(F32) + self.landed[index, 0].astype(F32)
        ).astype(BF)
        self.copies[index, 2] = self.send(
            self.relay.at[index], self.landed.at[index, 2], 6 * index + 2, {"mp": far}
        )

    def total(self, index, piece):
        self.copies[index, 1].wait_recv()
        self.copies[index, 2].wait_recv()
        return (
            self.part[self.me, piece].astype(F32)
            + self.landed[index, 1].astype(F32)
            + self.landed[index, 2].astype(F32)
        )

    def share(self, index, source, target):
        near, far = self.ways(index)
        self.copies[index, 3] = self.send(source, target(self.me), 6 * index + 3, {"mp": near})
        self.copies[index, 4] = self.send(source, target(self.me), 6 * index + 4, {"mp": far})

    def forward(self, index, target):
        near, far = self.ways(index)
        self.copies[index, 3].wait_recv()
        self.copies[index, 5] = self.send(target(near), target(near), 6 * index + 5, {"mp": far})

    def finish(self, count):
        for index in range(count):
            self.copies[index, 4].wait_recv()
            self.copies[index, 5].wait_recv()
        for copy in self.copies.values():
            copy.wait_send()


def piece_order(groups):
    return list(range(1, groups, 2)) + list(range(0, groups, 2)) if groups == 2 else (
        [1, 2, 0] + list(range(3, groups))
    )


def planes(groups, per):
    index = lax.axis_index("seq")
    return [{"seq": lax.rem(index + step * per, groups * per)} for step in range(groups)]


def mean_of(values):
    return jnp.mean(values, axis=-1, keepdims=True)


def normed(values):
    centre = values - mean_of(values)
    inverse = lax.rsqrt(mean_of(centre * centre) + EPSILON)
    return centre * inverse, inverse


def norm_back(grad, normal, inverse, gain):
    inner = grad * gain
    return inverse * (inner - mean_of(inner) - normal * mean_of(inner * normal))


def run_pieces(exchange, groups, work):
    order = piece_order(groups)
    places = list(enumerate(order))
    half = groups // 2
    first, second = places[:half], places[half:]
    for index, piece in first:
        exchange.start(index, piece)
    for index, piece in first:
        exchange.pass_on(index, piece)
    for index, piece in second:
        exchange.start(index, piece)
    for index, piece in first:
        work(index, piece, exchange.total(index, piece))
    for index, piece in second:
        exchange.pass_on(index, piece)
    return first, second


def first_norm_kernel(
    groups, part_ref, x_ref, rows_ref, low_ref, normal_ref, inverse_ref,
    landed, relay, ready, send_sem, recv_sem, local_sem,
):
    exchange = Exchange(part_ref, landed, relay, send_sem, recv_sem)
    greet([{"mp": exchange.along_x}, {"mp": exchange.along_y}])
    local = []

    def target(piece):
        return lambda device: low_ref.at[device, piece]

    def work(index, piece, total):
        values = x_ref[piece].astype(F32) + total + rows_ref[0:1]
        normal, inverse = normed(values)
        normal_ref[piece] = normal
        inverse_ref[piece] = inverse
        ready[index] = (normal * rows_ref[1:2] + rows_ref[2:3]).astype(BF)
        exchange.share(index, ready.at[index], target(piece))
        copy = pltpu.make_async_copy(
            ready.at[index], low_ref.at[exchange.me, piece], local_sem.at[index]
        )
        copy.start()
        local.append(copy)

    first, second = run_pieces(exchange, groups, work)
    for index, piece in first:
        exchange.forward(index, target(piece))
    for index, piece in second:
        work(index, piece, exchange.total(index, piece))
    for index, piece in second:
        exchange.forward(index, target(piece))
    exchange.finish(groups)
    for copy in local:
        copy.wait()


def second_norm_kernel(
    groups, per, part_ref, normal_ref, cotan_ref, rows_ref,
    low_ref, grad_ref, back_ref, sums_ref,
    landed, relay, ready, layer, cotan_in, send_sem, recv_sem, local_sem,
):
    exchange = Exchange(part_ref, landed, relay, send_sem, recv_sem)
    peers = planes(groups, per)
    greet([{"mp": exchange.along_x}, {"mp": exchange.along_y}] + peers[1:])
    base = 6 * groups
    arriving = {
        step: exchange.send(cotan_ref.at[step], cotan_in.at[step], base + step, peers[step])
        for step in range(1, groups)
    }
    leaving, local = [], []
    sums_ref[...] = jnp.zeros_like(sums_ref)

    def target(piece):
        return lambda device: low_ref.at[device, piece]

    def keep(source, place, slot):
        copy = pltpu.make_async_copy(source, place, local_sem.at[slot])
        copy.start()
        local.append(copy)

    def work(index, piece, total):
        gain_one, shift_one, bias = rows_ref[0:1], rows_ref[1:2], rows_ref[2:3]
        gain, shift = rows_ref[3:4], rows_ref[4:5]
        values = normal_ref[piece] * gain_one + shift_one + total + bias
        normal, inverse = normed(values)
        layer[index] = (normal * gain + shift).astype(BF)
        if piece == 0:
            keep(layer.at[index], back_ref.at[0], groups)
            cotan = cotan_ref[0].astype(F32)
        else:
            leaving.append(
                exchange.send(
                    layer.at[index], back_ref.at[piece], base + groups + piece, peers[groups - piece]
                )
            )
            arriving[piece].wait_recv()
            cotan = cotan_in[piece].astype(F32)
        grad = norm_back(cotan, normal, inverse, gain)
        grad_ref[piece] = grad
        ready[index] = grad.astype(BF)
        exchange.share(index, ready.at[index], target(piece))
        keep(ready.at[index], low_ref.at[exchange.me, piece], index)
        sums_ref[0:1] += jnp.sum(grad, axis=0, keepdims=True)
        sums_ref[1:2] += jnp.sum(cotan * normal, axis=0, keepdims=True)
        sums_ref[2:3] += jnp.sum(cotan, axis=0, keepdims=True)

    first, second = run_pieces(exchange, groups, work)
    for index, piece in first:
        exchange.forward(index, target(piece))
    for index, piece in second:
        work(index, piece, exchange.total(index, piece))
    for index, piece in second:
        exchange.forward(index, target(piece))
    exchange.finish(groups)
    for copy in leaving:
        copy.wait()
    for copy in arriving.values():
        copy.wait_send()
    for copy in local:
        copy.wait()


def first_back_kernel(
    groups, part_ref, grad_ref, normal_ref, inverse_ref, sums_in_ref, rows_ref,
    low_ref, out_ref, sums_ref,
    landed, relay, ready, own_sums, send_sem, recv_sem, local_sem,
):
    exchange = Exchange(part_ref, landed, relay, send_sem, recv_sem)
    greet([{"mp": exchange.along_x}, {"mp": exchange.along_y}, {"mp": exchange.across}])
    local = []
    own_sums[...] = sums_in_ref[...]

    def target(piece):
        return lambda device: low_ref.at[device, piece]

    def keep(source, place, slot):
        copy = pltpu.make_async_copy(source, place, local_sem.at[slot])
        copy.start()
        local.append(copy)

    def work(index, piece, total):
        grad = total + grad_ref[piece]
        normal = normal_ref[piece]
        moved = norm_back(grad, normal, inverse_ref[piece], rows_ref[0:1])
        out_ref[piece] = moved
        ready[index] = moved.astype(BF)
        exchange.share(index, ready.at[index], target(piece))
        keep(ready.at[index], low_ref.at[exchange.me, piece], index)
        own_sums[3:4] += jnp.sum(moved, axis=0, keepdims=True)
        own_sums[4:5] += jnp.sum(grad * normal, axis=0, keepdims=True)
        own_sums[5:6] += jnp.sum(grad, axis=0, keepdims=True)

    first, second = run_pieces(exchange, groups, work)
    for index, piece in first:
        exchange.forward(index, target(piece))
    for index, piece in second:
        work(index, piece, exchange.total(index, piece))
    others = [
        exchange.send(own_sums, sums_ref.at[exchange.me], 6 * groups + slot, {"mp": device})
        for slot, device in enumerate((exchange.along_x, exchange.along_y, exchange.across))
    ]
    keep(own_sums, sums_ref.at[exchange.me], groups)
    for index, piece in second:
        exchange.forward(index, target(piece))
    exchange.finish(groups)
    for copy in others:
        copy.wait()
    for copy in local:
        copy.wait()


def input_kernel(
    groups, per, part_ref, grad_ref, small_ref,
    all_ref, small_out,
    landed, relay, ready, back, send_sem, recv_sem, local_sem,
):
    exchange = Exchange(part_ref, landed, relay, send_sem, recv_sem)
    peers = planes(groups, per)
    members = groups * per
    here = lax.axis_index("seq")
    group = here // per
    devices = [{"seq": lax.rem(here + step, members)} for step in range(1, members)]
    greet([{"mp": exchange.along_x}, {"mp": exchange.along_y}] + devices)
    base = 6 * groups
    small = [
        exchange.send(
            small_ref.at[lax.rem(here + step, members)],
            small_out.at[here],
            base + groups + step,
            devices[step - 1],
        )
        for step in range(1, members)
    ]
    crossing, local = {}, []

    def keep(source, place, slot):
        copy = pltpu.make_async_copy(source, place, local_sem.at[slot])
        copy.start()
        local.append(copy)

    keep(small_ref.at[here], small_out.at[here], groups)

    def target(piece):
        sequence = lax.rem(group + piece, groups)
        return lambda device: all_ref.at[sequence, device]

    def work(index, piece, total):
        ready[piece] = (total + grad_ref[piece]).astype(BF)
        if piece > 0:
            crossing[piece] = exchange.send(
                ready.at[piece], back.at[piece], base + piece, peers[groups - piece]
            )

    def share(index, piece):
        source = ready.at[0]
        if piece > 0:
            crossing[piece].wait_recv()
            source = back.at[piece]
        exchange.share(index, source, target(piece))
        keep(source, target(piece)(exchange.me), index)

    first, second = run_pieces(exchange, groups, work)
    for index, piece in second:
        work(index, piece, exchange.total(index, piece))
    outward = [place for place in second if place[1] == 0] + first
    outward += [place for place in second if place[1] > 0]
    for index, piece in outward:
        share(index, piece)
    for index, piece in outward:
        exchange.forward(index, target(piece))
    exchange.finish(groups)
    for copy in small:
        copy.wait()
    for copy in crossing.values():
        copy.wait_send()
    for copy in local:
        copy.wait()


def exchange_call(kernel, ident, operands, results, groups, piece, width, scratch, extra):
    return pl.pallas_call(
        kernel,
        out_shape=tuple(jax.ShapeDtypeStruct(shape, dtype) for shape, dtype, _ in results),
        in_specs=[VMEM] * len(operands),
        out_specs=tuple(spec for _, _, spec in results),
        scratch_shapes=[
            pltpu.VMEM((groups, 3, piece, width), BF),
            pltpu.VMEM((groups, piece, width), BF),
            pltpu.VMEM((groups, piece, width), BF),
        ]
        + scratch
        + [
            pltpu.SemaphoreType.DMA((6 * groups + extra,)),
            pltpu.SemaphoreType.DMA((6 * groups + extra,)),
            pltpu.SemaphoreType.DMA((groups + 1,)),
        ],
        compiler_params=pltpu.CompilerParams(
            collective_id=ident, has_side_effects=True, vmem_limit_bytes=52 * MIB
        ),
        cost_estimate=pl.CostEstimate(flops=0, bytes_accessed=200 * MIB, transcendentals=0),
        name=f"exchange_{ident}",
    )(*operands)


def first_norm(part, x_part, rows, parts, ident):
    groups, piece, width = x_part.shape
    if parts != 4:
        total = lax.psum_scatter(part, "mp", scatter_dimension=0, tiled=True).astype(F32)
        values = x_part.astype(F32) + total.reshape(x_part.shape) + rows[0]
        normal, inverse = normed(values)
        low = lax.all_gather((normal * rows[1] + rows[2]).astype(BF), "mp", axis=0)
        return low, normal, inverse
    return exchange_call(
        functools.partial(first_norm_kernel, groups),
        ident,
        (part.reshape(parts, groups, piece, width), x_part, rows),
        [
            ((parts, groups, piece, width), BF, ANY),
            ((groups, piece, width), F32, VMEM),
            ((groups, piece, 1), F32, VMEM),
        ],
        groups, piece, width, [], 0,
    )


def second_norm(part, normal, cotan, rows, members, parts, ident):
    groups, piece, width = normal.shape
    if parts != 4:
        total = lax.psum_scatter(part, "mp", scatter_dimension=0, tiled=True).astype(F32)
        values = normal * rows[0] + rows[1] + total.reshape(normal.shape) + rows[2]
        normal, inverse = normed(values)
        layer = (normal * rows[3] + rows[4]).astype(BF)
        back = jnp.stack(swap_blocks(layer, members, -1))
        cotan = jnp.stack(swap_blocks(cotan, members, 1)).astype(F32)
        grad = norm_back(cotan, normal, inverse, rows[3])
        sums = [jnp.sum(array, axis=(0, 1)) for array in (grad, cotan * normal, cotan)]
        sums = jnp.stack(sums + [jnp.zeros_like(sums[0])] * 5)
        return lax.all_gather(grad.astype(BF), "mp", axis=0), grad, back, sums
    return exchange_call(
        functools.partial(second_norm_kernel, groups, members // groups),
        ident,
        (part.reshape(parts, groups, piece, width), normal, cotan, rows),
        [
            ((parts, groups, piece, width), BF, ANY),
            ((groups, piece, width), F32, VMEM),
            ((groups, piece, width), BF, ANY),
            ((8, width), F32, VMEM),
        ],
        groups, piece, width,
        [pltpu.VMEM((groups, piece, width), BF), pltpu.VMEM((groups, piece, width), BF)],
        2 * groups,
    )


def first_back(part, grad, normal, inverse, sums, rows, parts, ident):
    groups, piece, width = normal.shape
    if parts != 4:
        total = lax.psum_scatter(part, "mp", scatter_dimension=0, tiled=True).astype(F32)
        grad = total.reshape(normal.shape) + grad
        moved = norm_back(grad, normal, inverse, rows[0])
        more = [jnp.sum(array, axis=(0, 1)) for array in (moved, grad * normal, grad)]
        sums = sums.at[3:6].add(jnp.stack(more))
        return (
            lax.all_gather(moved.astype(BF), "mp", axis=0),
            moved,
            lax.all_gather(sums, "mp", axis=0),
        )
    return exchange_call(
        functools.partial(first_back_kernel, groups),
        ident,
        (part.reshape(parts, groups, piece, width), grad, normal, inverse, sums, rows),
        [
            ((parts, groups, piece, width), BF, ANY),
            ((groups, piece, width), F32, VMEM),
            ((parts, 8, width), F32, VMEM),
        ],
        groups, piece, width, [pltpu.VMEM((8, width), F32)], 3,
    )


def input_gradient(part, grad, small, members, parts, ident):
    groups, piece, width = grad.shape
    if parts != 4:
        total = lax.psum_scatter(part, "mp", scatter_dimension=0, tiled=True).astype(F32)
        ready = (total.reshape(grad.shape) + grad).astype(BF)
        back = jnp.stack(swap_blocks(ready, members, -1))
        back = jnp.roll(back, lax.axis_index("seq") // (members // groups), axis=0)
        return lax.all_gather(back, "mp", axis=1), lax.all_to_all(small, "seq", 0, 0)
    return exchange_call(
        functools.partial(input_kernel, groups, members // groups),
        ident,
        (part.reshape(parts, groups, piece, width), grad, small),
        [((groups, parts, piece, width), BF, ANY), (small.shape, F32, VMEM)],
        groups, piece, width, [pltpu.VMEM((groups, piece, width), BF)], groups + members,
    )


def share_kernel(own_ref, all_ref, send_sem, recv_sem, local_sem):
    me, along_x, along_y, _ = square()
    to_x, to_y = {"mp": along_x}, {"mp": along_y}
    greet([to_x, to_y])
    send = sender(send_sem, recv_sem)
    half = own_ref.shape[0] // 2
    upper, lower = pl.ds(0, half), pl.ds(half, half)
    copies = [
        send(own_ref.at[upper], all_ref.at[me, upper], 0, to_x),
        send(own_ref.at[lower], all_ref.at[me, lower], 1, to_y),
        send(own_ref.at[lower], all_ref.at[me, lower], 2, to_x),
        send(own_ref.at[upper], all_ref.at[me, upper], 3, to_y),
    ]
    local = pltpu.make_async_copy(own_ref, all_ref.at[me], local_sem)
    local.start()
    copies[0].wait_recv()
    copies.append(send(all_ref.at[along_x, upper], all_ref.at[along_x, upper], 4, to_y))
    copies[1].wait_recv()
    copies.append(send(all_ref.at[along_y, lower], all_ref.at[along_y, lower], 5, to_x))
    for copy in copies[2:]:
        copy.wait_recv()
    for copy in copies:
        copy.wait_send()
    local.wait()


def share_over_mp(own, parts, ident):
    if parts != 4:
        return lax.all_gather(own, "mp", axis=0)
    return pl.pallas_call(
        share_kernel,
        out_shape=jax.ShapeDtypeStruct((parts,) + own.shape, own.dtype),
        in_specs=[ANY],
        out_specs=ANY,
        scratch_shapes=[
            pltpu.SemaphoreType.DMA((6,)),
            pltpu.SemaphoreType.DMA((6,)),
            pltpu.SemaphoreType.DMA,
        ],
        compiler_params=pltpu.CompilerParams(collective_id=ident, has_side_effects=True),
        cost_estimate=pl.CostEstimate(flops=0, bytes_accessed=100 * MIB, transcendentals=0),
        name=f"share_over_mp_{ident}",
    )(own)


def swap_kernel(
    groups, per, sign, block_ref, small_ref, out_ref, small_out, send_sem, recv_sem, local_sem
):
    members = groups * per
    index = lax.axis_index("seq")
    devices = [{"seq": lax.rem(index + step, members)} for step in range(1, members)]
    greet(devices)
    send = sender(send_sem, recv_sem)
    copies = []
    for step in range(1, groups):
        ahead = step if sign > 0 else groups - step
        source = block_ref.at[step]
        copies.append(send(source, out_ref.at[step], step, devices[ahead * per - 1]))
    for step in range(1, members):
        target = lax.rem(index + step, members)
        copies.append(
            send(small_ref.at[target], small_out.at[index], groups + step, devices[step - 1])
        )
    locals_ = [
        pltpu.make_async_copy(block_ref.at[0], out_ref.at[0], local_sem.at[0]),
        pltpu.make_async_copy(small_ref.at[index], small_out.at[index], local_sem.at[1]),
    ]
    for local in locals_:
        local.start()
    for local in locals_:
        local.wait()
    for copy in copies:
        copy.wait()


def shift_pairs(members, ahead):
    return [(index, (index + ahead) % members) for index in range(members)]


def swap_blocks(blocks, members, sign):
    groups = blocks.shape[0]
    per = members // groups
    arrived = [blocks[0]]
    for step in range(1, groups):
        pairs = shift_pairs(members, sign * step * per)
        arrived.append(lax.ppermute(blocks[step], "seq", pairs))
    return arrived


def swap_groups(blocks, small, members, parts, sign, ident):
    groups = blocks.shape[0]
    per = members // groups
    if parts != 4:
        return jnp.stack(swap_blocks(blocks, members, sign)), lax.all_to_all(small, "seq", 0, 0)
    return pl.pallas_call(
        functools.partial(swap_kernel, groups, per, sign),
        out_shape=(
            jax.ShapeDtypeStruct(blocks.shape, blocks.dtype),
            jax.ShapeDtypeStruct(small.shape, small.dtype),
        ),
        in_specs=[ANY, ANY],
        out_specs=(ANY, ANY),
        scratch_shapes=[
            pltpu.SemaphoreType.DMA((groups + members,)),
            pltpu.SemaphoreType.DMA((groups + members,)),
            pltpu.SemaphoreType.DMA((2,)),
        ],
        compiler_params=pltpu.CompilerParams(collective_id=ident, has_side_effects=True),
        cost_estimate=pl.CostEstimate(flops=0, bytes_accessed=60 * MIB, transcendentals=0),
        name=f"swap_groups_{ident}",
    )(blocks, small)


def score_block(keys, queries):
    return lax.dot_general(keys, queries, (((1,), (1,)), ((), ())), preferred_element_type=F32)


def attend_kernel(
    query_ref, key_ref, value_ref, key_far_ref, value_far_ref, mix_ref, low_ref, log_ref, turned
):
    rows = key_ref.shape[0]

    @pl.when(pl.program_id(1) == 0)
    def _():
        turned[:, :rows] = value_ref[...].T
        turned[:, rows:] = value_far_ref[...].T

    scale = DH ** (-0.5)
    near = score_block(key_ref[...], query_ref[...])
    far = score_block(key_far_ref[...], query_ref[...])
    highest = jnp.maximum(
        jnp.max(near, axis=0, keepdims=True), jnp.max(far, axis=0, keepdims=True)
    )
    near = jnp.exp((near - highest) * scale)
    far = jnp.exp((far - highest) * scale)
    total = jnp.sum(near, axis=0, keepdims=True) + jnp.sum(far, axis=0, keepdims=True)
    mix = jnp.dot(turned[:, :rows], near.astype(BF), preferred_element_type=F32)
    mix += jnp.dot(turned[:, rows:], far.astype(BF), preferred_element_type=F32)
    mix = (mix / total).T
    mix_ref[...] = mix
    low_ref[...] = mix.astype(BF)
    log_ref[0] = highest * scale + jnp.log(total)


def attend(qkv, kv_far, heads):
    rows, cols = qkv.shape[0], heads * DH
    away = kv_far.shape[0]
    block = min(512, rows)

    def tile(offset):
        return pl.BlockSpec((block, DH), lambda h, i: (i, offset + h))

    def long(count, offset):
        return pl.BlockSpec((count, DH), lambda h, i: (0, offset + h))

    return pl.pallas_call(
        attend_kernel,
        grid=(heads, rows // block),
        out_shape=(
            jax.ShapeDtypeStruct((rows, cols), F32),
            jax.ShapeDtypeStruct((rows, cols), BF),
            jax.ShapeDtypeStruct((heads, 1, rows), F32),
        ),
        in_specs=[
            tile(0),
            long(rows, heads),
            long(rows, 2 * heads),
            long(away, 0),
            long(away, heads),
        ],
        out_specs=(tile(0), tile(0), pl.BlockSpec((1, 1, block), lambda h, i: (h, 0, i))),
        scratch_shapes=[pltpu.VMEM((DH, rows + away), BF)],
        compiler_params=pltpu.CompilerParams(vmem_limit_bytes=52 * MIB),
        cost_estimate=pl.CostEstimate(
            flops=8 * rows * (rows + away) * cols,
            bytes_accessed=20 * rows * cols,
            transcendentals=rows * (rows + away) * heads,
        ),
        name="attend",
    )(qkv, qkv, qkv, kv_far, kv_far)


def layer_copies(back_ref, all_ref, send_sem, recv_sem, groups, per):
    me, along_x, along_y, _ = square()
    group = lax.axis_index("seq") // per
    copies = []
    for piece in range(groups):
        near, far = (along_x, along_y) if piece % 2 == 0 else (along_y, along_x)
        sequence = lax.rem(group + piece, groups)
        block, own, passed = back_ref.at[piece], all_ref.at[sequence, me], all_ref.at[sequence, near]
        for kind, (source, target, device) in enumerate(
            ((block, own, near), (block, own, far), (passed, passed, far))
        ):
            copies.append(
                pltpu.make_async_remote_copy(
                    src_ref=source,
                    dst_ref=target,
                    send_sem=send_sem.at[3 * piece + kind],
                    recv_sem=recv_sem.at[3 * piece + kind],
                    device_id={"mp": device},
                    device_id_type=MESH,
                )
            )
    return copies[0::3], copies[1::3], copies[2::3]


def attend_back_kernel(
    groups,
    per,
    step,
    query_ref,
    key_ref,
    value_ref,
    key_far_ref,
    value_far_ref,
    grad_ref,
    mix_ref,
    log_ref,
    *rest,
):
    sharing = groups > 0
    if sharing:
        back_ref, *rest = rest
    dquery_ref, dkey_ref, dvalue_ref, dkey_far_ref, dvalue_far_ref, *rest = rest
    if sharing:
        all_ref, *rest = rest
    turned, key_sum, value_sum, *rest = rest
    block = pl.program_id(1)
    rows = key_ref.shape[0]
    if sharing:
        send_sem, recv_sem, local_sem = rest
        now = pl.program_id(0) * pl.num_programs(1) + block
        count = pl.num_programs(0) * pl.num_programs(1)
        near, far, passed = layer_copies(back_ref, all_ref, send_sem, recv_sem, groups, per)
        me, along_x, along_y, _ = square()
        group = lax.axis_index("seq") // per
        local = [
            pltpu.make_async_copy(
                back_ref.at[piece],
                all_ref.at[lax.rem(group + piece, groups), me],
                local_sem.at[piece],
            )
            for piece in range(groups)
        ]

        @pl.when(now == 0)
        def _():
            greet([{"mp": along_x}, {"mp": along_y}])
            for copy in near + far + local:
                copy.start()

        @pl.when(now == count * 5 // 8)
        def _():
            for first, second in zip(near, passed):
                first.wait_recv()
                second.start()

    @pl.when(block == 0)
    def _():
        turned[:, :rows] = key_ref[...].T
        turned[:, rows:] = key_far_ref[...].T
        key_sum[...] = jnp.zeros_like(key_sum)
        value_sum[...] = jnp.zeros_like(value_sum)

    scale = DH ** (-0.5)
    query, grad = query_ref[...], grad_ref[...]
    terms = jnp.sum((grad.astype(F32) * mix_ref[...]).T, axis=0, keepdims=True)
    logs = log_ref[0]
    dquery = jnp.zeros((DH, query.shape[0]), F32)
    spans = [(key_ref, value_ref, start, start) for start in range(0, rows, step)]
    spans += [
        (key_far_ref, value_far_ref, start, rows + start)
        for start in range(0, key_far_ref.shape[0], step)
    ]
    for keys, values, start, place in spans:
        part = pl.ds(place, step)
        probs = jnp.exp(score_block(keys[pl.ds(start, step)], query) * scale - logs)
        prob_grad = score_block(values[pl.ds(start, step)], grad)
        score_grad = (probs * (prob_grad - terms) * scale).astype(BF)
        value_sum[part] += jnp.dot(probs.astype(BF), grad, preferred_element_type=F32)
        key_sum[part] += jnp.dot(score_grad, query, preferred_element_type=F32)
        dquery += jnp.dot(turned[:, part], score_grad, preferred_element_type=F32)
    dquery_ref[...] = dquery.T.astype(BF)

    @pl.when(block == pl.num_programs(1) - 1)
    def _():
        dkey_ref[...] = key_sum[:rows]
        dvalue_ref[...] = value_sum[:rows]
        dkey_far_ref[...] = key_sum[rows:].astype(BF)
        dvalue_far_ref[...] = value_sum[rows:].astype(BF)

    if sharing:

        @pl.when(now == count - 1)
        def _():
            for copy in far + passed:
                copy.wait_recv()
            for copy in near + far + passed:
                copy.wait_send()
            for copy in local:
                copy.wait()


def attend_back(qkv, kv_far, grad, mix, logs, heads, layer_back, per, parts, ident):
    rows, cols = qkv.shape[0], heads * DH
    away = kv_far.shape[0]
    block, step = min(512, rows), min(512, rows)
    sharing = parts == 4
    groups, piece, width = layer_back.shape

    def tile(offset):
        return pl.BlockSpec((block, DH), lambda h, i: (i, offset + h))

    def long(count, offset):
        return pl.BlockSpec((count, DH), lambda h, i: (0, offset + h))

    results = pl.pallas_call(
        functools.partial(attend_back_kernel, groups if sharing else 0, per, step),
        grid=(heads, rows // block),
        out_shape=(
            jax.ShapeDtypeStruct((rows, cols), BF),
            jax.ShapeDtypeStruct((rows, cols), F32),
            jax.ShapeDtypeStruct((rows, cols), F32),
            jax.ShapeDtypeStruct((away, cols), BF),
            jax.ShapeDtypeStruct((away, cols), BF),
        )
        + ((jax.ShapeDtypeStruct((groups, parts, piece, width), BF),) if sharing else ()),
        in_specs=[
            tile(0),
            long(rows, heads),
            long(rows, 2 * heads),
            long(away, 0),
            long(away, heads),
            tile(0),
            tile(0),
            pl.BlockSpec((1, 1, block), lambda h, i: (h, 0, i)),
        ]
        + ([ANY] if sharing else []),
        out_specs=(tile(0), long(rows, 0), long(rows, 0), long(away, 0), long(away, 0))
        + ((ANY,) if sharing else ()),
        scratch_shapes=[
            pltpu.VMEM((DH, rows + away), BF),
            pltpu.VMEM((rows + away, DH), F32),
            pltpu.VMEM((rows + away, DH), F32),
        ]
        + (
            [
                pltpu.SemaphoreType.DMA((3 * groups,)),
                pltpu.SemaphoreType.DMA((3 * groups,)),
                pltpu.SemaphoreType.DMA((groups,)),
            ]
            if sharing
            else []
        ),
        compiler_params=pltpu.CompilerParams(
            vmem_limit_bytes=52 * MIB,
            **(dict(collective_id=ident, has_side_effects=True) if sharing else {}),
        ),
        cost_estimate=pl.CostEstimate(
            flops=20 * rows * (rows + away) * cols,
            bytes_accessed=30 * rows * cols,
            transcendentals=rows * (rows + away) * heads,
        ),
        name="attend_back",
    )(qkv, qkv, qkv, kv_far, kv_far, grad, mix, logs, *([layer_back] if sharing else []))
    if sharing:
        return results
    layer = jnp.roll(layer_back, lax.axis_index("seq") // per, axis=0)
    return (*results, lax.all_gather(layer, "mp", axis=1))


def from_group_members(block, members, per):
    blocks = []
    for step in range(1, per):
        pairs = [
            (base + place, base + (place - step) % per)
            for base in range(0, members, per)
            for place in range(per)
        ]
        blocks.append(lax.ppermute(block, "seq", pairs))
    return blocks


def to_group_members(total, blocks, members, per):
    for step in range(1, per):
        pairs = [
            (base + place, base + (place + step) % per)
            for base in range(0, members, per)
            for place in range(per)
        ]
        total = total + lax.ppermute(blocks[step - 1], "seq", pairs).astype(F32)
    return total


def packed(vectors, lines):
    flat = jnp.concatenate(vectors)
    return jnp.pad(flat, (0, lines * 128 - flat.shape[0])).reshape(lines, 128)


def after(value, *others):
    return lax.optimization_barrier((value,) + others)[0]


def on_device(members, parts, *arrays):
    (
        tokens,
        query_weight,
        query_bias,
        key_weight,
        value_weight,
        value_bias,
        proj_weight,
        proj_bias,
        gain_first,
        shift_first,
        inner_weight,
        inner_bias,
        outer_weight,
        outer_bias,
        gain_second,
        shift_second,
        cotangent,
    ) = arrays
    micro, seqs, length, width = tokens.shape
    groups = micro * seqs
    per = members // groups
    assert per * groups == members
    piece = length // parts
    rows = groups * length
    quarter = groups * piece
    mine = lax.axis_index("mp")
    group = lax.axis_index("seq") // per

    depth, cols = query_weight.shape
    narrow = width // members
    heads = cols // DH
    proj_fold = proj_weight.reshape(-1, depth, narrow)
    folds = proj_fold.shape[0]
    first = jnp.concatenate(
        [query_weight, key_weight, value_weight] + [proj_fold[i] for i in range(folds)], axis=1
    )
    first = lax.all_gather(first, "seq", axis=0, tiled=True)
    w_inner = lax.all_gather(inner_weight, "seq", axis=0, tiled=True)
    w_outer = lax.all_gather(outer_weight, "seq", axis=1, tiled=True)
    w_qkv = first[:, : 3 * cols]
    w_proj = first[:, 3 * cols :].reshape(members, depth, folds, narrow)
    w_proj = w_proj.transpose(2, 1, 0, 3).reshape(folds * depth, width)
    vectors = [
        query_bias,
        value_bias,
        inner_bias,
        proj_bias,
        gain_first,
        shift_first,
        outer_bias,
        gain_second,
        shift_second,
    ]
    sizes = [vector.shape[0] for vector in vectors]
    lines = -(-sum(sizes) // 2048) * 16
    own_vectors = packed(vectors, lines)

    def to_blocks(array):
        array = array.reshape(groups, length, width)
        return [
            lax.dynamic_slice(
                array, (lax.rem(group + k, groups), mine * piece, 0), (1, piece, width)
            )[0]
            for k in range(groups)
        ]

    x_part, all_vectors = swap_groups(
        jnp.stack(to_blocks(tokens)),
        jnp.broadcast_to(own_vectors[None], (members, lines, 128)),
        members,
        parts,
        1,
        1,
    )
    x_part = x_part.reshape(quarter, width)
    x_rows = share_over_mp(x_part, parts, 7).reshape(rows, width)
    all_vectors = all_vectors.reshape(members, -1).astype(F32)
    full = []
    start = 0
    for size in sizes:
        full.append(all_vectors[:, start : start + size].reshape(-1))
        start += size
    b_query, b_value, b_inner, b_proj, gain_one, shift_one, b_outer, gain_two, shift_two = full

    bias = jnp.concatenate([b_query, jnp.zeros_like(b_query), b_value])
    qkv = (matmul(x_rows, w_qkv) + bias).astype(BF)
    kv_far = from_group_members(qkv[:, cols:], members, per)
    kv_far = kv_far[0] if per == 2 else jnp.concatenate(kv_far, axis=0)
    mixture, mixture_low, logs = attend(qkv, kv_far, heads)

    def blocked(array):
        return array.reshape(groups, piece, width)

    first_low, normal_one, inverse_one = first_norm(
        matmul(mixture_low, w_proj).astype(BF),
        blocked(x_part),
        jnp.stack([b_proj, gain_one, shift_one]),
        parts,
        2,
    )
    first_low = first_low.reshape(rows, width)

    inner_pre = matmul(first_low, w_inner) + b_inner
    active = gelu_tanh(inner_pre).astype(BF)
    second_low, second_grad, layer_back, sums = second_norm(
        matmul(active, w_outer).astype(BF),
        normal_one,
        jnp.stack(to_blocks(cotangent)),
        jnp.stack([gain_one, shift_one, b_outer, gain_two, shift_two]),
        members,
        parts,
        3,
    )
    second_low = second_low.reshape(rows, width)

    outer_w_part = over_rows(active, second_low).astype(BF)
    outer_w_grad = lax.psum_scatter(outer_w_part, "seq", scatter_dimension=1, tiled=True)
    second_low = after(second_low, outer_w_part)
    _, pull_gelu = jax.vjp(gelu_tanh, inner_pre)
    inner_grad = pull_gelu(over_cols(second_low, w_outer))[0].astype(BF)
    inner_b_grad = jnp.sum(inner_grad.astype(F32), axis=0)
    first_part = over_cols(inner_grad, w_inner).astype(BF)
    inner_w_part = over_rows(first_low, inner_grad).astype(BF)
    inner_w_grad = lax.psum_scatter(inner_w_part, "seq", scatter_dimension=0, tiled=True)
    attn_low, attn_grad, summed_rows = first_back(
        after(first_part, inner_w_part),
        second_grad,
        normal_one,
        inverse_one,
        sums,
        gain_one[None],
        parts,
        4,
    )
    attn_low = after(attn_low.reshape(rows, width), outer_w_grad)
    summed_rows = jnp.sum(summed_rows, axis=0)

    proj_w_part = over_rows(mixture_low, attn_low).astype(BF)
    proj_w_grad = lax.psum_scatter(proj_w_part, "seq", scatter_dimension=1, tiled=True)
    mixture_grad = over_cols(after(attn_low, proj_w_part), w_proj).astype(BF)
    query_grad, key_grad, value_grad, key_away, value_away, layer_out = attend_back(
        qkv, kv_far, mixture_grad, mixture, logs, heads, layer_back, per, parts, 5
    )

    def blocks_of(array):
        return [array[i * rows : (i + 1) * rows] for i in range(per - 1)]

    key_grad = to_group_members(key_grad, blocks_of(key_away), members, per)
    value_grad = to_group_members(value_grad, blocks_of(value_away), members, per)
    qkv_grad = jnp.concatenate([query_grad, key_grad.astype(BF), value_grad.astype(BF)], axis=1)
    qkv_w_part = over_rows(x_rows, qkv_grad).astype(BF)
    qkv_w_grad = lax.psum_scatter(qkv_w_part, "seq", scatter_dimension=0, tiled=True).astype(F32)
    qkv_grad = after(qkv_grad, qkv_w_part, inner_w_grad)
    bias_grad = jnp.sum(qkv_grad.astype(F32), axis=0)
    small = jnp.concatenate(
        [
            bias_grad[:cols].reshape(members, -1),
            bias_grad[2 * cols :].reshape(members, -1),
            inner_b_grad.reshape(members, -1),
        ]
        + [summed_rows[i].reshape(members, -1) for i in (3, 4, 5, 0, 1, 2)],
        axis=1,
    )
    small = jnp.pad(small, ((0, 0), (0, lines * 128 - small.shape[1])))
    input_grad, small = input_gradient(
        over_cols(qkv_grad, w_qkv).astype(BF),
        attn_grad,
        small.reshape(members, lines, 128),
        members,
        parts,
        6,
    )
    input_grad = after(input_grad, proj_w_grad).astype(F32).reshape(micro, seqs, length, width)
    layer_out = layer_out.reshape(micro, seqs, length, width)
    small = jnp.sum(small, axis=0).reshape(-1)
    pieces = []
    start = 0
    for size in sizes:
        pieces.append(small[start : start + size])
        start += size
    return (
        layer_out,
        input_grad,
        qkv_w_grad[:, :cols],
        pieces[0],
        qkv_w_grad[:, cols : 2 * cols],
        qkv_w_grad[:, 2 * cols :],
        pieces[1],
        proj_w_grad.astype(F32),
        pieces[3],
        pieces[4],
        pieces[5],
        inner_w_grad.astype(F32),
        pieces[2],
        outer_w_grad.astype(F32),
        pieces[6],
        pieces[7],
        pieces[8],
    )


def solution(mesh):
    tokens = P(None, None, "seq", None)
    rows_cols, cols_rows, both, seq = P("seq", "mp"), P("mp", "seq"), P(("mp", "seq")), P("seq")
    weights = (
        rows_cols,
        both,
        rows_cols,
        rows_cols,
        both,
        cols_rows,
        seq,
        seq,
        seq,
        rows_cols,
        both,
        cols_rows,
        seq,
        seq,
        seq,
    )
    return jax.shard_map(
        functools.partial(on_device, mesh.shape["seq"], mesh.shape["mp"]),
        mesh=mesh,
        in_specs=(tokens,) + weights + (tokens,),
        out_specs=(tokens, tokens) + weights,
        check_vma=False,
    )
```

time: 1030 us -> 728 us (0.71)
  matrix products: 235 us -> 138 us
  Pallas kernels: 551 us -> 459 us
  local copies, waits for them, and re-layouts: 87.9 us -> 37.3 us
  other arithmetic: 62.1 us -> 20.8 us
  blocking collectives: 13.4 us -> 0 us
    pallas_call x6 -> x1, Pallas kernels: 210 us -> 37.3 us  [share_over_mp(): pl.pallas_call(share_kernel, out_shape=jax.ShapeDtypeStruct((parts,) + ow...]
    dot_general x6 -> x0, matrix products: 91.2 us -> none  [the longest x1 20.3 us: on_device(): jnp.einsum('qhd,khd->hqk', mixture_grad, values, preferred_element_type=F32)]
    pallas_call x8 -> x7, Pallas kernels: 341 us -> 421 us  [the longest x4 305 us: exchange_call(): pl.pallas_call(kernel, out_shape=tuple((jax.ShapeDtypeStruct(shape, dtype...]
    reshape x9 -> x4, local copies, waits for them, and re-layouts: 34.9 us -> 3.89 us  [the longest x2 3.74 us: on_device(): w_proj = first[:, 3 * cols:].reshape(members, depth, folds, narrow)]
    all_gather x1, waiting for transfers between devices: 0.01 us -> 26.1 us  [on_device(): w_outer = lax.all_gather(outer_weight, 'seq', axis=1, tiled=True)]
    reduce_scatter x4, waiting for transfers between devices: 39.3 us -> 13.4 us  [the longest x1 13.4 us: on_device(): lax.psum_scatter(qkv_w_part, 'seq', scatter_dimension=0, tiled=True)]
    reduce_sum x10 -> x2, other arithmetic: 23 us -> 0.03 us  [the longest x1 0.02 us: on_device(): summed_rows = jnp.sum(summed_rows, axis=0)]
    psum x1 -> x0, blocking collectives: 13.4 us -> none  [on_device(): summed_rows = lax.psum(whole_rows, 'mp')]
  transfers between devices with their start and end apart: 9 -> 10, of which waited for: 2 -> 3; matrix products, arithmetic and copies ran while one was open for 22% -> 20% of each run, Pallas kernels for 41% -> 53%
where the time goes in v2:
time: 728 us; the launch traced here: 718 us
  Pallas kernels  459 us (63%)
  matrix products  138 us (19%)
  waiting for transfers between devices  43.4 us (6%)
  local copies, waits for them, and re-layouts  37.3 us (5%)
  other arithmetic  20.8 us (3%)
  between operations  15.2 us (2%)
    pallas_call x4, Pallas kernels, exchange_call(): pl.pallas_call(kernel, out_shape=tuple((jax.ShapeDtypeStruct(shape, dtype...  305 us
    pallas_call x1, Pallas kernels, swap_groups(): pl.pallas_call(functools.partial(swap_kernel, groups, per, sign), out_sha...  56.9 us
    dot_general x4, matrix products, over_cols(): lax.dot_general(left, right, (((1,), (1,)), ((), ())), preferred_element_...  49.8 us
    dot_general x4, matrix products, matmul(): return jnp.dot(left, right, preferred_element_type=F32)  45.2 us
    dot_general x4, matrix products, over_rows(): lax.dot_general(left, right, (((0,), (0,)), ((), ())), preferred_element_...  42.7 us
    pallas_call x1, Pallas kernels, share_over_mp(): pl.pallas_call(share_kernel, out_shape=jax.ShapeDtypeStruct((parts,) + ow...  37.3 us
    pallas_call x1, Pallas kernels, attend_back(): pl.pallas_call(functools.partial(attend_back_kernel, groups if sharing el...  37.2 us
    all_gather x1, waiting for transfers between devices, on_device(): w_outer = lax.all_gather(outer_weight, 'seq', axis=1, tiled=True)  26.1 us
  transfers between devices with their start and end apart: 10, of which 3 were waited for; matrix products, arithmetic and copies ran while one was open for 20% of the time, Pallas kernels for 53%

profile of v2, /device:TPU:9, one launch (start us, length us, event | category | flops | bytes accessed | tf_op | source)
XLA Modules:
  0.0 718.4 jit_solution(6129062487970381409)
XLA Ops:
  14.6 6.1 concatenate.15
  24.3 56.9 %swap_groups_1.1 = (bf16[4,64,2048]{2,1,0:T(8,128)(2,1)}, bf16[8,16,128]{2,1,0:T(8,128)(2,1)}) custom-call(bf16[4,64,2048]{2,1,0:T(8,128)(2,1)} %pad_maximum_fusion.1.block_ref, bf16[8,16,128]{2,1,0:T(8,128)(2,1)} %broadcast_in_dim.12.small_ref), custom_call_target="tpu_custom_call" | custom-call | bytes 62914560 | tf_op jit(solution)/shard_map/swap_groups_1/pallas_call | solution.py:594
  82.2 37.3 %share_over_mp_7.1 = bf16[4,256,2048]{2,1,0:T(8,128)(2,1)} custom-call(bf16[256,2048]{1,0:T(8,128)(2,1)} %bitcast.91), custom_call_target="tpu_custom_call" | custom-call | bytes 104857600 | tf_op jit(solution)/shard_map/share_over_mp_7/pallas_call | solution.py:529
  119.6 10.0 %add_convert_fusion.query_ref.key_ref.value_ref = bf16[1024,1536]{1,0:T(8,128)(2,1)S(1)} fusion(bf16[1024,2048]{1,0:T(8,128)(2,1)} %bitcast.98, bf16[2048,2048]{1,0:T(8,128)(2,1)} %all-gather.4.cloned.1.call-done, f32[1536]{0:T(1024)S(1)} %pad_maximum_fusion.4), kind=kOutput, calls=%fused_computation.15 | convolution fusion | flops 6445596672 | bytes 13637632 | tf_op jit(solution)/shard_map/dot_general | solution.py:21
  133.6 3.0 slice.186
  136.7 2.6 reshape.142
  141.1 21.6 %attend.1 = (f32[1024,512]{1,0:T(8,128)}, bf16[1024,512]{1,0:T(8,128)(2,1)S(1)}, f32[4,1,1024]{2,1,0:T(1,128)S(1)}) custom-call(bf16[1024,1536]{1,0:T(8,128)(2,1)} %copy-done.7, bf16[1024,1536]{1,0:T(8,128)(2,1)} %copy-done.7, bf16[1024,1536]{1,0:T(8,128)(2,1)} %copy-done.7, bf16[1024,1024]{1,0:T(8,128)(2,1)} %collective-permute-done.key_far_ref.value_far_ref, ...), custom_call_target="tpu_custom_call" | custom-call | flops 8589934592 | bytes 10485760 | tf_op jit(solution)/shard_map/attend/pallas_call | solution.py:655
  162.8 4.4 convolution_convert_fusion.5
  167.1 73.5 %exchange_2.1 = (bf16[4,4,64,2048]{3,2,1,0:T(8,128)(2,1)}, f32[4,64,2048]{2,1,0:T(8,128)}, f32[4,64,1]{2,1,0:T(8,128)S(1)}) custom-call(bf16[4,4,64,2048]{3,2,1,0:T(8,128)(2,1)} %bitcast.102, bf16[4,64,2048]{2,1,0:T(8,128)(2,1)S(1)} %copy-done, f32[3,2048]{1,0:T(4,128)S(1)} %pad_maximum_fusion.3.rows_ref), custom_call_target="tpu_custom_call" | custom-call | bytes 209715200 | tf_op jit(solution)/shard_map/exchange_2/pallas_call | solution.py:383
  240.6 14.8 %fusion.21 = f32[1024,2048]{1,0:T(8,128)} fusion(bf16[1024,2048]{1,0:T(8,128)(2,1)} %bitcast.121, bf16[2048,2048]{1,0:T(8,128)(2,1)} %all-gather.6.cloned.1.call-done), kind=kOutput, calls=%fused_computation.75 | convolution fusion | flops 8589934592 | bytes 20971520 | tf_op jit(solution)/shard_map/dot_general | solution.py:21
  255.5 26.1 %all-gather.8.cloned.1.call-done = bf16[2048,2048]{1,0:T(8,128)(2,1)} async-done(((bf16[2048,256]{1,0:T(8,128)(2,1)}), bf16[2048,2048]{1,0:T(8,128)(2,1)}) %all-gather.8.cloned.1.call-update) | async-done | bytes 8388624 | tf_op jit(solution)/shard_map/all_gather | solution.py:943
  281.5 16.0 %convolution_convert_fusion.4 = bf16[1024,2048]{1,0:T(8,128)(2,1)} fusion(bf16[2048,2048]{1,0:T(8,128)(2,1)} %all-gather.8.cloned.1.call-done, f32[1024,2048]{1,0:T(8,128)} %fusion.21, f32[2048]{0:T(1024)S(1)} %bitcast.118), kind=kOutput, calls=%fused_computation.22 | convolution fusion | flops 8613003264 | bytes 20979712 | tf_op jit(solution)/shard_map/dot_general | solution.py:21
  297.5 78.4 %exchange_3.1 = (bf16[4,4,64,2048]{3,2,1,0:T(8,128)(2,1)}, f32[4,64,2048]{2,1,0:T(8,128)}, bf16[4,64,2048]{2,1,0:T(8,128)(2,1)S(1)}, f32[8,2048]{1,0:T(8,128)S(1)}) custom-call(bf16[4,4,64,2048]{3,2,1,0:T(8,128)(2,1)} %bitcast.101, f32[4,64,2048]{2,1,0:T(8,128)} %get-tuple-element.50.normal_ref, bf16[4,64,2048]{2,1,0:T(8,128)(2,1)} %pad_maximum_fusion.2.cotan_ref, ...), custom_call_target="tpu_custom_call" | custom-call | bytes 209715200 | tf_op jit(solution)/shard_map/exchange_3/pallas_call | solution.py:383
  376.9 15.8 %convolution_convert_fusion.2 = bf16[2048,2048]{1,0:T(8,128)(2,1)} fusion(bf16[1024,2048]{1,0:T(8,128)(2,1)} %bitcast.123, f32[1024,2048]{1,0:T(8,128)} %fusion.21, f32[2048]{0:T(1024)S(1)} %bitcast.119), kind=kOutput, calls=%fused_computation.13 | convolution fusion | flops 8615100416 | bytes 20979712 | tf_op jit(solution)/shard_map/dot_general | solution.py:25
  392.8 19.0 %convert_reduce_fusion = (f32[2048]{0:T(1024)S(1)}, bf16[1024,2048]{1,0:T(8,128)(2,1)S(1)}) fusion(f32[1024,2048]{1,0:T(8,128)} %fusion.21, f32[2048]{0:T(1024)S(1)} %bitcast.120, bf16[1024,2048]{1,0:T(8,128)(2,1)} %bitcast.124, bf16[2048,2048]{1,0:T(8,128)(2,1)} %all-gather.8.cloned.1.call-done), kind=kOutput, calls=%fused_computation.9 | convolution fusion | flops 8638167040 | bytes 25182208 | tf_op jit(solution)/shard_map/dot_general | solution.py:29
  413.8 11.4 %convolution_convert_fusion.1 = bf16[2048,2048]{1,0:T(8,128)(2,1)} fusion(bf16[1024,2048]{1,0:T(8,128)(2,1)S(1)} %bitcast.122, bf16[1024,2048]{1,0:T(8,128)(2,1)S(1)} %get-tuple-element.82), kind=kOutput, calls=%fused_computation.12 | convolution fusion | flops 8594128896 | bytes 16777216 | tf_op jit(solution)/shard_map/dot_general | solution.py:25
  425.3 14.2 %convolution_convert_fusion.3 = bf16[1024,2048]{1,0:T(8,128)(2,1)} fusion(bf16[1024,2048]{1,0:T(8,128)(2,1)} %copy-done.10, bf16[2048,2048]{1,0:T(8,128)(2,1)} %all-gather.6.cloned.1.call-done), kind=kOutput, calls=%fused_computation.21 | convolution fusion | flops 8592031744 | bytes 16777216 | tf_op jit(solution)/shard_map/dot_general | solution.py:29
  439.5 75.6 %exchange_4.1 = (bf16[4,4,64,2048]{3,2,1,0:T(8,128)(2,1)}, f32[4,64,2048]{2,1,0:T(8,128)}, f32[4,8,2048]{2,1,0:T(8,128)S(1)}) custom-call(bf16[4,4,64,2048]{3,2,1,0:T(8,128)(2,1)} %bitcast.100, f32[4,64,2048]{2,1,0:T(8,128)} %get-tuple-element.54.grad_ref, f32[4,64,2048]{2,1,0:T(8,128)} %get-tuple-element.50.normal_ref, ...), custom_call_target="tpu_custom_call" | custom-call | bytes 209715200 | tf_op jit(solution)/shard_map/exchange_4/pallas_call | solution.py:383
  515.1 6.1 convolution_convert_fusion.6
  521.2 5.5 convolution_convert_fusion.7.grad_ref
  526.8 37.2 %attend_back.1 = (bf16[1024,512]{1,0:T(8,128)(2,1)S(1)}, f32[1024,512]{1,0:T(8,128)}, f32[1024,512]{1,0:T(8,128)}, bf16[1024,512]{1,0:T(8,128)(2,1)}, bf16[1024,...) custom-call(bf16[1024,1536]{1,0:T(8,128)(2,1)} %copy-done.7, bf16[1024,1536]{1,0:T(8,128)(2,1)} %copy-done.7, ...), custom_call_target="tpu_custom_call" | custom-call | flops 21474836480 | bytes 15728640 | tf_op jit(solution)/shard_map/attend_back/pallas_call | solution.py:816
  564.0 4.2 collective-permute-start.1
  568.3 2.4 collective-permute-done.1
  574.7 9.4 %convolution_convert_fusion = bf16[2048,1536]{1,0:T(8,128)(2,1)} fusion(bf16[1024,2048]{1,0:T(8,128)(2,1)S(1)} %bitcast.99, bf16[1024,512]{1,0:T(8,128)(2,1)S(1)} %add_convert_fusion.1, bf16[1024,512]{1,0:T(8,128)(2,1)S(1)} %add_convert_fusion.2, bf16[1024,512]{1,0:T(8,128)(2,1)S(1)} %get-tuple-element.64), kind=kOutput, calls=%fused_computation.11 | convolution fusion | flops 6455033856 | bytes 13631488 | tf_op jit(solution)/shard_map/dot_general | solution.py:25
  584.4 2.7 convert_element_type.100
  587.1 2.8 convert_element_type.99
  592.6 11.1 %fusion.11 = bf16[1024,2048]{1,0:T(8,128)(2,1)} fusion(bf16[1024,1536]{1,0:T(8,128)(2,1)} %copy-done.2, bf16[2048,2048]{1,0:T(8,128)(2,1)} %all-gather.4.cloned.1.call-done), kind=kOutput, calls=%fused_computation.20 | convolution fusion | flops 6444548096 | bytes 13631488 | tf_op jit(solution)/shard_map/dot_general | solution.py:29
  603.7 78.0 %exchange_6.1 = (bf16[4,4,64,2048]{3,2,1,0:T(8,128)(2,1)}, f32[8,16,128]{2,1,0:T(8,128)S(1)}) custom-call(bf16[4,4,64,2048]{3,2,1,0:T(8,128)(2,1)} %bitcast.103, f32[4,64,2048]{2,1,0:T(8,128)} %get-tuple-element.70.grad_ref, f32[8,16,128]{2,1,0:T(8,128)S(1)} %bitcast.92), custom_call_target="tpu_custom_call" | custom-call | bytes 209715200 | tf_op jit(solution)/shard_map/exchange_6/pallas_call | solution.py:383
  683.0 6.8 convert.2
  690.6 13.4 %reduce-scatter.11.cloned.1.call-done = bf16[256,1536]{1,0:T(8,128)(2,1)} async-done(((bf16[2048,1536]{1,0:T(8,128)(2,1)}), bf16[256,1536]{1,0:T(8,128)(2,1)}) %reduce-scatter.11.cloned.1.call-update) | async-done | bytes 786448 | tf_op jit(solution)/shard_map/reduce_scatter | solution.py:1056
  703.9 2.3 fusion.17
  706.3 4.8 copy.54
  (98 shorter events, 29.8 us)
Async XLA Ops:
  7.2 112.4 %all-gather.4.cloned.1.call-start = ((), (), s32[]{:S(2)}) async-start(), calls=%async_computation.4 | async-start | bytes 9437184 | tf_op jit(solution)/shard_map/all_gather | solution.py:941
  12.0 1.0 copy-start.6
  13.0 227.6 %all-gather.6.cloned.1.call-start = ((), (), s32[]{:S(2)}) async-start(), calls=%async_computation.5 | async-start | bytes 9437184 | tf_op jit(solution)/shard_map/all_gather | solution.py:942
  13.8 267.8 %all-gather.8.cloned.1.call-start = ((), (), s32[]{:S(2)}) async-start(), calls=%async_computation.6 | async-start | bytes 9437184 | tf_op jit(solution)/shard_map/all_gather | solution.py:943
  14.5 500.6 %reduce-scatter.5.cloned.1.call-start = ((), (), s32[]{:S(2)}) async-start(), calls=%async_computation.7 | async-start | bytes 9437184 | tf_op jit(solution)/shard_map/reduce_scatter | solution.py:1021
  129.7 2.8 copy-start.7
  131.5 9.7 %collective-permute-start = (bf16[1024,1024]{1,0:T(8,128)(2,1)}, bf16[1024,1024]{1,0:T(8,128)(2,1)}, u32[]{:S(2)}, u32[]{:S(2)}) collective-permute-start(bf16[1024,1024]{1,0:T(8,128)(2,1)} %slice.185), channel_id=1, source_target_pairs={{0,4},{4,0},{8,12},{12,8},{16,20},{20,16},{24,28},{28,24},{1,5},{5... | collective-permute-start | bytes 6291464 | tf_op jit(solution)/shard_map/ppermute | solution.py:879
  141.1 21.7 %copy-start.4 = (bf16[64,8,8,256]{3,1,2,0:T(8,128)(2,1)}, bf16[64,8,8,256]{3,1,2,0:T(8,128)(2,1)S(1)}, u32[]{:S(2)}) copy-start(bf16[64,8,8,256]{3,1,2,0:T(8,128)(2,1)S(1)} %copy.36) | copy-start | bytes 6291460
  162.8 4.4 copy-start
  375.9 1.0 copy-start.1
  392.8 194.3 %reduce-scatter.7.cloned.1.call-start = ((), (), s32[]{:S(2)}) async-start(), calls=%async_computation.8 | async-start | bytes 9437184 | tf_op jit(solution)/shard_map/reduce_scatter | solution.py:1028
  392.8 21.0 %copy-start.9 = (bf16[4,4,64,2048]{3,2,1,0:T(8,128)(2,1)S(1)}, bf16[4,4,64,2048]{3,2,1,0:T(8,128)(2,1)}, u32[]{:S(2)}) copy-start(bf16[4,4,64,2048]{3,2,1,0:T(8,128)(2,1)} %get-tuple-element.49) | copy-start | bytes 12582916
  411.8 2.0 copy-start.10
  425.2 257.7 %reduce-scatter.9.cloned.1.call-start = ((), (), s32[]{:S(2)}) async-start(), calls=%async_computation.9 | async-start | bytes 2359296 | tf_op jit(solution)/shard_map/reduce_scatter | solution.py:1043
  515.1 6.1 copy-start.5
  526.7 177.2 %reduce-scatter.11.cloned.1.call-start = ((), (), s32[]{:S(2)}) async-start(), calls=%async_computation.10 | async-start | bytes 7077888 | tf_op jit(solution)/shard_map/reduce_scatter | solution.py:1056
  564.0 10.7 %copy-start.3 = (bf16[4,256,2048]{2,1,0:T(8,128)(2,1)S(1)}, bf16[4,256,2048]{2,1,0:T(8,128)(2,1)}, u32[]{:S(2)}) copy-start(bf16[4,256,2048]{2,1,0:T(8,128)(2,1)} %share_over_mp_7.1) | copy-start | bytes 12582916
  564.0 6.7 collective-permute-start.1
  568.2 4.5 collective-permute-start.2
  590.1 1.7 copy-start.2
  683.0 6.8 copy-start.8
Sparse Core Ops, SparseCore 0:
  13.1 101.1 all-gather.3
  115.9 83.2 all-gather.5
  200.8 80.6 all-gather.7
  392.9 90.6 reduce-scatter.4
  486.3 87.6 reduce-scatter.6
  576.1 30.8 reduce-scatter.8
  609.3 94.6 reduce-scatter.10

commit v3 on v2

--- a/solution.py
+++ b/solution.py
@@ -64,9 +64,12 @@
 class Exchange:
     def __init__(self, part_ref, landed, relay, send_sem, recv_sem):
         self.me, self.along_x, self.along_y, self.across = square()
-        self.part, self.landed, self.relay = part_ref, landed, relay
+        self.parts, self.landed, self.relay = part_ref, landed, relay
         self.send = sender(send_sem, recv_sem)
         self.copies = {}
+
+    def part(self, owner, piece):
+        return self.parts.at[row_place(owner, piece, 2 * self.parts.shape[2])]
 
     def ways(self, index):
         pair = (self.along_x, self.along_y)
@@ -76,14 +79,14 @@
         near, _ = self.ways(index)
         for kind, owner in enumerate((self.across, near)):
             self.copies[index, kind] = self.send(
-                self.part.at[owner, piece], self.landed.at[index, kind], 6 * index + kind, {"mp": near}
+                self.part(owner, piece), self.landed.at[index, kind], 6 * index + kind, {"mp": near}
             )
 
     def pass_on(self, index, piece):
         _, far = self.ways(index)
         self.copies[index, 0].wait_recv()
         self.relay[index] = (
-            self.part[far, piece].astype(F32) + self.landed[index, 0].astype(F32)
+            self.part(far, piece)[...].astype(F32) + self.landed[index, 0].astype(F32)
         ).astype(BF)
         self.copies[index, 2] = self.send(
             self.relay.at[index], self.landed.at[index, 2], 6 * index + 2, {"mp": far}
@@ -93,7 +96,7 @@
         self.copies[index, 1].wait_recv()
         self.copies[index, 2].wait_recv()
         return (
-            self.part[self.me, piece].astype(F32)
+            self.part(self.me, piece)[...].astype(F32)
             + self.landed[index, 1].astype(F32)
             + self.landed[index, 2].astype(F32)
         )
@@ -108,18 +111,23 @@
         self.copies[index, 3].wait_recv()
         self.copies[index, 5] = self.send(target(near), target(near), 6 * index + 5, {"mp": far})
 
-    def finish(self, count):
-        for index in range(count):
+    def arrived(self, indices):
+        for index in indices:
             self.copies[index, 4].wait_recv()
             self.copies[index, 5].wait_recv()
+
+    def sent(self):
         for copy in self.copies.values():
             copy.wait_send()
 
-
-def piece_order(groups):
-    return list(range(1, groups, 2)) + list(range(0, groups, 2)) if groups == 2 else (
-        [1, 2, 0] + list(range(3, groups))
-    )
+    def finish(self, count):
+        self.arrived(range(count))
+        self.sent()
+
+
+def row_place(owner, piece, groups):
+    half = groups // 2
+    return piece // half, owner, piece % half
 
 
 def planes(groups, per):
@@ -142,17 +150,77 @@
     return inverse * (inner - mean_of(inner) - normal * mean_of(inner * normal))
 
 
-def run_pieces(exchange, groups, work):
-    order = piece_order(groups)
+class Product:
+    def __init__(self, exchange, turned, left_ref, weight_ref, weight, rows, load_sem):
+        self.exchange, self.turned = exchange, turned
+        self.left, self.weight, self.rows = left_ref, weight, rows
+        width = exchange.parts.shape[-1]
+        self.count = load_sem.shape[0]
+        self.step = width // self.count
+        depth = left_ref.shape[-1]
+        self.loads = []
+        for index in range(self.count):
+            span = pl.ds(index * self.step, self.step)
+            place = (span, pl.ds(0, depth)) if turned else (pl.ds(0, depth), span)
+            copy = pltpu.make_async_copy(
+                weight_ref.at[place], weight.at[place], load_sem.at[index]
+            )
+            copy.start()
+            self.loads.append(copy)
+
+    def make(self, batch, first=False):
+        _, _, half, piece_rows, _ = self.left.shape
+        for place, (owner, piece) in enumerate(batch):
+            self.rows[place * piece_rows : (place + 1) * piece_rows] = self.left[
+                row_place(owner, piece, 2 * half)
+            ]
+
+        def columns(index):
+            span = pl.ds(pl.multiple_of(index * self.step, self.step), self.step)
+            if self.turned:
+                product = over_cols(self.rows[...], self.weight[span])
+            else:
+                product = matmul(self.rows[...], self.weight[:, span])
+            product = product.astype(BF)
+            for place, (owner, piece) in enumerate(batch):
+                self.exchange.part(owner, piece)[:, span] = product[
+                    place * piece_rows : (place + 1) * piece_rows
+                ]
+
+        if first:
+            for index in range(self.count):
+                self.loads[index].wait()
+                columns(index)
+        else:
+            pl.loop(0, self.count)(columns)
+
+
+def run_pieces(exchange, order, work, product=None):
+    groups = len(order)
     places = list(enumerate(order))
     half = groups // 2
     first, second = places[:half], places[half:]
+
+    def make(half_places, near):
+        if product is None:
+            return
+        batch = []
+        for index, piece in half_places:
+            ways = exchange.ways(index)
+            owners = (exchange.across, ways[0]) if near else (ways[1], exchange.me)
+            batch += [(owner, piece) for owner in owners]
+        product.make(batch, near and half_places is first)
+
+    make(first, True)
     for index, piece in first:
         exchange.start(index, piece)
+    make(first, False)
     for index, piece in first:
         exchange.pass_on(index, piece)
+    make(second, True)
     for index, piece in second:
         exchange.start(index, piece)
+    make(second, False)
     for index, piece in first:
         work(index, piece, exchange.total(index, piece))
     for index, piece in second:
@@ -169,7 +237,7 @@
     local = []
 
     def target(piece):
-        return lambda device: low_ref.at[device, piece]
+        return lambda device: low_ref.at[row_place(device, piece, groups)]
 
     def work(index, piece, total):
         values = x_ref[piece].astype(F32) + total + rows_ref[0:1]
@@ -179,12 +247,12 @@
         ready[index] = (normal * rows_ref[1:2] + rows_ref[2:3]).astype(BF)
         exchange.share(index, ready.at[index], target(piece))
         copy = pltpu.make_async_copy(
-            ready.at[index], low_ref.at[exchange.me, piece], local_sem.at[index]
+            ready.at[index], target(piece)(exchange.me), local_sem.at[index]
         )
         copy.start()
         local.append(copy)
 
-    first, second = run_pieces(exchange, groups, work)
+    first, second = run_pieces(exchange, range(groups), work)
     for index, piece in first:
         exchange.forward(index, target(piece))
     for index, piece in second:
@@ -197,11 +265,13 @@
 
 
 def second_norm_kernel(
-    groups, per, part_ref, normal_ref, cotan_ref, rows_ref,
-    low_ref, grad_ref, back_ref, sums_ref,
-    landed, relay, ready, layer, cotan_in, send_sem, recv_sem, local_sem,
+    groups, per, left_ref, weight_ref, turned_ref, normal_ref, cotan_ref, rows_ref,
+    low_ref, grad_ref, back_ref, sums_ref, weight_grad_ref,
+    landed, relay, ready, layer, cotan_in, part_ref, weight, rows, load_sem, put_sem,
+    send_sem, recv_sem, local_sem,
 ):
     exchange = Exchange(part_ref, landed, relay, send_sem, recv_sem)
+    product = Product(exchange, False, left_ref, weight_ref, weight, rows, load_sem)
     peers = planes(groups, per)
     greet([{"mp": exchange.along_x}, {"mp": exchange.along_y}] + peers[1:])
     base = 6 * groups
@@ -213,7 +283,7 @@
     sums_ref[...] = jnp.zeros_like(sums_ref)
 
     def target(piece):
-        return lambda device: low_ref.at[device, piece]
+        return lambda device: low_ref.at[row_place(device, piece, groups)]
 
     def keep(source, place, slot):
         copy = pltpu.make_async_copy(source, place, local_sem.at[slot])
@@ -241,39 +311,77 @@
         grad_ref[piece] = grad
         ready[index] = grad.astype(BF)
         exchange.share(index, ready.at[index], target(piece))
-        keep(ready.at[index], low_ref.at[exchange.me, piece], index)
+        keep(ready.at[index], target(piece)(exchange.me), index)
         sums_ref[0:1] += jnp.sum(grad, axis=0, keepdims=True)
         sums_ref[1:2] += jnp.sum(cotan * normal, axis=0, keepdims=True)
         sums_ref[2:3] += jnp.sum(cotan, axis=0, keepdims=True)
 
-    first, second = run_pieces(exchange, groups, work)
+    first, second = run_pieces(exchange, range(groups), work, product)
     for index, piece in first:
         exchange.forward(index, target(piece))
     for index, piece in second:
         work(index, piece, exchange.total(index, piece))
     for index, piece in second:
         exchange.forward(index, target(piece))
-    exchange.finish(groups)
+    step = 256
+    count = weight.shape[1] // step
+    depth = turned_ref.shape[1] // 2
+
+    def columns(index):
+        return pl.ds(pl.multiple_of(index * step, step), step)
+
+    def put(index):
+        span = columns(index)
+        return pltpu.make_async_copy(
+            weight.at[:, span], weight_grad_ref.at[:, span], put_sem.at[index]
+        )
+
+    def product_of(part, span):
+        low = low_ref[part, :, :, :, span].reshape(depth, step)
+        return matmul(turned_ref[:, part * depth : (part + 1) * depth], low)
+
+    exchange.arrived([index for index, _ in first])
+    for copy in local[: len(first) + 1]:
+        copy.wait()
+
+    @pl.loop(0, count)
+    def _(index):
+        span = columns(index)
+        weight[:, span] = product_of(0, span).astype(BF)
+
+    exchange.arrived([index for index, _ in second])
+    for copy in local[len(first) + 1 :]:
+        copy.wait()
+
+    @pl.loop(0, count)
+    def _(index):
+        span = columns(index)
+        weight[:, span] = (product_of(1, span) + weight[:, span].astype(F32)).astype(BF)
+        put(index).start()
+
+    exchange.sent()
     for copy in leaving:
         copy.wait()
     for copy in arriving.values():
         copy.wait_send()
-    for copy in local:
-        copy.wait()
+    for index in range(count):
+        put(index).wait()
 
 
 def first_back_kernel(
-    groups, part_ref, grad_ref, normal_ref, inverse_ref, sums_in_ref, rows_ref,
+    groups, left_ref, weight_ref, grad_ref, normal_ref, inverse_ref, sums_in_ref, rows_ref,
     low_ref, out_ref, sums_ref,
-    landed, relay, ready, own_sums, send_sem, recv_sem, local_sem,
+    landed, relay, ready, own_sums, part_ref, weight, rows, load_sem,
+    send_sem, recv_sem, local_sem,
 ):
     exchange = Exchange(part_ref, landed, relay, send_sem, recv_sem)
+    product = Product(exchange, True, left_ref, weight_ref, weight, rows, load_sem)
     greet([{"mp": exchange.along_x}, {"mp": exchange.along_y}, {"mp": exchange.across}])
     local = []
     own_sums[...] = sums_in_ref[...]
 
     def target(piece):
-        return lambda device: low_ref.at[device, piece]
+        return lambda device: low_ref.at[row_place(device, piece, groups)]
 
     def keep(source, place, slot):
         copy = pltpu.make_async_copy(source, place, local_sem.at[slot])
@@ -287,12 +395,12 @@
         out_ref[piece] = moved
         ready[index] = moved.astype(BF)
         exchange.share(index, ready.at[index], target(piece))
-        keep(ready.at[index], low_ref.at[exchange.me, piece], index)
+        keep(ready.at[index], target(piece)(exchange.me), index)
         own_sums[3:4] += jnp.sum(moved, axis=0, keepdims=True)
         own_sums[4:5] += jnp.sum(grad * normal, axis=0, keepdims=True)
         own_sums[5:6] += jnp.sum(grad, axis=0, keepdims=True)
 
-    first, second = run_pieces(exchange, groups, work)
+    first, second = run_pieces(exchange, range(groups), work, product)
     for index, piece in first:
         exchange.forward(index, target(piece))
     for index, piece in second:
@@ -311,12 +419,18 @@
         copy.wait()
 
 
+def input_order(groups):
+    return list(range(1, groups - 1)) + [0, groups - 1]
+
+
 def input_kernel(
-    groups, per, part_ref, grad_ref, small_ref,
+    groups, per, left_ref, weight_ref, grad_ref, small_ref,
     all_ref, small_out,
-    landed, relay, ready, back, send_sem, recv_sem, local_sem,
+    landed, relay, ready, back, part_ref, weight, rows, load_sem,
+    send_sem, recv_sem, local_sem,
 ):
     exchange = Exchange(part_ref, landed, relay, send_sem, recv_sem)
+    product = Product(exchange, True, left_ref, weight_ref, weight, rows, load_sem)
     peers = planes(groups, per)
     members = groups * per
     here = lax.axis_index("seq")
@@ -361,7 +475,7 @@
         exchange.share(index, source, target(piece))
         keep(source, target(piece)(exchange.me), index)
 
-    first, second = run_pieces(exchange, groups, work)
+    first, second = run_pieces(exchange, input_order(groups), work, product)
     for index, piece in second:
         work(index, piece, exchange.total(index, piece))
     outward = [place for place in second if place[1] == 0] + first
@@ -379,11 +493,22 @@
         copy.wait()
 
 
-def exchange_call(kernel, ident, operands, results, groups, piece, width, scratch, extra):
+def product_scratch(parts, groups, piece, width, depth, turned):
+    return [
+        pltpu.VMEM((2, parts, groups // 2, piece, width), BF),
+        pltpu.VMEM((width, depth) if turned else (depth, width), BF),
+        pltpu.VMEM((groups * piece, depth), BF),
+        pltpu.SemaphoreType.DMA((width // 512,)),
+    ]
+
+
+def exchange_call(
+    kernel, ident, operands, results, groups, piece, width, scratch, extra, outside=()
+):
     return pl.pallas_call(
         kernel,
         out_shape=tuple(jax.ShapeDtypeStruct(shape, dtype) for shape, dtype, _ in results),
-        in_specs=[VMEM] * len(operands),
+        in_specs=[ANY if place in outside else VMEM for place in range(len(operands))],
         out_specs=tuple(spec for _, _, spec in results),
         scratch_shapes=[
             pltpu.VMEM((groups, 3, piece, width), BF),
@@ -397,7 +522,7 @@
             pltpu.SemaphoreType.DMA((groups + 1,)),
         ],
         compiler_params=pltpu.CompilerParams(
-            collective_id=ident, has_side_effects=True, vmem_limit_bytes=52 * MIB
+            collective_id=ident, has_side_effects=True, vmem_limit_bytes=58 * MIB
         ),
         cost_estimate=pl.CostEstimate(flops=0, bytes_accessed=200 * MIB, transcendentals=0),
         name=f"exchange_{ident}",
@@ -406,6 +531,7 @@
 
 def first_norm(part, x_part, rows, parts, ident):
     groups, piece, width = x_part.shape
+    half = groups // 2
     if parts != 4:
         total = lax.psum_scatter(part, "mp", scatter_dimension=0, tiled=True).astype(F32)
         values = x_part.astype(F32) + total.reshape(x_part.shape) + rows[0]
@@ -415,9 +541,9 @@
     return exchange_call(
         functools.partial(first_norm_kernel, groups),
         ident,
-        (part.reshape(parts, groups, piece, width), x_part, rows),
+        (part.reshape(2, parts, half, piece, width), x_part, rows),
         [
-            ((parts, groups, piece, width), BF, ANY),
+            ((2, parts, half, piece, width), BF, ANY),
             ((groups, piece, width), F32, VMEM),
             ((groups, piece, 1), F32, VMEM),
         ],
@@ -425,9 +551,12 @@
     )
 
 
-def second_norm(part, normal, cotan, rows, members, parts, ident):
+def second_norm(left, weight, turned, normal, cotan, rows, members, parts, ident):
     groups, piece, width = normal.shape
+    depth = left.shape[-1]
+    half = groups // 2
     if parts != 4:
+        part = matmul(left, weight).astype(BF)
         total = lax.psum_scatter(part, "mp", scatter_dimension=0, tiled=True).astype(F32)
         values = normal * rows[0] + rows[1] + total.reshape(normal.shape) + rows[2]
         normal, inverse = normed(values)
@@ -437,26 +566,33 @@
         grad = norm_back(cotan, normal, inverse, rows[3])
         sums = [jnp.sum(array, axis=(0, 1)) for array in (grad, cotan * normal, cotan)]
         sums = jnp.stack(sums + [jnp.zeros_like(sums[0])] * 5)
-        return lax.all_gather(grad.astype(BF), "mp", axis=0), grad, back, sums
+        low = lax.all_gather(grad.astype(BF), "mp", axis=0)
+        return low, grad, back, sums, matmul(turned, low.reshape(-1, width)).astype(BF)
     return exchange_call(
         functools.partial(second_norm_kernel, groups, members // groups),
         ident,
-        (part.reshape(parts, groups, piece, width), normal, cotan, rows),
+        (left.reshape(2, parts, half, piece, depth), weight, turned, normal, cotan, rows),
         [
-            ((parts, groups, piece, width), BF, ANY),
+            ((2, parts, half, piece, width), BF, VMEM),
             ((groups, piece, width), F32, VMEM),
             ((groups, piece, width), BF, ANY),
             ((8, width), F32, VMEM),
+            ((depth, width), BF, ANY),
         ],
         groups, piece, width,
-        [pltpu.VMEM((groups, piece, width), BF), pltpu.VMEM((groups, piece, width), BF)],
+        [pltpu.VMEM((groups, piece, width), BF), pltpu.VMEM((groups, piece, width), BF)]
+        + product_scratch(parts, groups, piece, width, depth, False)
+        + [pltpu.SemaphoreType.DMA((width // 256,))],
         2 * groups,
-    )
-
-
-def first_back(part, grad, normal, inverse, sums, rows, parts, ident):
+        (1,),
+    )
+
+
+def first_back(left, weight, grad, normal, inverse, sums, rows, parts, ident):
     groups, piece, width = normal.shape
+    depth = left.shape[-1]
     if parts != 4:
+        part = over_cols(left, weight).astype(BF)
         total = lax.psum_scatter(part, "mp", scatter_dimension=0, tiled=True).astype(F32)
         grad = total.reshape(normal.shape) + grad
         moved = norm_back(grad, normal, inverse, rows[0])
@@ -467,22 +603,32 @@
             moved,
             lax.all_gather(sums, "mp", axis=0),
         )
+    half = groups // 2
     return exchange_call(
         functools.partial(first_back_kernel, groups),
         ident,
-        (part.reshape(parts, groups, piece, width), grad, normal, inverse, sums, rows),
+        (
+            left.reshape(2, parts, half, piece, depth), weight,
+            grad, normal, inverse, sums, rows,
+        ),
         [
-            ((parts, groups, piece, width), BF, ANY),
+            ((2, parts, half, piece, width), BF, ANY),
             ((groups, piece, width), F32, VMEM),
             ((parts, 8, width), F32, VMEM),
         ],
-        groups, piece, width, [pltpu.VMEM((8, width), F32)], 3,
-    )
-
-
-def input_gradient(part, grad, small, members, parts, ident):
+        groups, piece, width,
+        [pltpu.VMEM((8, width), F32)]
+        + product_scratch(parts, groups, piece, width, depth, True),
+        3,
+        (1,),
+    )
+
+
+def input_gradient(left, weight, grad, small, members, parts, ident):
     groups, piece, width = grad.shape
+    depth = left.shape[-1]
     if parts != 4:
+        part = over_cols(left, weight[:, :depth]).astype(BF)
         total = lax.psum_scatter(part, "mp", scatter_dimension=0, tiled=True).astype(F32)
         ready = (total.reshape(grad.shape) + grad).astype(BF)
         back = jnp.stack(swap_blocks(ready, members, -1))
@@ -491,9 +637,13 @@
     return exchange_call(
         functools.partial(input_kernel, groups, members // groups),
         ident,
-        (part.reshape(parts, groups, piece, width), grad, small),
+        (left.reshape(2, parts, groups // 2, piece, depth), weight, grad, small),
         [((groups, parts, piece, width), BF, ANY), (small.shape, F32, VMEM)],
-        groups, piece, width, [pltpu.VMEM((groups, piece, width), BF)], groups + members,
+        groups, piece, width,
+        [pltpu.VMEM((groups, piece, width), BF)]
+        + product_scratch(parts, groups, piece, width, depth, True),
+        groups + members,
+        (1,),
     )
 
 
@@ -505,22 +655,27 @@
     half = own_ref.shape[0] // 2
     upper, lower = pl.ds(0, half), pl.ds(half, half)
     copies = [
-        send(own_ref.at[upper], all_ref.at[me, upper], 0, to_x),
-        send(own_ref.at[lower], all_ref.at[me, lower], 1, to_y),
-        send(own_ref.at[lower], all_ref.at[me, lower], 2, to_x),
-        send(own_ref.at[upper], all_ref.at[me, upper], 3, to_y),
+        send(own_ref.at[upper], all_ref.at[0, me], 0, to_x),
+        send(own_ref.at[lower], all_ref.at[1, me], 1, to_y),
+        send(own_ref.at[lower], all_ref.at[1, me], 2, to_x),
+        send(own_ref.at[upper], all_ref.at[0, me], 3, to_y),
     ]
-    local = pltpu.make_async_copy(own_ref, all_ref.at[me], local_sem)
-    local.start()
+    local = [
+        pltpu.make_async_copy(own_ref.at[upper], all_ref.at[0, me], local_sem.at[0]),
+        pltpu.make_async_copy(own_ref.at[lower], all_ref.at[1, me], local_sem.at[1]),
+    ]
+    for copy in local:
+        copy.start()
     copies[0].wait_recv()
-    copies.append(send(all_ref.at[along_x, upper], all_ref.at[along_x, upper], 4, to_y))
+    copies.append(send(all_ref.at[0, along_x], all_ref.at[0, along_x], 4, to_y))
     copies[1].wait_recv()
-    copies.append(send(all_ref.at[along_y, lower], all_ref.at[along_y, lower], 5, to_x))
+    copies.append(send(all_ref.at[1, along_y], all_ref.at[1, along_y], 5, to_x))
     for copy in copies[2:]:
         copy.wait_recv()
     for copy in copies:
         copy.wait_send()
-    local.wait()
+    for copy in local:
+        copy.wait()
 
 
 def share_over_mp(own, parts, ident):
@@ -528,13 +683,13 @@
         return lax.all_gather(own, "mp", axis=0)
     return pl.pallas_call(
         share_kernel,
-        out_shape=jax.ShapeDtypeStruct((parts,) + own.shape, own.dtype),
+        out_shape=jax.ShapeDtypeStruct((2, parts, own.shape[0] // 2, own.shape[1]), own.dtype),
         in_specs=[ANY],
         out_specs=ANY,
         scratch_shapes=[
             pltpu.SemaphoreType.DMA((6,)),
             pltpu.SemaphoreType.DMA((6,)),
-            pltpu.SemaphoreType.DMA,
+            pltpu.SemaphoreType.DMA((2,)),
         ],
         compiler_params=pltpu.CompilerParams(collective_id=ident, has_side_effects=True),
         cost_estimate=pl.CostEstimate(flops=0, bytes_accessed=100 * MIB, transcendentals=0),
@@ -748,7 +903,7 @@
             for copy in near + far + local:
                 copy.start()
 
-        @pl.when(now == count * 5 // 8)
+        @pl.when(now == count * 3 // 8)
         def _():
             for first, second in zip(near, passed):
                 first.wait_recv()
@@ -891,6 +1046,57 @@
     return total
 
 
+def last_kernel(
+    turned_ref, query_ref, key_ref, value_ref, key_in_ref, value_in_ref, proj_ref,
+    grad_ref, sums_ref, part_ref, made, copy_sem,
+):
+    rows, cols = query_ref.shape
+    copies = [
+        pltpu.make_async_copy(proj_ref, part_ref.at[:, pl.ds(3 * cols, cols)], copy_sem.at[3])
+    ]
+    copies[0].start()
+    for index, (own, far) in enumerate(
+        ((query_ref, None), (key_ref, key_in_ref), (value_ref, value_in_ref))
+    ):
+        span = pl.ds(index * cols, cols)
+        grad = own[...] if far is None else (own[...] + far[...].astype(F32)).astype(BF)
+        grad_ref[:, span] = grad
+        sums_ref[:, span] = jnp.sum(grad.astype(F32), axis=0, keepdims=True)
+        step = 512
+
+        @pl.loop(0, turned_ref.shape[0] // step)
+        def _(place, index=index, span=span):
+            block = pl.ds(pl.multiple_of(place * step, step), step)
+            made[index, block] = matmul(turned_ref[block], grad_ref[:, span]).astype(BF)
+
+        copy = pltpu.make_async_copy(made.at[index], part_ref.at[:, span], copy_sem.at[index])
+        copy.start()
+        copies.append(copy)
+    for copy in copies:
+        copy.wait()
+
+
+def last_gradients(turned, query, key, value, key_in, value_in, proj_part):
+    rows, cols = query.shape
+    width = turned.shape[0]
+    return pl.pallas_call(
+        last_kernel,
+        out_shape=(
+            jax.ShapeDtypeStruct((rows, 3 * cols), BF),
+            jax.ShapeDtypeStruct((1, 3 * cols), F32),
+            jax.ShapeDtypeStruct((width, 4 * cols), BF),
+        ),
+        in_specs=[VMEM] * 7,
+        out_specs=(VMEM, VMEM, ANY),
+        scratch_shapes=[pltpu.VMEM((3, width, cols), BF), pltpu.SemaphoreType.DMA((4,))],
+        compiler_params=pltpu.CompilerParams(vmem_limit_bytes=48 * MIB),
+        cost_estimate=pl.CostEstimate(
+            flops=6 * rows * width * cols, bytes_accessed=32 * MIB, transcendentals=0
+        ),
+        name="last_gradients",
+    )(turned, query, key, value, key_in, value_in, proj_part)
+
+
 def packed(vectors, lines):
     flat = jnp.concatenate(vectors)
     return jnp.pad(flat, (0, lines * 128 - flat.shape[0])).reshape(lines, 128)
@@ -1006,8 +1212,11 @@
 
     inner_pre = matmul(first_low, w_inner) + b_inner
     active = gelu_tanh(inner_pre).astype(BF)
-    second_low, second_grad, layer_back, sums = second_norm(
-        matmul(active, w_outer).astype(BF),
+    active_turned, x_turned, active = lax.optimization_barrier((active.T, x_rows.T, active))
+    second_low, second_grad, layer_back, sums, outer_w_part = second_norm(
+        active,
+        w_outer,
+        active_turned,
         normal_one,
         jnp.stack(to_blocks(cotangent)),
         jnp.stack([gain_one, shift_one, b_outer, gain_two, shift_two]),
@@ -1017,21 +1226,19 @@
     )
     second_low = second_low.reshape(rows, width)
 
-    outer_w_part = over_rows(active, second_low).astype(BF)
     outer_w_grad = lax.psum_scatter(outer_w_part, "seq", scatter_dimension=1, tiled=True)
-    second_low = after(second_low, outer_w_part)
     _, pull_gelu = jax.vjp(gelu_tanh, inner_pre)
     inner_grad = pull_gelu(over_cols(second_low, w_outer))[0].astype(BF)
     inner_b_grad = jnp.sum(inner_grad.astype(F32), axis=0)
-    first_part = over_cols(inner_grad, w_inner).astype(BF)
     inner_w_part = over_rows(first_low, inner_grad).astype(BF)
     inner_w_grad = lax.psum_scatter(inner_w_part, "seq", scatter_dimension=0, tiled=True)
     attn_low, attn_grad, summed_rows = first_back(
-        after(first_part, inner_w_part),
+        inner_grad,
+        w_inner,
         second_grad,
         normal_one,
         inverse_one,
-        sums,
+        after(sums, inner_w_part),
         gain_one[None],
         parts,
         4,
@@ -1039,8 +1246,7 @@
     attn_low = after(attn_low.reshape(rows, width), outer_w_grad)
     summed_rows = jnp.sum(summed_rows, axis=0)
 
-    proj_w_part = over_rows(mixture_low, attn_low).astype(BF)
-    proj_w_grad = lax.psum_scatter(proj_w_part, "seq", scatter_dimension=1, tiled=True)
+    proj_w_part = over_rows(attn_low, mixture_low).astype(BF)
     mixture_grad = over_cols(after(attn_low, proj_w_part), w_proj).astype(BF)
     query_grad, key_grad, value_grad, key_away, value_away, layer_out = attend_back(
         qkv, kv_far, mixture_grad, mixture, logs, heads, layer_back, per, parts, 5
@@ -1049,13 +1255,25 @@
     def blocks_of(array):
         return [array[i * rows : (i + 1) * rows] for i in range(per - 1)]
 
-    key_grad = to_group_members(key_grad, blocks_of(key_away), members, per)
-    value_grad = to_group_members(value_grad, blocks_of(value_away), members, per)
-    qkv_grad = jnp.concatenate([query_grad, key_grad.astype(BF), value_grad.astype(BF)], axis=1)
-    qkv_w_part = over_rows(x_rows, qkv_grad).astype(BF)
-    qkv_w_grad = lax.psum_scatter(qkv_w_part, "seq", scatter_dimension=0, tiled=True).astype(F32)
-    qkv_grad = after(qkv_grad, qkv_w_part, inner_w_grad)
-    bias_grad = jnp.sum(qkv_grad.astype(F32), axis=0)
+    if parts == 4 and per == 2:
+        pairs = [(index, index + 1 - 2 * (index % 2)) for index in range(members)]
+        qkv_grad, bias_grad, last_w_part = last_gradients(
+            x_turned,
+            query_grad,
+            key_grad,
+            value_grad,
+            lax.ppermute(key_away, "seq", pairs),
+            lax.ppermute(value_away, "seq", pairs),
+            proj_w_part,
+        )
+        bias_grad = bias_grad[0]
+    else:
+        key_grad = to_group_members(key_grad, blocks_of(key_away), members, per)
+        value_grad = to_group_members(value_grad, blocks_of(value_away), members, per)
+        qkv_grad = jnp.concatenate([query_grad, key_grad.astype(BF), value_grad.astype(BF)], axis=1)
+        last_w_part = jnp.concatenate([matmul(x_turned, qkv_grad).astype(BF), proj_w_part], axis=1)
+        bias_grad = jnp.sum(qkv_grad.astype(F32), axis=0)
+    last_w_grad = lax.psum_scatter(last_w_part, "seq", scatter_dimension=0, tiled=True).astype(F32)
     small = jnp.concatenate(
         [
             bias_grad[:cols].reshape(members, -1),
@@ -1067,14 +1285,15 @@
     )
     small = jnp.pad(small, ((0, 0), (0, lines * 128 - small.shape[1])))
     input_grad, small = input_gradient(
-        over_cols(qkv_grad, w_qkv).astype(BF),
+        qkv_grad,
+        first,
         attn_grad,
         small.reshape(members, lines, 128),
         members,
         parts,
         6,
     )
-    input_grad = after(input_grad, proj_w_grad).astype(F32).reshape(micro, seqs, length, width)
+    input_grad = after(input_grad, inner_w_grad).astype(F32).reshape(micro, seqs, length, width)
     layer_out = layer_out.reshape(micro, seqs, length, width)
     small = jnp.sum(small, axis=0).reshape(-1)
     pieces = []
@@ -1085,12 +1304,12 @@
     return (
         layer_out,
         input_grad,
-        qkv_w_grad[:, :cols],
+        last_w_grad[:, :cols],
         pieces[0],
-        qkv_w_grad[:, cols : 2 * cols],
-        qkv_w_grad[:, 2 * cols :],
+        last_w_grad[:, cols : 2 * cols],
+        last_w_grad[:, 2 * cols : 3 * cols],
         pieces[1],
-        proj_w_grad.astype(F32),
+        last_w_grad[:, 3 * cols :].T,
         pieces[3],
         pieces[4],
         pieces[5],

time: 728 us -> 700 us (0.962)
  matrix products: 138 us -> 68.4 us
  Pallas kernels: 459 us -> 494 us
  local copies, waits for them, and re-layouts: 37.3 us -> 62.2 us
  waiting for transfers between devices: 43.4 us -> 24.7 us
    dot_general x4 -> x2, matrix products: 49.8 us -> 20.2 us  [over_cols(): lax.dot_general(left, right, (((1,), (1,)), ((), ())), preferred_element_...]
    dot_general x4 -> x2, matrix products: 42.7 us -> 17.5 us  [over_rows(): lax.dot_general(left, right, (((0,), (0,)), ((), ())), preferred_element_...]
    all_gather x1, waiting for transfers between devices: 26.1 us -> 3.19 us  [on_device(): w_outer = lax.all_gather(outer_weight, 'seq', axis=1, tiled=True)]
    pallas_call x4, Pallas kernels: 305 us -> 325 us  [exchange_call(): pl.pallas_call(kernel, out_shape=tuple((jax.ShapeDtypeStruct(shape, dtype...]
    pallas_call x1 -> x2, Pallas kernels: 37.3 us -> 53.3 us  [the longest x1 37.3 us: share_over_mp(): pl.pallas_call(share_kernel, out_shape=jax.ShapeDtypeStruct((2, parts, ow...]
    dot_general x4 -> x3, matrix products: 45.2 us -> 30.8 us  [matmul(): return jnp.dot(left, right, preferred_element_type=F32)]
    unnamed x39 -> x38, local copies, waits for them, and re-layouts: 15.1 us -> 21.7 us
    reduce_scatter x2 -> x1, waiting for transfers between devices: 13.4 us -> 15.9 us  [on_device(): lax.psum_scatter(last_w_part, 'seq', scatter_dimension=0, tiled=True)]
  transfers between devices with their start and end apart: 10 -> 9, of which waited for: 3 -> 4; matrix products, arithmetic and copies ran while one was open for 20% -> 18% of each run, Pallas kernels for 53% -> 58%
where the time goes in v3:
time: 700 us; the launch traced here: 690 us
  Pallas kernels  494 us (71%)
  matrix products  68.4 us (10%)
  local copies, waits for them, and re-layouts  62.2 us (9%)
  waiting for transfers between devices  24.7 us (4%)
  other arithmetic  21.2 us (3%)
  between operations  14.8 us (2%)
    pallas_call x4, Pallas kernels, exchange_call(): pl.pallas_call(kernel, out_shape=tuple((jax.ShapeDtypeStruct(shape, dtype...  325 us
    pallas_call x1, Pallas kernels, swap_groups(): pl.pallas_call(functools.partial(swap_kernel, groups, per, sign), out_sha...  56.9 us
    pallas_call x1, Pallas kernels, share_over_mp(): pl.pallas_call(share_kernel, out_shape=jax.ShapeDtypeStruct((2, parts, ow...  37.3 us
    pallas_call x1, Pallas kernels, attend_back(): pl.pallas_call(functools.partial(attend_back_kernel, groups if sharing el...  37.3 us
    dot_general x3, matrix products, matmul(): return jnp.dot(left, right, preferred_element_type=F32)  30.8 us
    unnamed x38, local copies, waits for them, and re-layouts  21.7 us
    pallas_call x1, Pallas kernels, attend(): pl.pallas_call(attend_kernel, grid=(heads, rows // block), out_shape=(jax...  20.9 us
    dot_general x2, matrix products, over_cols(): lax.dot_general(left, right, (((1,), (1,)), ((), ())), preferred_element_...  20.2 us
  transfers between devices with their start and end apart: 9, of which 4 were waited for; matrix products, arithmetic and copies ran while one was open for 18% of the time, Pallas kernels for 58%

profile of v3, /device:TPU:9, one launch (start us, length us, event | category | flops | bytes accessed | tf_op | source)
XLA Modules:
  0.0 690.0 jit_solution(6082176241647705069)
XLA Ops:
  14.6 6.1 concatenate.12
  24.3 56.9 %swap_groups_1.1 = (bf16[4,64,2048]{2,1,0:T(8,128)(2,1)}, bf16[8,16,128]{2,1,0:T(8,128)(2,1)}) custom-call(bf16[4,64,2048]{2,1,0:T(8,128)(2,1)} %pad_maximum_fusion.block_ref, bf16[8,16,128]{2,1,0:T(8,128)(2,1)} %broadcast_in_dim.12.small_ref), custom_call_target="tpu_custom_call" | custom-call | bytes 62914560 | tf_op jit(solution)/shard_map/swap_groups_1/pallas_call | solution.py:749
  82.2 37.3 %share_over_mp_7.1 = bf16[2,4,128,2048]{3,2,1,0:T(8,128)(2,1)} custom-call(bf16[256,2048]{1,0:T(8,128)(2,1)} %bitcast.96), custom_call_target="tpu_custom_call" | custom-call | bytes 104857600 | tf_op jit(solution)/shard_map/share_over_mp_7/pallas_call | solution.py:684
  119.6 10.0 %add_convert_fusion.query_ref.key_ref.value_ref = bf16[1024,1536]{1,0:T(8,128)(2,1)S(1)} fusion(bf16[1024,2048]{1,0:T(8,128)(2,1)} %bitcast.91, bf16[2048,2048]{1,0:T(8,128)(2,1)} %all-gather.4.cloned.1.call-done.weight_ref, f32[1536]{0:T(1024)S(1)} %pad_maximum_fusion.3), kind=kOutput, calls=%fused_computation.23 | convolution fusion | flops 6445596672 | bytes 13637632 | tf_op jit(solution)/shard_map/dot_general | solution.py:21
  133.7 6.4 copy.51
  142.7 2.0 reshape.130
  144.7 2.8 copy.42
  148.2 20.9 %attend.1 = (f32[1024,512]{1,0:T(8,128)}, bf16[1024,512]{1,0:T(8,128)(2,1)S(1)}, f32[4,1,1024]{2,1,0:T(1,128)S(1)}) custom-call(bf16[1024,1536]{1,0:T(8,128)(2,1)} %copy-done.4, bf16[1024,1536]{1,0:T(8,128)(2,1)} %copy-done.4, bf16[1024,1536]{1,0:T(8,128)(2,1)} %copy-done.4, bf16[1024,1024]{1,0:T(8,128)(2,1)} %collective-permute-done.key_far_ref.value_far_ref, ...), custom_call_target="tpu_custom_call" | custom-call | flops 8589934592 | bytes 10485760 | tf_op jit(solution)/shard_map/attend/pallas_call | solution.py:810
  169.1 4.4 convolution_convert_fusion.1
  173.5 74.2 %exchange_2.1 = (bf16[2,4,2,64,2048]{4,3,2,1,0:T(8,128)(2,1)}, f32[4,64,2048]{2,1,0:T(8,128)}, f32[4,64,1]{2,1,0:T(8,128)}) custom-call(bf16[2,4,2,64,2048]{4,3,2,1,0:T(8,128)(2,1)} %bitcast.97, bf16[4,64,2048]{2,1,0:T(8,128)(2,1)} %get-tuple-element.51.x_ref, f32[3,2048]{1,0:T(4,128)} %pad_maximum_fusion.2.rows_ref), custom_call_target="tpu_custom_call" | custom-call | bytes 209715200 | tf_op jit(solution)/shard_map/exchange_2/pallas_call | solution.py:508
  247.7 16.4 %fusion.14 = (bf16[2048,1024]{1,0:T(8,128)(2,1)}, f32[1024,2048]{0,1:T(8,128)S(1)}) fusion(f32[2048]{0:T(1024)S(1)} %bitcast.118, bf16[1024,2048]{1,0:T(8,128)(2,1)} %bitcast.121, bf16[2048,2048]{1,0:T(8,128)(2,1)} %all-gather.6.cloned.1.call-done.weight_ref), kind=kOutput, calls=%fused_computation.17 | convolution fusion | flops 8610906112 | bytes 25174016 | tf_op jit(solution)/shard_map/dot_general | solution.py:21
  264.1 3.4 copy-done.1
  267.5 4.3 multiply_convert_fusion
  271.8 6.5 copy.44
  278.3 3.2 all-gather.8.cloned.1.call-done.weight_ref
  281.5 90.3 %exchange_3.1 = (bf16[2,4,2,64,2048]{4,3,2,1,0:T(8,128)(2,1)}, f32[4,64,2048]{2,1,0:T(8,128)}, bf16[4,64,2048]{2,1,0:T(8,128)(2,1)}, f32[8,2048]{1,0:T(8,128)}, bf16[2048,2048]{1,0:T(8,128)(2,1)}) custom-call(bf16[2,4,2,64,2048]{4,3,2,1,0:T(8,128)(2,1)} %bitcast.90, bf16[2048,2048]{1,0:T(8,128)(2,1)} %all-gather.8.cloned.1.call-done.weight_ref, ...), custom_call_target="tpu_custom_call" | custom-call | bytes 209715200 | tf_op jit(solution)/shard_map/exchange_3/pallas_call | solution.py:508
  371.9 16.8 %convert_reduce_fusion = (f32[2048]{0:T(1024)S(1)}, bf16[1024,2048]{0,1:T(8,128)(2,1)S(1)}) fusion(f32[1024,2048]{0,1:T(8,128)} %copy-done.1, f32[2048]{0:T(1024)S(1)} %bitcast.120, bf16[1024,2048]{1,0:T(8,128)(2,1)} %bitcast.123, bf16[2048,2048]{1,0:T(8,128)(2,1)} %all-gather.8.cloned.1.call-done.weight_ref), kind=kOutput, calls=%fused_computation.18 | convolution fusion | flops 8638167040 | bytes 25182208 | tf_op jit(solution)/shard_map/dot_general | solution.py:29
  390.8 11.4 %convolution_convert_fusion = bf16[2048,2048]{1,0:T(8,128)(2,1)} fusion(bf16[1024,2048]{1,0:T(8,128)(2,1)S(1)} %bitcast.122, bf16[1024,2048]{0,1:T(8,128)(2,1)S(1)} %get-tuple-element.128), kind=kOutput, calls=%fused_computation.20 | convolution fusion | flops 8594128896 | bytes 16777216 | tf_op jit(solution)/shard_map/dot_general | solution.py:25
  402.2 7.0 %copy.47 = bf16[1024,2048]{1,0:T(8,128)(2,1)} copy(bf16[1024,2048]{0,1:T(8,128)(2,1)} %copy-done.2) | data formatting | bytes 8388608 | tf_op jit(solution)/shard_map/convert_element_type | solution.py:1231
  409.1 79.9 %exchange_4.1 = (bf16[2,4,2,64,2048]{4,3,2,1,0:T(8,128)(2,1)}, f32[4,64,2048]{2,1,0:T(8,128)}, f32[4,8,2048]{2,1,0:T(8,128)}) custom-call(bf16[2,4,2,64,2048]{4,3,2,1,0:T(8,128)(2,1)} %bitcast.93, bf16[2048,2048]{1,0:T(8,128)(2,1)} %all-gather.6.cloned.1.call-done.weight_ref, f32[4,64,2048]{2,1,0:T(8,128)} %get-tuple-element.59.grad_ref, ...), custom_call_target="tpu_custom_call" | custom-call | bytes 209715200 | tf_op jit(solution)/shard_map/exchange_4/pallas_call | solution.py:508
  489.1 6.1 convolution_convert_fusion.2.proj_ref
  495.2 3.4 convolution_convert_fusion.3.grad_ref
  498.6 37.3 %attend_back.1 = (bf16[1024,512]{1,0:T(8,128)(2,1)S(1)}, f32[1024,512]{1,0:T(8,128)}, f32[1024,512]{1,0:T(8,128)}, bf16[1024,512]{1,0:T(8,128)(2,1)}, bf16[1024,...) custom-call(bf16[1024,1536]{1,0:T(8,128)(2,1)} %copy-done.4, bf16[1024,1536]{1,0:T(8,128)(2,1)} %copy-done.4, ...), custom_call_target="tpu_custom_call" | custom-call | flops 21474836480 | bytes 15728640 | tf_op jit(solution)/shard_map/attend_back/pallas_call | solution.py:971
  535.9 3.8 collective-permute-start.1
  539.7 2.6 collective-permute-done.1.key_in_ref
  545.4 16.0 %last_gradients.1 = (bf16[1024,1536]{1,0:T(8,128)(2,1)}, f32[1,1536]{1,0:T(1,128)S(1)}, bf16[2048,2048]{1,0:T(8,128)(2,1)}) custom-call(bf16[2048,1024]{1,0:T(8,128)(2,1)} %bitcast.98, bf16[1024,512]{1,0:T(8,128)(2,1)S(1)} %get-tuple-element.72.query_ref, f32[1024,512]{1,0:T(8,128)S(1)} %copy-done, f32[1024,512]{1,0:T(8,128)} %get-tuple-element.74.value_ref, ...), custom_call_target="tpu_custom_call" | custom-call | flops 6442450944 | bytes 33554432 | tf_op jit(solution)/shard_map/last_gradients/pallas_call | solution.py:1082
  564.2 2.8 convert_element_type.59
  567.9 80.8 %exchange_6.1 = (bf16[4,4,64,2048]{3,2,1,0:T(8,128)(2,1)}, f32[8,16,128]{2,1,0:T(8,128)}) custom-call(bf16[2,4,2,64,1536]{4,3,2,1,0:T(8,128)(2,1)} %bitcast.100, bf16[2048,2048]{1,0:T(8,128)(2,1)} %all-gather.4.cloned.1.call-done.weight_ref, f32[4,64,2048]{2,1,0:T(8,128)} %get-tuple-element.78.grad_ref, f32[8,16,128]{2,1,0:T(8,128)} %bitcast.103), custom_call_target="tpu_custom_call" | custom-call | bytes 209715200 | tf_op jit(solution)/shard_map/exchange_6/pallas_call | solution.py:508
  649.6 6.7 convert.2
  657.4 15.9 %reduce-scatter.8.cloned.1.call-done = bf16[256,2048]{1,0:T(8,128)(2,1)} async-done(((bf16[2048,2048]{1,0:T(8,128)(2,1)}), bf16[256,2048]{1,0:T(8,128)(2,1)}) %reduce-scatter.8.cloned.1.call-update) | async-done | bytes 1048592 | tf_op jit(solution)/shard_map/reduce_scatter | solution.py:1276
  675.8 2.3 fusion.20
  678.1 4.8 copy.71
  (92 shorter events, 32.6 us)
Async XLA Ops:
  7.2 112.4 %all-gather.4.cloned.1.call-start = ((), (), s32[]{:S(2)}) async-start(), calls=%async_computation.3 | async-start | bytes 9437184 | tf_op jit(solution)/shard_map/all_gather | solution.py:1147
  12.0 1.0 copy-start.3
  13.0 234.7 %all-gather.6.cloned.1.call-start = ((), (), s32[]{:S(2)}) async-start(), calls=%async_computation.4 | async-start | bytes 9437184 | tf_op jit(solution)/shard_map/all_gather | solution.py:1148
  13.8 267.8 %all-gather.8.cloned.1.call-start = ((), (), s32[]{:S(2)}) async-start(), calls=%async_computation.5 | async-start | bytes 9437184 | tf_op jit(solution)/shard_map/all_gather | solution.py:1149
  14.5 474.6 %reduce-scatter.4.cloned.1.call-start = ((), (), s32[]{:S(2)}) async-start(), calls=%async_computation.6 | async-start | bytes 9437184 | tf_op jit(solution)/shard_map/reduce_scatter | solution.py:1229
  129.7 1.6 copy-start.4
  132.9 9.9 %slice-start = ((bf16[2048,2048]{1,0:T(8,128)(2,1)}), bf16[2048,512]{1,0:T(8,128)(2,1)S(1)}, s32[]{:S(2)}) async-start(bf16[2048,2048]{1,0:T(8,128)(2,1)} %all-gather.4.cloned.1.call-done.weight_ref), calls=%async_computation.9 | async-start | bytes 4194304 | tf_op jit(solution)/shard_map/slice | solution.py:1151
  132.9 15.3 %collective-permute-start = (bf16[1024,1024]{1,0:T(8,128)(2,1)}, bf16[1024,1024]{1,0:T(8,128)(2,1)}, u32[]{:S(2)}, u32[]{:S(2)}) collective-permute-start(bf16[1024,1024]{1,0:T(8,128)(2,1)} %slice.175), channel_id=1, source_target_pairs={{0,4},{4,0},{8,12},{12,8},{16,20},{20,16},{24,28},{28,24},{1,5},{5... | collective-permute-start | bytes 6291464 | tf_op jit(solution)/shard_map/ppermute | solution.py:1034
  140.3 7.9 %copy-start.7 = (f32[1,1,8,256]{3,1,2,0:T(1,128)}, f32[1,1,8,256]{3,1,2,0:T(1,128)S(1)}, u32[]{:S(2)}) copy-start(f32[1,1,8,256]{3,1,2,0:T(1,128)S(1)} %copy.55) | copy-start | bytes 24580
  264.1 3.4 copy-start.1
  371.9 192.3 %reduce-scatter.6.cloned.1.call-start = ((), (), s32[]{:S(2)}) async-start(), calls=%async_computation.7 | async-start | bytes 9437184 | tf_op jit(solution)/shard_map/reduce_scatter | solution.py:1234
  371.9 18.8 %copy-start.8 = (bf16[2,4,2,64,2048]{4,3,2,1,0:T(8,128)(2,1)S(1)}, bf16[2,4,2,64,2048]{4,3,2,1,0:T(8,128)(2,1)}, u32[]{:S(2)}) copy-start(bf16[2,4,2,64,2048]{4,3,2,1,0:T(8,128)(2,1)} %get-tuple-element.54) | copy-start | bytes 12582916
  388.7 2.0 copy-start.2
  402.1 271.2 %reduce-scatter.8.cloned.1.call-start = ((), (), s32[]{:S(2)}) async-start(), calls=%async_computation.8 | async-start | bytes 9437184 | tf_op jit(solution)/shard_map/reduce_scatter | solution.py:1276
  489.1 6.1 copy-start.9
  535.9 6.4 collective-permute-start.1
  539.6 4.2 collective-permute-start.2
  543.8 1.6 copy-start
  561.4 1.0 copy-start.6
  561.4 1.3 copy-start.5
Sparse Core Ops, SparseCore 0:
  13.1 101.1 all-gather.3
  115.9 83.2 all-gather.5
  200.8 80.6 all-gather.7
  372.0 89.1 reduce-scatter.3
  463.9 87.6 reduce-scatter.5
  561.6 111.7 reduce-scatter.7

commit v4 on v3

--- a/solution.py
+++ b/solution.py
@@ -1,4 +1,5 @@
 import functools
+import math
 
 import jax
 import jax.numpy as jnp
@@ -45,7 +46,7 @@
     pl.semaphore_wait(barrier, len(devices))
 
 
-def sender(send_sem, recv_sem):
+def sender(send_sem, recv_sem, start=True):
     def send(source, target, slot, device):
         copy = pltpu.make_async_remote_copy(
             src_ref=source,
@@ -55,7 +56,8 @@
             device_id=device,
             device_id_type=MESH,
         )
-        copy.start()
+        if start:
+            copy.start()
         return copy
 
     return send
@@ -148,6 +150,19 @@
 def norm_back(grad, normal, inverse, gain):
     inner = grad * gain
     return inverse * (inner - mean_of(inner) - normal * mean_of(inner * normal))
+
+
+def turner(rows_of, turned_ref):
+    width, rows = turned_ref.shape
+    step = 256
+
+    def fill(part):
+        @pl.loop(0, width // (2 * step))
+        def _(index):
+            span = pl.ds(pl.multiple_of(part * (width // 2) + index * step, step), step)
+            turned_ref[span] = rows_of(span).reshape(rows, step).T
+
+    return fill
 
 
 class Product:
@@ -195,7 +210,7 @@
             pl.loop(0, self.count)(columns)
 
 
-def run_pieces(exchange, order, work, product=None):
+def run_pieces(exchange, order, work, product=None, fill=None):
     groups = len(order)
     places = list(enumerate(order))
     half = groups // 2
@@ -215,12 +230,16 @@
     for index, piece in first:
         exchange.start(index, piece)
     make(first, False)
+    if fill is not None:
+        fill(0)
     for index, piece in first:
         exchange.pass_on(index, piece)
     make(second, True)
     for index, piece in second:
         exchange.start(index, piece)
     make(second, False)
+    if fill is not None:
+        fill(1)
     for index, piece in first:
         work(index, piece, exchange.total(index, piece))
     for index, piece in second:
@@ -229,7 +248,7 @@
 
 
 def first_norm_kernel(
-    groups, part_ref, x_ref, rows_ref, low_ref, normal_ref, inverse_ref,
+    groups, part_ref, x_ref, all_ref, rows_ref, low_ref, normal_ref, inverse_ref, turned_ref,
     landed, relay, ready, send_sem, recv_sem, local_sem,
 ):
     exchange = Exchange(part_ref, landed, relay, send_sem, recv_sem)
@@ -252,7 +271,9 @@
         copy.start()
         local.append(copy)
 
-    first, second = run_pieces(exchange, range(groups), work)
+    first, second = run_pieces(
+        exchange, range(groups), work, None, turner(lambda span: all_ref[:, span], turned_ref)
+    )
     for index, piece in first:
         exchange.forward(index, target(piece))
     for index, piece in second:
@@ -264,14 +285,47 @@
         copy.wait()
 
 
+def half_sum_kernel(
+    groups, left_ref, weight_ref, total_ref, turned_ref,
+    landed, relay, part_ref, weight, rows, load_sem, send_sem, recv_sem,
+):
+    exchange = Exchange(part_ref, landed, relay, send_sem, recv_sem)
+    product = Product(exchange, False, left_ref, weight_ref, weight, rows, load_sem)
+    greet([{"mp": exchange.along_x}, {"mp": exchange.along_y}])
+
+    def work(index, piece, total):
+        total_ref[piece] = total
+
+    fill = turner(lambda span: left_ref[:, :, :, :, span], turned_ref)
+    _, second = run_pieces(exchange, range(groups), work, product, fill)
+    for index, piece in second:
+        work(index, piece, exchange.total(index, piece))
+    exchange.sent()
+
+
 def second_norm_kernel(
-    groups, per, left_ref, weight_ref, turned_ref, normal_ref, cotan_ref, rows_ref,
-    low_ref, grad_ref, back_ref, sums_ref, weight_grad_ref,
-    landed, relay, ready, layer, cotan_in, part_ref, weight, rows, load_sem, put_sem,
+    groups, per, left_ref, weights_ref, weight_ref, turned_ref, done_ref,
+    normal_ref, cotan_ref, rows_ref,
+    low_ref, grad_ref, back_ref, sums_ref, weight_grad_ref, whole_ref,
+    landed, relay, part_ref, weight, rows, load_sem,
+    ready, layer, cotan_in, done_weight, whole, put_sem, whole_sem,
     send_sem, recv_sem, local_sem,
 ):
     exchange = Exchange(part_ref, landed, relay, send_sem, recv_sem)
     product = Product(exchange, False, left_ref, weight_ref, weight, rows, load_sem)
+    members = groups * per
+    narrow = weight.shape[1] // members
+    load_done = pltpu.make_async_copy(weights_ref, done_weight, whole_sem.at[0])
+    load_done.start()
+
+    def join(part):
+        if part == 0:
+            load_done.wait()
+        for place in range(part * members // 2, (part + 1) * members // 2):
+            for index, source in enumerate((done_weight, weight)):
+                target = pl.ds((2 * place + index) * narrow, narrow)
+                whole[:, target] = source[:, place * narrow : (place + 1) * narrow]
+
     peers = planes(groups, per)
     greet([{"mp": exchange.along_x}, {"mp": exchange.along_y}] + peers[1:])
     base = 6 * groups
@@ -293,6 +347,15 @@
     def work(index, piece, total):
         gain_one, shift_one, bias = rows_ref[0:1], rows_ref[1:2], rows_ref[2:3]
         gain, shift = rows_ref[3:4], rows_ref[4:5]
+        done = done_ref[piece]
+        total = jnp.concatenate(
+            [
+                half[:, place * narrow : (place + 1) * narrow]
+                for place in range(members)
+                for half in (done, total)
+            ],
+            axis=1,
+        )
         values = normal_ref[piece] * gain_one + shift_one + total + bias
         normal, inverse = normed(values)
         layer[index] = (normal * gain + shift).astype(BF)
@@ -316,7 +379,9 @@
         sums_ref[1:2] += jnp.sum(cotan * normal, axis=0, keepdims=True)
         sums_ref[2:3] += jnp.sum(cotan, axis=0, keepdims=True)
 
-    first, second = run_pieces(exchange, range(groups), work, product)
+    first, second = run_pieces(exchange, range(groups), work, product, join)
+    put_whole = pltpu.make_async_copy(whole, whole_ref, whole_sem.at[1])
+    put_whole.start()
     for index, piece in first:
         exchange.forward(index, target(piece))
     for index, piece in second:
@@ -324,7 +389,7 @@
     for index, piece in second:
         exchange.forward(index, target(piece))
     step = 256
-    count = weight.shape[1] // step
+    count = whole.shape[1] // step
     depth = turned_ref.shape[1] // 2
 
     def columns(index):
@@ -333,7 +398,7 @@
     def put(index):
         span = columns(index)
         return pltpu.make_async_copy(
-            weight.at[:, span], weight_grad_ref.at[:, span], put_sem.at[index]
+            whole.at[:, span], weight_grad_ref.at[:, span], put_sem.at[index]
         )
 
     def product_of(part, span):
@@ -341,13 +406,14 @@
         return matmul(turned_ref[:, part * depth : (part + 1) * depth], low)
 
     exchange.arrived([index for index, _ in first])
+    put_whole.wait()
     for copy in local[: len(first) + 1]:
         copy.wait()
 
     @pl.loop(0, count)
     def _(index):
         span = columns(index)
-        weight[:, span] = product_of(0, span).astype(BF)
+        whole[:, span] = product_of(0, span).astype(BF)
 
     exchange.arrived([index for index, _ in second])
     for copy in local[len(first) + 1 :]:
@@ -356,7 +422,7 @@
     @pl.loop(0, count)
     def _(index):
         span = columns(index)
-        weight[:, span] = (product_of(1, span) + weight[:, span].astype(F32)).astype(BF)
+        whole[:, span] = (product_of(1, span) + whole[:, span].astype(F32)).astype(BF)
         put(index).start()
 
     exchange.sent()
@@ -502,9 +568,8 @@
     ]
 
 
-def exchange_call(
-    kernel, ident, operands, results, groups, piece, width, scratch, extra, outside=()
-):
+def exchange_call(kernel, ident, operands, results, sums, scratch, extra, outside=(), local=True):
+    groups, piece, width = sums
     return pl.pallas_call(
         kernel,
         out_shape=tuple(jax.ShapeDtypeStruct(shape, dtype) for shape, dtype, _ in results),
@@ -513,14 +578,13 @@
         scratch_shapes=[
             pltpu.VMEM((groups, 3, piece, width), BF),
             pltpu.VMEM((groups, piece, width), BF),
-            pltpu.VMEM((groups, piece, width), BF),
         ]
         + scratch
         + [
             pltpu.SemaphoreType.DMA((6 * groups + extra,)),
             pltpu.SemaphoreType.DMA((6 * groups + extra,)),
-            pltpu.SemaphoreType.DMA((groups + 1,)),
-        ],
+        ]
+        + ([pltpu.SemaphoreType.DMA((groups + 1,))] if local else []),
         compiler_params=pltpu.CompilerParams(
             collective_id=ident, has_side_effects=True, vmem_limit_bytes=58 * MIB
         ),
@@ -529,7 +593,7 @@
     )(*operands)
 
 
-def first_norm(part, x_part, rows, parts, ident):
+def first_norm(part, x_part, x_rows, rows, parts, ident):
     groups, piece, width = x_part.shape
     half = groups // 2
     if parts != 4:
@@ -537,25 +601,45 @@
         values = x_part.astype(F32) + total.reshape(x_part.shape) + rows[0]
         normal, inverse = normed(values)
         low = lax.all_gather((normal * rows[1] + rows[2]).astype(BF), "mp", axis=0)
-        return low, normal, inverse
+        return low, normal, inverse, x_rows.T
     return exchange_call(
         functools.partial(first_norm_kernel, groups),
         ident,
-        (part.reshape(2, parts, half, piece, width), x_part, rows),
+        (part.reshape(2, parts, half, piece, width), x_part, x_rows, rows),
         [
             ((2, parts, half, piece, width), BF, ANY),
             ((groups, piece, width), F32, VMEM),
             ((groups, piece, 1), F32, VMEM),
+            ((width, x_rows.shape[0]), BF, VMEM),
         ],
-        groups, piece, width, [], 0,
-    )
-
-
-def second_norm(left, weight, turned, normal, cotan, rows, members, parts, ident):
+        (groups, piece, width),
+        [pltpu.VMEM((groups, piece, width), BF)],
+        0,
+    )
+
+
+def half_sum(left, weight, groups, piece, parts, ident):
+    rows, depth = left.shape
+    width = weight.shape[1]
+    return exchange_call(
+        functools.partial(half_sum_kernel, groups),
+        ident,
+        (left.reshape(2, parts, groups // 2, piece, depth), weight),
+        [((groups, piece, width), F32, VMEM), ((depth, rows), BF, VMEM)],
+        (groups, piece, width),
+        product_scratch(parts, groups, piece, width, depth, False),
+        0,
+        (1,),
+        False,
+    )
+
+
+def second_norm(left, shard, normal, cotan, rows, members, parts, ident):
     groups, piece, width = normal.shape
     depth = left.shape[-1]
     half = groups // 2
     if parts != 4:
+        weight = lax.all_gather(shard, "seq", axis=1, tiled=True)
         part = matmul(left, weight).astype(BF)
         total = lax.psum_scatter(part, "mp", scatter_dimension=0, tiled=True).astype(F32)
         values = normal * rows[0] + rows[1] + total.reshape(normal.shape) + rows[2]
@@ -567,24 +651,42 @@
         sums = [jnp.sum(array, axis=(0, 1)) for array in (grad, cotan * normal, cotan)]
         sums = jnp.stack(sums + [jnp.zeros_like(sums[0])] * 5)
         low = lax.all_gather(grad.astype(BF), "mp", axis=0)
-        return low, grad, back, sums, matmul(turned, low.reshape(-1, width)).astype(BF)
+        return low, grad, back, sums, over_rows(left, low.reshape(-1, width)).astype(BF), weight
+    narrow = shard.shape[1] // 2
+    weights = [
+        lax.all_gather(block, "seq", axis=1, tiled=True)
+        for block in (shard[:, :narrow], shard[:, narrow:])
+    ]
+    done, turned = half_sum(left, weights[0], groups, piece, parts, ident + 10)
+    block = pltpu.VMEM((groups, piece, width), BF)
     return exchange_call(
         functools.partial(second_norm_kernel, groups, members // groups),
         ident,
-        (left.reshape(2, parts, half, piece, depth), weight, turned, normal, cotan, rows),
+        (
+            left.reshape(2, parts, half, piece, depth),
+            weights[0], weights[1], turned, done, normal, cotan, rows,
+        ),
         [
             ((2, parts, half, piece, width), BF, VMEM),
             ((groups, piece, width), F32, VMEM),
             ((groups, piece, width), BF, ANY),
             ((8, width), F32, VMEM),
             ((depth, width), BF, ANY),
+            ((depth, width), BF, ANY),
         ],
-        groups, piece, width,
-        [pltpu.VMEM((groups, piece, width), BF), pltpu.VMEM((groups, piece, width), BF)]
-        + product_scratch(parts, groups, piece, width, depth, False)
-        + [pltpu.SemaphoreType.DMA((width // 256,))],
+        (groups, piece, width // 2),
+        product_scratch(parts, groups, piece, width // 2, depth, False)
+        + [
+            block,
+            block,
+            block,
+            pltpu.VMEM((depth, width // 2), BF),
+            pltpu.VMEM((depth, width), BF),
+            pltpu.SemaphoreType.DMA((width // 256,)),
+            pltpu.SemaphoreType.DMA((2,)),
+        ],
         2 * groups,
-        (1,),
+        (1, 2),
     )
 
 
@@ -616,8 +718,8 @@
             ((groups, piece, width), F32, VMEM),
             ((parts, 8, width), F32, VMEM),
         ],
-        groups, piece, width,
-        [pltpu.VMEM((8, width), F32)]
+        (groups, piece, width),
+        [pltpu.VMEM((groups, piece, width), BF), pltpu.VMEM((8, width), F32)]
         + product_scratch(parts, groups, piece, width, depth, True),
         3,
         (1,),
@@ -639,8 +741,8 @@
         ident,
         (left.reshape(2, parts, groups // 2, piece, depth), weight, grad, small),
         [((groups, parts, piece, width), BF, ANY), (small.shape, F32, VMEM)],
-        groups, piece, width,
-        [pltpu.VMEM((groups, piece, width), BF)]
+        (groups, piece, width),
+        [pltpu.VMEM((groups, piece, width), BF)] * 2
         + product_scratch(parts, groups, piece, width, depth, True),
         groups + members,
         (1,),
@@ -834,33 +936,112 @@
     )(qkv, qkv, qkv, kv_far, kv_far)
 
 
-def layer_copies(back_ref, all_ref, send_sem, recv_sem, groups, per):
+def share_meanwhile(now, count, pieces, back_ref, all_ref, send_sem, recv_sem, local_sem):
     me, along_x, along_y, _ = square()
-    group = lax.axis_index("seq") // per
-    copies = []
-    for piece in range(groups):
-        near, far = (along_x, along_y) if piece % 2 == 0 else (along_y, along_x)
-        sequence = lax.rem(group + piece, groups)
-        block, own, passed = back_ref.at[piece], all_ref.at[sequence, me], all_ref.at[sequence, near]
-        for kind, (source, target, device) in enumerate(
-            ((block, own, near), (block, own, far), (passed, passed, far))
-        ):
-            copies.append(
-                pltpu.make_async_remote_copy(
-                    src_ref=source,
-                    dst_ref=target,
-                    send_sem=send_sem.at[3 * piece + kind],
-                    recv_sem=recv_sem.at[3 * piece + kind],
-                    device_id={"mp": device},
-                    device_id_type=MESH,
-                )
-            )
-    return copies[0::3], copies[1::3], copies[2::3]
+    send = sender(send_sem, recv_sem, False)
+    near, far, passed, local = [], [], [], []
+    for index, piece in enumerate(pieces):
+        ways = (along_x, along_y) if index % 2 == 0 else (along_y, along_x)
+        block, own = back_ref.at[piece], all_ref.at[index, me]
+        relayed = all_ref.at[index, ways[0]]
+        near.append(send(block, own, 3 * index, {"mp": ways[0]}))
+        far.append(send(block, own, 3 * index + 1, {"mp": ways[1]}))
+        passed.append(send(relayed, relayed, 3 * index + 2, {"mp": ways[1]}))
+        local.append(pltpu.make_async_copy(block, own, local_sem.at[index]))
+
+    @pl.when(now == 0)
+    def _():
+        greet([{"mp": along_x}, {"mp": along_y}])
+        for copy in near + far + local:
+            copy.start()
+
+    @pl.when(now == count // 4)
+    def _():
+        for first, second in zip(near, passed):
+            first.wait_recv()
+            second.start()
+
+    def finish():
+        @pl.when(now == count - 1)
+        def _():
+            for copy in far + passed:
+                copy.wait_recv()
+            for copy in near + far + passed:
+                copy.wait_send()
+            for copy in local:
+                copy.wait()
+
+    return finish
+
+
+def meanwhile_scratch(pieces):
+    return [
+        pltpu.SemaphoreType.DMA((3 * len(pieces),)),
+        pltpu.SemaphoreType.DMA((3 * len(pieces),)),
+        pltpu.SemaphoreType.DMA((len(pieces),)),
+    ]
+
+
+def feed_back_kernel(
+    pieces, low_ref, weight_ref, pre_ref, turned_ref, back_ref,
+    grad_ref, sums_ref, weight_grad_ref, all_ref, send_sem, recv_sem, local_sem,
+):
+    now, count = pl.program_id(0), pl.num_programs(0)
+    finish = share_meanwhile(now, count, pieces, back_ref, all_ref, send_sem, recv_sem, local_sem)
+    value = pre_ref[...]
+    root = (2 / math.pi) ** 0.5
+    square_of = value * value
+    bent = jnp.tanh(root * value * (1 + 0.044715 * square_of))
+    slope = 0.5 * (1 + bent) + (0.5 * root) * value * (1 - bent * bent) * (
+        1 + 3 * 0.044715 * square_of
+    )
+    grad = (over_cols(low_ref[...], weight_ref[...]) * slope).astype(BF)
+    grad_ref[...] = grad
+    sums_ref[...] = jnp.sum(grad.astype(F32), axis=0, keepdims=True)
+    weight_grad_ref[...] = matmul(turned_ref[...], grad).astype(BF)
+    finish()
+
+
+def feed_back(low, weight, inner_pre, turned, layer_back, pieces, parts, ident):
+    rows, hidden = inner_pre.shape
+    width = low.shape[1]
+    step = 512
+    _, piece, _ = layer_back.shape
+    return pl.pallas_call(
+        functools.partial(feed_back_kernel, pieces),
+        grid=(hidden // step,),
+        out_shape=(
+            jax.ShapeDtypeStruct((rows, hidden), BF),
+            jax.ShapeDtypeStruct((1, hidden), F32),
+            jax.ShapeDtypeStruct((width, hidden), BF),
+            jax.ShapeDtypeStruct((len(pieces), parts, piece, width), BF),
+        ),
+        in_specs=[
+            pl.BlockSpec((rows, width), lambda i: (0, 0)),
+            pl.BlockSpec((step, width), lambda i: (i, 0)),
+            pl.BlockSpec((rows, step), lambda i: (0, i)),
+            pl.BlockSpec((width, rows), lambda i: (0, 0)),
+            ANY,
+        ],
+        out_specs=(
+            pl.BlockSpec((rows, step), lambda i: (0, i)),
+            pl.BlockSpec((1, step), lambda i: (0, i)),
+            pl.BlockSpec((width, step), lambda i: (0, i)),
+            ANY,
+        ),
+        scratch_shapes=meanwhile_scratch(pieces),
+        compiler_params=pltpu.CompilerParams(
+            collective_id=ident, has_side_effects=True, vmem_limit_bytes=58 * MIB
+        ),
+        cost_estimate=pl.CostEstimate(
+            flops=4 * rows * width * hidden, bytes_accessed=40 * MIB, transcendentals=rows * hidden
+        ),
+        name="feed_back",
+    )(low, weight, inner_pre, turned, layer_back)
 
 
 def attend_back_kernel(
-    groups,
-    per,
+    pieces,
     step,
     query_ref,
     key_ref,
@@ -872,7 +1053,7 @@
     log_ref,
     *rest,
 ):
-    sharing = groups > 0
+    sharing = len(pieces) > 0
     if sharing:
         back_ref, *rest = rest
     dquery_ref, dkey_ref, dvalue_ref, dkey_far_ref, dvalue_far_ref, *rest = rest
@@ -885,29 +1066,9 @@
         send_sem, recv_sem, local_sem = rest
         now = pl.program_id(0) * pl.num_programs(1) + block
         count = pl.num_programs(0) * pl.num_programs(1)
-        near, far, passed = layer_copies(back_ref, all_ref, send_sem, recv_sem, groups, per)
-        me, along_x, along_y, _ = square()
-        group = lax.axis_index("seq") // per
-        local = [
-            pltpu.make_async_copy(
-                back_ref.at[piece],
-                all_ref.at[lax.rem(group + piece, groups), me],
-                local_sem.at[piece],
-            )
-            for piece in range(groups)
-        ]
-
-        @pl.when(now == 0)
-        def _():
-            greet([{"mp": along_x}, {"mp": along_y}])
-            for copy in near + far + local:
-                copy.start()
-
-        @pl.when(now == count * 3 // 8)
-        def _():
-            for first, second in zip(near, passed):
-                first.wait_recv()
-                second.start()
+        finish = share_meanwhile(
+            now, count, pieces, back_ref, all_ref, send_sem, recv_sem, local_sem
+        )
 
     @pl.when(block == 0)
     def _():
@@ -944,23 +1105,15 @@
         dvalue_far_ref[...] = value_sum[rows:].astype(BF)
 
     if sharing:
-
-        @pl.when(now == count - 1)
-        def _():
-            for copy in far + passed:
-                copy.wait_recv()
-            for copy in near + far + passed:
-                copy.wait_send()
-            for copy in local:
-                copy.wait()
-
-
-def attend_back(qkv, kv_far, grad, mix, logs, heads, layer_back, per, parts, ident):
+        finish()
+
+
+def attend_back(qkv, kv_far, grad, mix, logs, heads, layer_back, pieces, parts, ident):
     rows, cols = qkv.shape[0], heads * DH
     away = kv_far.shape[0]
     block, step = min(512, rows), min(512, rows)
-    sharing = parts == 4
-    groups, piece, width = layer_back.shape
+    sharing = len(pieces) > 0
+    _, piece, width = layer_back.shape
 
     def tile(offset):
         return pl.BlockSpec((block, DH), lambda h, i: (i, offset + h))
@@ -968,8 +1121,8 @@
     def long(count, offset):
         return pl.BlockSpec((count, DH), lambda h, i: (0, offset + h))
 
-    results = pl.pallas_call(
-        functools.partial(attend_back_kernel, groups if sharing else 0, per, step),
+    return pl.pallas_call(
+        functools.partial(attend_back_kernel, pieces, step),
         grid=(heads, rows // block),
         out_shape=(
             jax.ShapeDtypeStruct((rows, cols), BF),
@@ -978,7 +1131,7 @@
             jax.ShapeDtypeStruct((away, cols), BF),
             jax.ShapeDtypeStruct((away, cols), BF),
         )
-        + ((jax.ShapeDtypeStruct((groups, parts, piece, width), BF),) if sharing else ()),
+        + ((jax.ShapeDtypeStruct((len(pieces), parts, piece, width), BF),) if sharing else ()),
         in_specs=[
             tile(0),
             long(rows, heads),
@@ -997,15 +1150,7 @@
             pltpu.VMEM((rows + away, DH), F32),
             pltpu.VMEM((rows + away, DH), F32),
         ]
-        + (
-            [
-                pltpu.SemaphoreType.DMA((3 * groups,)),
-                pltpu.SemaphoreType.DMA((3 * groups,)),
-                pltpu.SemaphoreType.DMA((groups,)),
-            ]
-            if sharing
-            else []
-        ),
+        + (meanwhile_scratch(pieces) if sharing else []),
         compiler_params=pltpu.CompilerParams(
             vmem_limit_bytes=52 * MIB,
             **(dict(collective_id=ident, has_side_effects=True) if sharing else {}),
@@ -1017,10 +1162,6 @@
         ),
         name="attend_back",
     )(qkv, qkv, qkv, kv_far, kv_far, grad, mix, logs, *([layer_back] if sharing else []))
-    if sharing:
-        return results
-    layer = jnp.roll(layer_back, lax.axis_index("seq") // per, axis=0)
-    return (*results, lax.all_gather(layer, "mp", axis=1))
 
 
 def from_group_members(block, members, per):
@@ -1047,14 +1188,32 @@
 
 
 def last_kernel(
-    turned_ref, query_ref, key_ref, value_ref, key_in_ref, value_in_ref, proj_ref,
-    grad_ref, sums_ref, part_ref, made, copy_sem,
+    per, turned_hbm, query_ref, key_ref, value_ref, key_in_ref, value_in_ref, proj_hbm, layer_hbm, layer_more_hbm,
+    grad_ref, sums_ref, part_ref, layer_ref, turned_ref, made, proj, layer, load_sem, put_sem,
 ):
     rows, cols = query_ref.shape
-    copies = [
-        pltpu.make_async_copy(proj_ref, part_ref.at[:, pl.ds(3 * cols, cols)], copy_sem.at[3])
-    ]
-    copies[0].start()
+    count = load_sem.shape[0] - 3
+    step = turned_ref.shape[0] // count
+    loads = []
+    for place in range(count):
+        block = pl.ds(place * step, step)
+        loads.append(
+            pltpu.make_async_copy(turned_hbm.at[block], turned_ref.at[block], load_sem.at[place])
+        )
+    loads.append(pltpu.make_async_copy(proj_hbm, proj, load_sem.at[count]))
+    groups = layer.shape[0]
+    for place, source in enumerate((layer_hbm, layer_more_hbm)):
+        block = pl.ds(place * (groups // 2), groups // 2)
+        loads.append(pltpu.make_async_copy(source, layer.at[block], load_sem.at[count + 1 + place]))
+    for copy in loads:
+        copy.start()
+    puts = []
+
+    def put(source, target):
+        copy = pltpu.make_async_copy(source, target, put_sem.at[len(puts)])
+        copy.start()
+        puts.append(copy)
+
     for index, (own, far) in enumerate(
         ((query_ref, None), (key_ref, key_in_ref), (value_ref, value_in_ref))
     ):
@@ -1062,39 +1221,51 @@
         grad = own[...] if far is None else (own[...] + far[...].astype(F32)).astype(BF)
         grad_ref[:, span] = grad
         sums_ref[:, span] = jnp.sum(grad.astype(F32), axis=0, keepdims=True)
-        step = 512
-
-        @pl.loop(0, turned_ref.shape[0] // step)
-        def _(place, index=index, span=span):
-            block = pl.ds(pl.multiple_of(place * step, step), step)
+        for place in range(count):
+            block = pl.ds(place * step, step)
+            if index == 0:
+                loads[place].wait()
             made[index, block] = matmul(turned_ref[block], grad_ref[:, span]).astype(BF)
-
-        copy = pltpu.make_async_copy(made.at[index], part_ref.at[:, span], copy_sem.at[index])
-        copy.start()
-        copies.append(copy)
-    for copy in copies:
+        put(made.at[index], part_ref.at[:, span])
+        if index == 1:
+            loads[count].wait()
+            put(proj, part_ref.at[:, pl.ds(3 * cols, cols)])
+            for copy in loads[count + 1 :]:
+                copy.wait()
+            group = lax.axis_index("seq") // per
+            for piece in range(groups):
+                put(layer.at[piece], layer_ref.at[lax.rem(group + piece, groups)])
+    for copy in puts:
         copy.wait()
 
 
-def last_gradients(turned, query, key, value, key_in, value_in, proj_part):
+def last_gradients(turned, query, key, value, key_in, value_in, proj_part, layer, layer_more, per):
     rows, cols = query.shape
     width = turned.shape[0]
     return pl.pallas_call(
-        last_kernel,
+        functools.partial(last_kernel, per),
         out_shape=(
             jax.ShapeDtypeStruct((rows, 3 * cols), BF),
             jax.ShapeDtypeStruct((1, 3 * cols), F32),
             jax.ShapeDtypeStruct((width, 4 * cols), BF),
+            jax.ShapeDtypeStruct((2 * layer.shape[0],) + layer.shape[1:], layer.dtype),
         ),
-        in_specs=[VMEM] * 7,
-        out_specs=(VMEM, VMEM, ANY),
-        scratch_shapes=[pltpu.VMEM((3, width, cols), BF), pltpu.SemaphoreType.DMA((4,))],
-        compiler_params=pltpu.CompilerParams(vmem_limit_bytes=48 * MIB),
+        in_specs=[ANY] + [VMEM] * 5 + [ANY] * 3,
+        out_specs=(VMEM, VMEM, ANY, ANY),
+        scratch_shapes=[
+            pltpu.VMEM(turned.shape, BF),
+            pltpu.VMEM((3, width, cols), BF),
+            pltpu.VMEM(proj_part.shape, BF),
+            pltpu.VMEM((2 * layer.shape[0],) + layer.shape[1:], BF),
+            pltpu.SemaphoreType.DMA((7,)),
+            pltpu.SemaphoreType.DMA((4 + 2 * layer.shape[0],)),
+        ],
+        compiler_params=pltpu.CompilerParams(vmem_limit_bytes=52 * MIB),
         cost_estimate=pl.CostEstimate(
             flops=6 * rows * width * cols, bytes_accessed=32 * MIB, transcendentals=0
         ),
         name="last_gradients",
-    )(turned, query, key, value, key_in, value_in, proj_part)
+    )(turned, query, key, value, key_in, value_in, proj_part, layer, layer_more)
 
 
 def packed(vectors, lines):
@@ -1137,19 +1308,12 @@
     group = lax.axis_index("seq") // per
 
     depth, cols = query_weight.shape
-    narrow = width // members
     heads = cols // DH
-    proj_fold = proj_weight.reshape(-1, depth, narrow)
-    folds = proj_fold.shape[0]
-    first = jnp.concatenate(
-        [query_weight, key_weight, value_weight] + [proj_fold[i] for i in range(folds)], axis=1
-    )
+    first = jnp.concatenate([query_weight, key_weight, value_weight, proj_weight.T], axis=1)
     first = lax.all_gather(first, "seq", axis=0, tiled=True)
     w_inner = lax.all_gather(inner_weight, "seq", axis=0, tiled=True)
-    w_outer = lax.all_gather(outer_weight, "seq", axis=1, tiled=True)
     w_qkv = first[:, : 3 * cols]
-    w_proj = first[:, 3 * cols :].reshape(members, depth, folds, narrow)
-    w_proj = w_proj.transpose(2, 1, 0, 3).reshape(folds * depth, width)
+    w_proj = first[:, 3 * cols :]
     vectors = [
         query_bias,
         value_bias,
@@ -1183,7 +1347,7 @@
         1,
     )
     x_part = x_part.reshape(quarter, width)
-    x_rows = share_over_mp(x_part, parts, 7).reshape(rows, width)
+    x_rows = share_over_mp(x_part, parts, 8).reshape(rows, width)
     all_vectors = all_vectors.reshape(members, -1).astype(F32)
     full = []
     start = 0
@@ -1201,9 +1365,10 @@
     def blocked(array):
         return array.reshape(groups, piece, width)
 
-    first_low, normal_one, inverse_one = first_norm(
-        matmul(mixture_low, w_proj).astype(BF),
+    first_low, normal_one, inverse_one, x_turned = first_norm(
+        over_cols(mixture_low, w_proj).astype(BF),
         blocked(x_part),
+        x_rows,
         jnp.stack([b_proj, gain_one, shift_one]),
         parts,
         2,
@@ -1212,14 +1377,13 @@
 
     inner_pre = matmul(first_low, w_inner) + b_inner
     active = gelu_tanh(inner_pre).astype(BF)
-    active_turned, x_turned, active = lax.optimization_barrier((active.T, x_rows.T, active))
-    second_low, second_grad, layer_back, sums, outer_w_part = second_norm(
+    first_turned = first_low.T
+    second_low, second_grad, layer_back, sums, outer_w_part, w_outer = second_norm(
         active,
-        w_outer,
-        active_turned,
+        outer_weight,
         normal_one,
         jnp.stack(to_blocks(cotangent)),
-        jnp.stack([gain_one, shift_one, b_outer, gain_two, shift_two]),
+        after(jnp.stack([gain_one, shift_one, b_outer, gain_two, shift_two]), first_turned),
         members,
         parts,
         3,
@@ -1227,10 +1391,19 @@
     second_low = second_low.reshape(rows, width)
 
     outer_w_grad = lax.psum_scatter(outer_w_part, "seq", scatter_dimension=1, tiled=True)
-    _, pull_gelu = jax.vjp(gelu_tanh, inner_pre)
-    inner_grad = pull_gelu(over_cols(second_low, w_outer))[0].astype(BF)
-    inner_b_grad = jnp.sum(inner_grad.astype(F32), axis=0)
-    inner_w_part = over_rows(first_low, inner_grad).astype(BF)
+    fused = parts == 4 and per == 2
+    pieces = list(range(groups)) if fused else []
+    early, late = pieces[: groups // 2], pieces[groups // 2 :]
+    if fused:
+        inner_grad, inner_b_grad, inner_w_part, layer_out = feed_back(
+            second_low, w_outer, inner_pre, first_turned, layer_back, early, parts, 7
+        )
+    else:
+        _, pull_gelu = jax.vjp(gelu_tanh, inner_pre)
+        inner_grad = pull_gelu(over_cols(second_low, w_outer))[0].astype(BF)
+        inner_b_grad = jnp.sum(inner_grad.astype(F32), axis=0)
+        inner_w_part = matmul(first_turned, inner_grad).astype(BF)
+        layer_out = lax.all_gather(jnp.roll(layer_back, group, axis=0), "mp", axis=1)
     inner_w_grad = lax.psum_scatter(inner_w_part, "seq", scatter_dimension=0, tiled=True)
     attn_low, attn_grad, summed_rows = first_back(
         inner_grad,
@@ -1247,17 +1420,17 @@
     summed_rows = jnp.sum(summed_rows, axis=0)
 
     proj_w_part = over_rows(attn_low, mixture_low).astype(BF)
-    mixture_grad = over_cols(after(attn_low, proj_w_part), w_proj).astype(BF)
-    query_grad, key_grad, value_grad, key_away, value_away, layer_out = attend_back(
-        qkv, kv_far, mixture_grad, mixture, logs, heads, layer_back, per, parts, 5
+    mixture_grad = matmul(after(attn_low, proj_w_part), w_proj).astype(BF)
+    query_grad, key_grad, value_grad, key_away, value_away, *layer_more = attend_back(
+        qkv, kv_far, mixture_grad, mixture, logs, heads, layer_back, late, parts, 5
     )
 
     def blocks_of(array):
         return [array[i * rows : (i + 1) * rows] for i in range(per - 1)]
 
-    if parts == 4 and per == 2:
+    if fused:
         pairs = [(index, index + 1 - 2 * (index % 2)) for index in range(members)]
-        qkv_grad, bias_grad, last_w_part = last_gradients(
+        qkv_grad, bias_grad, last_w_part, layer_out = last_gradients(
             x_turned,
             query_grad,
             key_grad,
@@ -1265,6 +1438,9 @@
             lax.ppermute(key_away, "seq", pairs),
             lax.ppermute(value_away, "seq", pairs),
             proj_w_part,
+            layer_out,
+            layer_more[0],
+            per,
         )
         bias_grad = bias_grad[0]
     else:

time: 700 us -> 679 us (0.970)
  local copies, waits for them, and re-layouts: 62.2 us -> 19.3 us
  Pallas kernels: 494 us -> 522 us
  matrix products: 68.4 us -> 44.2 us
  waiting for transfers between devices: 24.7 us -> 40.4 us
    pallas_call x2 -> x3, Pallas kernels: 53.2 us -> 74.5 us  [the longest x1 29.9 us: feed_back(): pl.pallas_call(functools.partial(feed_back_kernel, pieces), grid=(hidden...]
    unnamed x38 -> x53, local copies, waits for them, and re-layouts: 21.7 us -> 4.98 us
    dot_general x2 -> x1, matrix products: 20.2 us -> 5.98 us  [over_cols(): lax.dot_general(left, right, (((1,), (1,)), ((), ())), preferred_element_...]
    dot_general x2 -> x1, matrix products: 17.5 us -> 6.05 us  [over_rows(): lax.dot_general(left, right, (((0,), (0,)), ((), ())), preferred_element_...]
    all_gather x1 -> x2, waiting for transfers between devices: 3.19 us -> 11.2 us  [second_norm(): lax.all_gather(block, 'seq', axis=1, tiled=True)]
    pallas_call x4 -> x5, Pallas kernels: 325 us -> 330 us  [exchange_call(): pl.pallas_call(kernel, out_shape=tuple((jax.ShapeDtypeStruct(shape, dtype...]
  transfers between devices with their start and end apart: 9 -> 10, of which waited for: 4 -> 5; matrix products, arithmetic and copies ran while one was open for 18% -> 11% of each run, Pallas kernels for 58% -> 67%
where the time goes in v4:
time: 679 us; the launch traced here: 670 us
  Pallas kernels  522 us (77%)
  matrix products  44.2 us (7%)
  waiting for transfers between devices  40.4 us (6%)
  local copies, waits for them, and re-layouts  19.3 us (3%)
  other arithmetic  19.1 us (3%)
  between operations  14.9 us (2%)
  starting transfers between devices  10.5 us (2%)
    pallas_call x5, Pallas kernels, exchange_call(): pl.pallas_call(kernel, out_shape=tuple((jax.ShapeDtypeStruct(shape, dtype...  330 us
    pallas_call x1, Pallas kernels, swap_groups(): pl.pallas_call(functools.partial(swap_kernel, groups, per, sign), out_sha...  59.1 us
    pallas_call x1, Pallas kernels, share_over_mp(): pl.pallas_call(share_kernel, out_shape=jax.ShapeDtypeStruct((2, parts, ow...  37 us
    dot_general x3, matrix products, matmul(): return jnp.dot(left, right, preferred_element_type=F32)  32.2 us
    pallas_call x1, Pallas kernels, feed_back(): pl.pallas_call(functools.partial(feed_back_kernel, pieces), grid=(hidden...  29.9 us
    pallas_call x1, Pallas kernels, attend_back(): pl.pallas_call(functools.partial(attend_back_kernel, pieces, step), grid=...  29.7 us
    reduce_scatter x1, waiting for transfers between devices, on_device(): lax.psum_scatter(last_w_part, 'seq', scatter_dimension=0, tiled=True)  21.2 us
    pallas_call x1, Pallas kernels, attend(): pl.pallas_call(attend_kernel, grid=(heads, rows // block), out_shape=(jax...  20.9 us
  transfers between devices with their start and end apart: 10, of which 5 were waited for; matrix products, arithmetic and copies ran while one was open for 11% of the time, Pallas kernels for 67%

profile of v4, /device:TPU:9, one launch (start us, length us, event | category | flops | bytes accessed | tf_op | source)
XLA Modules:
  0.0 670.4 jit_solution(18372982017108123519)
XLA Ops:
  7.3 1.2 copy.37
  8.5 2.2 pad_maximum_fusion.1
  13.5 1.7 constant_dynamic-slice_fusion.3
  16.9 59.1 %swap_groups_1.1 = (bf16[4,64,2048]{2,1,0:T(8,128)(2,1)}, bf16[8,16,128]{2,1,0:T(8,128)(2,1)}) custom-call(bf16[4,64,2048]{2,1,0:T(8,128)(2,1)} %pad_maximum_fusion.block_ref, bf16[8,16,128]{2,1,0:T(8,128)(2,1)} %broadcast_in_dim.12.small_ref), custom_call_target="tpu_custom_call" | custom-call | bytes 62914560 | tf_op jit(solution)/shard_map/swap_groups_1/pallas_call | solution.py:851
  77.0 37.0 %share_over_mp_8.1 = bf16[2,4,128,2048]{3,2,1,0:T(8,128)(2,1)} custom-call(bf16[256,2048]{1,0:T(8,128)(2,1)} %bitcast.84), custom_call_target="tpu_custom_call" | custom-call | bytes 104857600 | tf_op jit(solution)/shard_map/share_over_mp_8/pallas_call | solution.py:786
  114.1 10.0 %add_convert_fusion.query_ref.key_ref.value_ref = bf16[1024,1536]{1,0:T(8,128)(2,1)S(1)} fusion(bf16[1024,2048]{1,0:T(8,128)(2,1)} %bitcast.81, bf16[2048,2048]{1,0:T(8,128)(2,1)} %all-gather.5.cloned.1.call-done.weight_ref, f32[1536]{0:T(1024)S(1)} %pad_maximum_fusion.4), kind=kOutput, calls=%fused_computation.11 | convolution fusion | flops 6445596672 | bytes 13637632 | tf_op jit(solution)/shard_map/dot_general | solution.py:22
  124.4 1.3 collective-permute-start
  128.4 2.5 collective-permute-done.key_far_ref.value_far_ref
  131.0 20.9 %attend.1 = (f32[1024,512]{1,0:T(8,128)}, bf16[1024,512]{1,0:T(8,128)(2,1)S(1)}, f32[4,1,1024]{2,1,0:T(1,128)S(1)}) custom-call(bf16[1024,1536]{1,0:T(8,128)(2,1)} %copy-done.1, bf16[1024,1536]{1,0:T(8,128)(2,1)} %copy-done.1, bf16[1024,1536]{1,0:T(8,128)(2,1)} %copy-done.1, bf16[1024,1024]{1,0:T(8,128)(2,1)} %collective-permute-done.key_far_ref.value_far_ref, ...), custom_call_target="tpu_custom_call" | custom-call | flops 8589934592 | bytes 10485760 | tf_op jit(solution)/shard_map/attend/pallas_call | solution.py:912
  151.8 6.0 convolution_convert_fusion
  157.8 76.5 %exchange_2.1 = (bf16[2,4,2,64,2048]{4,3,2,1,0:T(8,128)(2,1)}, f32[4,64,2048]{2,1,0:T(8,128)}, f32[4,64,1]{2,1,0:T(8,128)}, bf16[2048,1024]{1,0:T(8,128)(2,1)}) custom-call(bf16[2,4,2,64,2048]{4,3,2,1,0:T(8,128)(2,1)} %bitcast.88, bf16[4,64,2048]{2,1,0:T(8,128)(2,1)} %get-tuple-element.58.x_ref, bf16[1024,2048]{1,0:T(8,128)(2,1)} %bitcast.82, ...), custom_call_target="tpu_custom_call" | custom-call | bytes 209715200 | tf_op jit(solution)/shard_map/exchange_2/pallas_call | solution.py:573
  234.3 6.4 copy.38
  240.7 17.3 %fusion.7 = (bf16[1024,2048]{1,0:T(8,128)(2,1)}, f32[1024,2048]{1,0:T(8,128)}) fusion(f32[2048]{0:T(1024)S(1)} %bitcast.107, bf16[1024,2048]{1,0:T(8,128)(2,1)} %bitcast.87, bf16[2048,2048]{1,0:T(8,128)(2,1)} %all-gather.7.cloned.1.call-done.weight_ref), kind=kOutput, calls=%fused_computation.8 | convolution fusion | flops 8610906112 | bytes 25174016 | tf_op jit(solution)/shard_map/dot_general | solution.py:22
  257.9 25.0 %exchange_13.1 = (f32[4,64,1024]{2,1,0:T(8,128)}, bf16[2048,1024]{1,0:T(8,128)(2,1)}) custom-call(bf16[2,4,2,64,2048]{4,3,2,1,0:T(8,128)(2,1)} %bitcast.79, bf16[2048,1024]{1,0:T(8,128)(2,1)} %all-gather.9.cloned.1.call-done.weight_ref.weights_ref), custom_call_target="tpu_custom_call" | custom-call | bytes 209715200 | tf_op jit(solution)/shard_map/exchange_13/pallas_call | solution.py:573
  282.9 11.2 %all-gather.11.cloned.1.call-done.weight_ref = bf16[2048,1024]{1,0:T(8,128)(2,1)} async-done(((bf16[2048,128]{1,0:T(8,128)(2,1)}), bf16[2048,1024]{1,0:T(8,128)(2,1)}) %all-gather.11.cloned.1.call-update) | async-done | bytes 4194320 | tf_op jit(solution)/shard_map/all_gather | solution.py:657
  294.1 70.6 %exchange_3.1 = (bf16[2,4,2,64,2048]{4,3,2,1,0:T(8,128)(2,1)}, f32[4,64,2048]{2,1,0:T(8,128)}, bf16[4,64,2048]{2,1,0:T(8,128)(2,1)}, f32[8,2048]{1,0:T(8,128)}, ...) custom-call(bf16[2,4,2,64,2048]{4,3,2,1,0:T(8,128)(2,1)} %bitcast.80, ...), custom_call_target="tpu_custom_call" | custom-call | bytes 209715200 | tf_op jit(solution)/shard_map/exchange_3/pallas_call | solution.py:573
  364.8 29.9 %feed_back.1 = (bf16[1024,2048]{1,0:T(8,128)(2,1)}, f32[1,2048]{1,0:T(1,128)}, bf16[2048,2048]{1,0:T(8,128)(2,1)}, bf16[2,4,64,2048]{3,2,1,0:T(8,128)(2,1)}) custom-call(bf16[1024,2048]{1,0:T(8,128)(2,1)} %bitcast.108, bf16[2048,2048]{1,0:T(8,128)(2,1)} %get-tuple-element.68.weight_ref, f32[1024,2048]{1,0:T(8,128)} %get-tuple-element.173.pre_ref, ...), custom_call_target="tpu_custom_call" | custom-call | flops 17179869184 | bytes 41943040 | tf_op jit(solution)/shard_map/feed_back/pallas_call | solution.py:1010
  394.8 77.3 %exchange_4.1 = (bf16[2,4,2,64,2048]{4,3,2,1,0:T(8,128)(2,1)}, f32[4,64,2048]{2,1,0:T(8,128)}, f32[4,8,2048]{2,1,0:T(8,128)}) custom-call(bf16[2,4,2,64,2048]{4,3,2,1,0:T(8,128)(2,1)} %bitcast.89, bf16[2048,2048]{1,0:T(8,128)(2,1)} %all-gather.7.cloned.1.call-done.weight_ref, f32[4,64,2048]{2,1,0:T(8,128)} %get-tuple-element.71.grad_ref, ...), custom_call_target="tpu_custom_call" | custom-call | bytes 209715200 | tf_op jit(solution)/shard_map/exchange_4/pallas_call | solution.py:573
  472.2 6.0 convolution_convert_fusion.1.proj_hbm
  478.3 4.9 fusion.15.grad_ref
  483.2 29.7 %attend_back.1 = (bf16[1024,512]{1,0:T(8,128)(2,1)S(1)}, f32[1024,512]{1,0:T(8,128)}, f32[1024,512]{1,0:T(8,128)}, bf16[1024,512]{1,0:T(8,128)(2,1)}, bf16[1024,...) custom-call(bf16[1024,1536]{1,0:T(8,128)(2,1)} %copy-done.1, bf16[1024,1536]{1,0:T(8,128)(2,1)} %copy-done.1, ...), custom_call_target="tpu_custom_call" | custom-call | flops 21474836480 | bytes 15728640 | tf_op jit(solution)/shard_map/attend_back/pallas_call | solution.py:1124
  512.9 8.8 %collective-permute-start.1 = (bf16[1024,512]{1,0:T(8,128)(2,1)}, bf16[1024,512]{1,0:T(8,128)(2,1)S(1)}, u32[]{:S(2)}, u32[]{:S(2)}) collective-permute-start(bf16[1024,512]{1,0:T(8,128)(2,1)} %get-tuple-element.85), channel_id=1, source_target_pairs={{0,4},{4,0},{8,12},{12,8},{16,20},{20,16},{24,28},{28,24},{1,5},{5... | collective-permute-start | bytes 3145736 | tf_op jit(solution)/shard_map/ppermute | solution.py:1438
  521.8 2.4 collective-permute-done.1.key_in_ref
  524.2 1.7 collective-permute-done.2.value_in_ref
  526.9 14.9 %last_gradients.1 = (bf16[1024,1536]{1,0:T(8,128)(2,1)}, f32[1,1536]{1,0:T(1,128)S(1)}, bf16[2048,2048]{1,0:T(8,128)(2,1)}, bf16[4,4,64,2048]{3,2,1,0:T(8,128)(2,1)}) custom-call(bf16[2048,1024]{1,0:T(8,128)(2,1)} %get-tuple-element.61.turned_hbm, bf16[1024,512]{1,0:T(8,128)(2,1)S(1)} %get-tuple-element.82.query_ref, f32[1024,512]{1,0:T(8,128)} %get-tuple-element.83.key_ref, ...), custom_call_target="tpu_custom_call" | custom-call | flops 6442450944 | bytes 33554432 | tf_op jit(solution)/shard_map/last_gradients/pallas_call | solution.py:1245
  544.2 1.5 convert_element_type.44
  545.7 2.8 convert_element_type.43
  549.4 81.1 %exchange_6.1 = (bf16[4,4,64,2048]{3,2,1,0:T(8,128)(2,1)}, f32[8,16,128]{2,1,0:T(8,128)}) custom-call(bf16[2,4,2,64,1536]{4,3,2,1,0:T(8,128)(2,1)} %bitcast.90, bf16[2048,2048]{1,0:T(8,128)(2,1)} %all-gather.5.cloned.1.call-done.weight_ref, f32[4,64,2048]{2,1,0:T(8,128)} %get-tuple-element.91.grad_ref, f32[8,16,128]{2,1,0:T(8,128)} %bitcast.92), custom_call_target="tpu_custom_call" | custom-call | bytes 209715200 | tf_op jit(solution)/shard_map/exchange_6/pallas_call | solution.py:573
  630.4 6.7 %convert.2 = f32[2,2,256,2048]{3,2,1,0:T(8,128)} convert(bf16[2,2,256,2048]{3,2,1,0:T(8,128)(2,1)} %bitcast.83) | non-fusion elementwise | flops 2097152 | bytes 12582912 | tf_op jit(solution)/shard_map/reshape | solution.py:1472
  638.4 21.2 %reduce-scatter.8.cloned.1.call-done = bf16[256,2048]{1,0:T(8,128)(2,1)} async-done(((bf16[2048,2048]{1,0:T(8,128)(2,1)}), bf16[256,2048]{1,0:T(8,128)(2,1)}) %reduce-scatter.8.cloned.1.call-update) | async-done | bytes 1048592 | tf_op jit(solution)/shard_map/reduce_scatter | solution.py:1452
  659.6 1.5 convert_element_type.42
  662.2 1.2 fusion.18
  (106 shorter events, 14.9 us)
Async XLA Ops:
  7.2 4.3 copy-start.3
  7.2 6.1 copy-start.8
  7.2 6.1 copy-start.9
  7.2 6.1 copy-start.11
  7.2 6.1 copy-start.12
  7.2 6.1 copy-start.13
  7.3 6.1 copy-start.10
  7.3 6.1 copy-start.14
  7.3 6.1 copy-start.15
  7.3 6.1 copy-start.16
  7.3 106.8 %all-gather.5.cloned.1.call-start = ((), (), s32[]{:S(2)}) async-start(), calls=%async_computation.3 | async-start | bytes 9437184 | tf_op jit(solution)/shard_map/all_gather | solution.py:1313
  10.7 229.9 %all-gather.7.cloned.1.call-start = ((), (), s32[]{:S(2)}) async-start(), calls=%async_computation.4 | async-start | bytes 9437184 | tf_op jit(solution)/shard_map/all_gather | solution.py:1314
  11.5 246.4 %all-gather.9.cloned.1.call-start = ((), (), s32[]{:S(2)}) async-start(), calls=%async_computation.5 | async-start | bytes 4718592 | tf_op jit(solution)/shard_map/all_gather | solution.py:657
  12.6 281.5 %all-gather.11.cloned.1.call-start = ((), (), s32[]{:S(2)}) async-start(), calls=%async_computation.6 | async-start | bytes 4718592 | tf_op jit(solution)/shard_map/all_gather | solution.py:657
  13.2 459.0 %reduce-scatter.4.cloned.1.call-start = ((), (), s32[]{:S(2)}) async-start(), calls=%async_computation.7 | async-start | bytes 9437184 | tf_op jit(solution)/shard_map/reduce_scatter | solution.py:1393
  124.2 1.7 copy-start.1
  124.4 6.5 collective-permute-start
  125.9 25.9 %copy-start.5 = (f32[1,1,8,256]{3,1,2,0:T(1,128)}, f32[1,1,8,256]{3,1,2,0:T(1,128)S(1)}, u32[]{:S(2)}) copy-start(f32[1,1,8,256]{3,1,2,0:T(1,128)S(1)} %copy.42) | copy-start | bytes 24580
  364.8 180.9 %reduce-scatter.6.cloned.1.call-start = ((), (), s32[]{:S(2)}) async-start(), calls=%async_computation.8 | async-start | bytes 9437184 | tf_op jit(solution)/shard_map/reduce_scatter | solution.py:1407
  394.8 264.8 %reduce-scatter.8.cloned.1.call-start = ((), (), s32[]{:S(2)}) async-start(), calls=%async_computation.9 | async-start | bytes 9437184 | tf_op jit(solution)/shard_map/reduce_scatter | solution.py:1452
  472.2 6.1 copy-start.17
  512.9 11.3 %collective-permute-start.1 = (bf16[1024,512]{1,0:T(8,128)(2,1)}, bf16[1024,512]{1,0:T(8,128)(2,1)S(1)}, u32[]{:S(2)}, u32[]{:S(2)}) collective-permute-start(bf16[1024,512]{1,0:T(8,128)(2,1)} %get-tuple-element.85), channel_id=1, source_target_pairs={{0,4},{4,0},{8,12},{12,8},{16,20},{20,16},{24,28},{28,24},{1,5},{5... | collective-permute-start | bytes 3145736 | tf_op jit(solution)/shard_map/ppermute | solution.py:1438
  521.7 4.2 collective-permute-start.2
  524.2 1.7 copy-start.18
  525.9 1.0 copy-start.19
  541.8 1.0 copy-start.4
  541.8 1.7 copy-start.7
  541.8 2.4 copy-start.2
  630.4 6.7 %copy-start.6 = (f32[8,16,128]{2,1,0:T(8,128)S(1)}, f32[8,16,128]{2,1,0:T(8,128)}, u32[]{:S(2)}) copy-start(f32[8,16,128]{2,1,0:T(8,128)} %get-tuple-element.98) | copy-start | bytes 196612
  659.6 2.6 copy-start
Sparse Core Ops, SparseCore 0:
  10.9 100.4 all-gather.4
  113.0 83.0 all-gather.6
  198.3 47.6 all-gather.8
  248.0 46.0 all-gather.10
  364.9 90.2 reduce-scatter.3
  457.3 87.7 reduce-scatter.5
  547.4 112.1 reduce-scatter.7

commit v5 on v4

--- a/solution.py
+++ b/solution.py
@@ -166,22 +166,25 @@
 
 
 class Product:
-    def __init__(self, exchange, turned, left_ref, weight_ref, weight, rows, load_sem):
+    def __init__(self, exchange, turned, left_ref, weight_ref, weight, rows, load_sem, blocks=None):
         self.exchange, self.turned = exchange, turned
         self.left, self.weight, self.rows = left_ref, weight, rows
         width = exchange.parts.shape[-1]
-        self.count = load_sem.shape[0]
-        self.step = width // self.count
+        self.step = min(512, width)
+        self.count = width // self.step
         depth = left_ref.shape[-1]
-        self.loads = []
+        self.loads, slot = [], 0
         for index in range(self.count):
             span = pl.ds(index * self.step, self.step)
             place = (span, pl.ds(0, depth)) if turned else (pl.ds(0, depth), span)
-            copy = pltpu.make_async_copy(
-                weight_ref.at[place], weight.at[place], load_sem.at[index]
-            )
-            copy.start()
-            self.loads.append(copy)
+            pairs = [(weight_ref.at[place], weight.at[place])] if blocks is None else blocks(index)
+            copies = []
+            for source, target in pairs:
+                copy = pltpu.make_async_copy(source, target, load_sem.at[slot])
+                copy.start()
+                copies.append(copy)
+                slot += 1
+            self.loads.append(copies)
 
     def make(self, batch, first=False):
         _, _, half, piece_rows, _ = self.left.shape
@@ -204,7 +207,8 @@
 
         if first:
             for index in range(self.count):
-                self.loads[index].wait()
+                for copy in self.loads[index]:
+                    copy.wait()
                 columns(index)
         else:
             pl.loop(0, self.count)(columns)
@@ -286,46 +290,59 @@
 
 
 def half_sum_kernel(
-    groups, left_ref, weight_ref, total_ref, turned_ref,
-    landed, relay, part_ref, weight, rows, load_sem, send_sem, recv_sem,
+    groups, members, left_ref, weight_ref, first_ref, total_ref, turned_ref, weight_out, first_turned_ref,
+    landed, relay, part_ref, weight, rows, load_sem, put_sem, send_sem, recv_sem,
 ):
     exchange = Exchange(part_ref, landed, relay, send_sem, recv_sem)
-    product = Product(exchange, False, left_ref, weight_ref, weight, rows, load_sem)
+    width, depth = weight.shape
+    narrow, half = width // members, depth // 2
+    apart = weight_ref.shape[1] - half
+
+    def blocks(index):
+        step = min(512, width)
+        for place in range(index * step // narrow, (index + 1) * step // narrow):
+            for part in range(2):
+                yield (
+                    weight_ref.at[pl.ds((2 * place + part) * narrow, narrow), pl.ds(apart, half)],
+                    weight.at[pl.ds(place * narrow, narrow), pl.ds(part * half, half)],
+                )
+
+    product = Product(exchange, True, left_ref, weight_ref, weight, rows, load_sem, blocks)
     greet([{"mp": exchange.along_x}, {"mp": exchange.along_y}])
 
     def work(index, piece, total):
         total_ref[piece] = total
 
-    fill = turner(lambda span: left_ref[:, :, :, :, span], turned_ref)
+    turn_left = turner(lambda span: left_ref[:, :, :, :, span], turned_ref)
+    turn_first = turner(lambda span: first_ref[:, span], first_turned_ref)
+
+    def fill(part):
+        turn_left(part)
+        turn_first(part)
+
     _, second = run_pieces(exchange, range(groups), work, product, fill)
+    put = pltpu.make_async_copy(weight, weight_out, put_sem)
+    put.start()
     for index, piece in second:
         work(index, piece, exchange.total(index, piece))
+    put.wait()
     exchange.sent()
 
 
 def second_norm_kernel(
-    groups, per, left_ref, weights_ref, weight_ref, turned_ref, done_ref,
+    groups, per, left_ref, weight_ref, turned_hbm, done_ref,
     normal_ref, cotan_ref, rows_ref,
-    low_ref, grad_ref, back_ref, sums_ref, weight_grad_ref, whole_ref,
+    low_ref, grad_ref, back_ref, sums_ref, weight_grad_ref,
     landed, relay, part_ref, weight, rows, load_sem,
-    ready, layer, cotan_in, done_weight, whole, put_sem, whole_sem,
+    ready, layer, cotan_in, turned_ref, whole, put_sem, turned_sem,
     send_sem, recv_sem, local_sem,
 ):
     exchange = Exchange(part_ref, landed, relay, send_sem, recv_sem)
-    product = Product(exchange, False, left_ref, weight_ref, weight, rows, load_sem)
+    product = Product(exchange, True, left_ref, weight_ref, weight, rows, load_sem)
     members = groups * per
-    narrow = weight.shape[1] // members
-    load_done = pltpu.make_async_copy(weights_ref, done_weight, whole_sem.at[0])
-    load_done.start()
-
-    def join(part):
-        if part == 0:
-            load_done.wait()
-        for place in range(part * members // 2, (part + 1) * members // 2):
-            for index, source in enumerate((done_weight, weight)):
-                target = pl.ds((2 * place + index) * narrow, narrow)
-                whole[:, target] = source[:, place * narrow : (place + 1) * narrow]
-
+    narrow = weight.shape[0] // members
+    load_turned = pltpu.make_async_copy(turned_hbm, turned_ref, turned_sem)
+    load_turned.start()
     peers = planes(groups, per)
     greet([{"mp": exchange.along_x}, {"mp": exchange.along_y}] + peers[1:])
     base = 6 * groups
@@ -379,9 +396,7 @@
         sums_ref[1:2] += jnp.sum(cotan * normal, axis=0, keepdims=True)
         sums_ref[2:3] += jnp.sum(cotan, axis=0, keepdims=True)
 
-    first, second = run_pieces(exchange, range(groups), work, product, join)
-    put_whole = pltpu.make_async_copy(whole, whole_ref, whole_sem.at[1])
-    put_whole.start()
+    first, second = run_pieces(exchange, range(groups), work, product)
     for index, piece in first:
         exchange.forward(index, target(piece))
     for index, piece in second:
@@ -406,7 +421,7 @@
         return matmul(turned_ref[:, part * depth : (part + 1) * depth], low)
 
     exchange.arrived([index for index, _ in first])
-    put_whole.wait()
+    load_turned.wait()
     for copy in local[: len(first) + 1]:
         copy.wait()
 
@@ -559,12 +574,12 @@
         copy.wait()
 
 
-def product_scratch(parts, groups, piece, width, depth, turned):
+def product_scratch(parts, groups, piece, width, depth, turned, loads=1):
     return [
         pltpu.VMEM((2, parts, groups // 2, piece, width), BF),
         pltpu.VMEM((width, depth) if turned else (depth, width), BF),
         pltpu.VMEM((groups * piece, depth), BF),
-        pltpu.SemaphoreType.DMA((width // 512,)),
+        pltpu.SemaphoreType.DMA((max(width // 512, loads),)),
     ]
 
 
@@ -618,29 +633,34 @@
     )
 
 
-def half_sum(left, weight, groups, piece, parts, ident):
+def half_sum(left, second, first, groups, piece, members, parts, ident):
     rows, depth = left.shape
-    width = weight.shape[1]
+    width = second.shape[0] // 2
     return exchange_call(
-        functools.partial(half_sum_kernel, groups),
+        functools.partial(half_sum_kernel, groups, members),
         ident,
-        (left.reshape(2, parts, groups // 2, piece, depth), weight),
-        [((groups, piece, width), F32, VMEM), ((depth, rows), BF, VMEM)],
+        (left.reshape(2, parts, groups // 2, piece, depth), second, first),
+        [
+            ((groups, piece, width), F32, VMEM),
+            ((depth, rows), BF, VMEM),
+            ((width, depth), BF, ANY),
+            (first.shape[::-1], BF, VMEM),
+        ],
         (groups, piece, width),
-        product_scratch(parts, groups, piece, width, depth, False),
+        product_scratch(parts, groups, piece, width, depth, True, 2 * members)
+        + [pltpu.SemaphoreType.DMA],
         0,
         (1,),
         False,
     )
 
 
-def second_norm(left, shard, normal, cotan, rows, members, parts, ident):
+def second_norm(left, weight, turned, done, normal, cotan, rows, members, parts, ident):
     groups, piece, width = normal.shape
     depth = left.shape[-1]
     half = groups // 2
     if parts != 4:
-        weight = lax.all_gather(shard, "seq", axis=1, tiled=True)
-        part = matmul(left, weight).astype(BF)
+        part = over_cols(left, weight).astype(BF)
         total = lax.psum_scatter(part, "mp", scatter_dimension=0, tiled=True).astype(F32)
         values = normal * rows[0] + rows[1] + total.reshape(normal.shape) + rows[2]
         normal, inverse = normed(values)
@@ -651,20 +671,14 @@
         sums = [jnp.sum(array, axis=(0, 1)) for array in (grad, cotan * normal, cotan)]
         sums = jnp.stack(sums + [jnp.zeros_like(sums[0])] * 5)
         low = lax.all_gather(grad.astype(BF), "mp", axis=0)
-        return low, grad, back, sums, over_rows(left, low.reshape(-1, width)).astype(BF), weight
-    narrow = shard.shape[1] // 2
-    weights = [
-        lax.all_gather(block, "seq", axis=1, tiled=True)
-        for block in (shard[:, :narrow], shard[:, narrow:])
-    ]
-    done, turned = half_sum(left, weights[0], groups, piece, parts, ident + 10)
+        return low, grad, back, sums, over_rows(left, low.reshape(-1, width)).astype(BF)
     block = pltpu.VMEM((groups, piece, width), BF)
     return exchange_call(
         functools.partial(second_norm_kernel, groups, members // groups),
         ident,
         (
             left.reshape(2, parts, half, piece, depth),
-            weights[0], weights[1], turned, done, normal, cotan, rows,
+            weight, turned, done, normal, cotan, rows,
         ),
         [
             ((2, parts, half, piece, width), BF, VMEM),
@@ -672,18 +686,17 @@
             ((groups, piece, width), BF, ANY),
             ((8, width), F32, VMEM),
             ((depth, width), BF, ANY),
-            ((depth, width), BF, ANY),
         ],
         (groups, piece, width // 2),
-        product_scratch(parts, groups, piece, width // 2, depth, False)
+        product_scratch(parts, groups, piece, width // 2, depth, True)
         + [
             block,
             block,
             block,
-            pltpu.VMEM((depth, width // 2), BF),
+            pltpu.VMEM(turned.shape, BF),
             pltpu.VMEM((depth, width), BF),
             pltpu.SemaphoreType.DMA((width // 256,)),
-            pltpu.SemaphoreType.DMA((2,)),
+            pltpu.SemaphoreType.DMA,
         ],
         2 * groups,
         (1, 2),
@@ -694,7 +707,7 @@
     groups, piece, width = normal.shape
     depth = left.shape[-1]
     if parts != 4:
-        part = over_cols(left, weight).astype(BF)
+        part = over_cols(left, weight[:, :depth]).astype(BF)
         total = lax.psum_scatter(part, "mp", scatter_dimension=0, tiled=True).astype(F32)
         grad = total.reshape(normal.shape) + grad
         moved = norm_back(grad, normal, inverse, rows[0])
@@ -936,7 +949,9 @@
     )(qkv, qkv, qkv, kv_far, kv_far)
 
 
-def share_meanwhile(now, count, pieces, back_ref, all_ref, send_sem, recv_sem, local_sem):
+def share_meanwhile(
+    now, count, pieces, back_ref, all_ref, send_sem, recv_sem, local_sem, also=()
+):
     me, along_x, along_y, _ = square()
     send = sender(send_sem, recv_sem, False)
     near, far, passed, local = [], [], [], []
@@ -951,7 +966,7 @@
 
     @pl.when(now == 0)
     def _():
-        greet([{"mp": along_x}, {"mp": along_y}])
+        greet([{"mp": along_x}, {"mp": along_y}, *also])
         for copy in near + far + local:
             copy.start()
 
@@ -983,7 +998,7 @@
 
 
 def feed_back_kernel(
-    pieces, low_ref, weight_ref, pre_ref, turned_ref, back_ref,
+    pieces, members, low_ref, weight_ref, more_ref, pre_ref, turned_ref, back_ref,
     grad_ref, sums_ref, weight_grad_ref, all_ref, send_sem, recv_sem, local_sem,
 ):
     now, count = pl.program_id(0), pl.num_programs(0)
@@ -995,20 +1010,29 @@
     slope = 0.5 * (1 + bent) + (0.5 * root) * value * (1 - bent * bent) * (
         1 + 3 * 0.044715 * square_of
     )
-    grad = (over_cols(low_ref[...], weight_ref[...]) * slope).astype(BF)
+    narrow = weight_ref.shape[0] // members
+    weight = jnp.concatenate(
+        [
+            half[place * narrow : (place + 1) * narrow]
+            for place in range(members)
+            for half in (weight_ref, more_ref)
+        ],
+        axis=0,
+    )
+    grad = (matmul(low_ref[...], weight) * slope).astype(BF)
     grad_ref[...] = grad
     sums_ref[...] = jnp.sum(grad.astype(F32), axis=0, keepdims=True)
     weight_grad_ref[...] = matmul(turned_ref[...], grad).astype(BF)
     finish()
 
 
-def feed_back(low, weight, inner_pre, turned, layer_back, pieces, parts, ident):
+def feed_back(low, weight, more, inner_pre, turned, layer_back, pieces, members, parts, ident):
     rows, hidden = inner_pre.shape
     width = low.shape[1]
     step = 512
     _, piece, _ = layer_back.shape
     return pl.pallas_call(
-        functools.partial(feed_back_kernel, pieces),
+        functools.partial(feed_back_kernel, pieces, members),
         grid=(hidden // step,),
         out_shape=(
             jax.ShapeDtypeStruct((rows, hidden), BF),
@@ -1018,7 +1042,8 @@
         ),
         in_specs=[
             pl.BlockSpec((rows, width), lambda i: (0, 0)),
-            pl.BlockSpec((step, width), lambda i: (i, 0)),
+            pl.BlockSpec((width // 2, step), lambda i: (0, i)),
+            pl.BlockSpec((width // 2, step), lambda i: (0, i)),
             pl.BlockSpec((rows, step), lambda i: (0, i)),
             pl.BlockSpec((width, rows), lambda i: (0, 0)),
             ANY,
@@ -1037,7 +1062,12 @@
             flops=4 * rows * width * hidden, bytes_accessed=40 * MIB, transcendentals=rows * hidden
         ),
         name="feed_back",
-    )(low, weight, inner_pre, turned, layer_back)
+    )(low, weight, more, inner_pre, turned, layer_back)
+
+
+def sibling():
+    here = lax.axis_index("seq")
+    return {"seq": here + 1 - 2 * lax.rem(here, 2)}
 
 
 def attend_back_kernel(
@@ -1056,19 +1086,31 @@
     sharing = len(pieces) > 0
     if sharing:
         back_ref, *rest = rest
-    dquery_ref, dkey_ref, dvalue_ref, dkey_far_ref, dvalue_far_ref, *rest = rest
+    dquery_ref, dkey_ref, dvalue_ref, *rest = rest
     if sharing:
-        all_ref, *rest = rest
+        in_ref, all_ref, *rest = rest
+    else:
+        dkey_far_ref, dvalue_far_ref, *rest = rest
     turned, key_sum, value_sum, *rest = rest
     block = pl.program_id(1)
     rows = key_ref.shape[0]
     if sharing:
-        send_sem, recv_sem, local_sem = rest
+        away, pair_send, pair_recv, send_sem, recv_sem, local_sem = rest
         now = pl.program_id(0) * pl.num_programs(1) + block
         count = pl.num_programs(0) * pl.num_programs(1)
         finish = share_meanwhile(
-            now, count, pieces, back_ref, all_ref, send_sem, recv_sem, local_sem
+            now, count, pieces, back_ref, all_ref, send_sem, recv_sem, local_sem, [sibling()]
         )
+
+        def cross(kind, head):
+            return pltpu.make_async_remote_copy(
+                src_ref=away.at[kind, head],
+                dst_ref=in_ref.at[kind, head],
+                send_sem=pair_send.at[kind, head],
+                recv_sem=pair_recv.at[kind, head],
+                device_id=sibling(),
+                device_id_type=MESH,
+            )
 
     @pl.when(block == 0)
     def _():
@@ -1101,10 +1143,23 @@
     def _():
         dkey_ref[...] = key_sum[:rows]
         dvalue_ref[...] = value_sum[:rows]
-        dkey_far_ref[...] = key_sum[rows:].astype(BF)
-        dvalue_far_ref[...] = value_sum[rows:].astype(BF)
+        if sharing:
+            head = pl.program_id(0)
+            for kind, total in enumerate((key_sum, value_sum)):
+                away[kind, head] = total[rows:].astype(BF)
+                cross(kind, head).start()
+        else:
+            dkey_far_ref[...] = key_sum[rows:].astype(BF)
+            dvalue_far_ref[...] = value_sum[rows:].astype(BF)
 
     if sharing:
+
+        @pl.when(now == count - 1)
+        def _():
+            for kind in range(2):
+                for head in range(away.shape[1]):
+                    cross(kind, head).wait()
+
         finish()
 
 
@@ -1128,10 +1183,15 @@
             jax.ShapeDtypeStruct((rows, cols), BF),
             jax.ShapeDtypeStruct((rows, cols), F32),
             jax.ShapeDtypeStruct((rows, cols), F32),
-            jax.ShapeDtypeStruct((away, cols), BF),
-            jax.ShapeDtypeStruct((away, cols), BF),
         )
-        + ((jax.ShapeDtypeStruct((len(pieces), parts, piece, width), BF),) if sharing else ()),
+        + (
+            (
+                jax.ShapeDtypeStruct((2, heads, rows, DH), BF),
+                jax.ShapeDtypeStruct((len(pieces), parts, piece, width), BF),
+            )
+            if sharing
+            else (jax.ShapeDtypeStruct((away, cols), BF),) * 2
+        ),
         in_specs=[
             tile(0),
             long(rows, heads),
@@ -1143,14 +1203,23 @@
             pl.BlockSpec((1, 1, block), lambda h, i: (h, 0, i)),
         ]
         + ([ANY] if sharing else []),
-        out_specs=(tile(0), long(rows, 0), long(rows, 0), long(away, 0), long(away, 0))
-        + ((ANY,) if sharing else ()),
+        out_specs=(tile(0), long(rows, 0), long(rows, 0))
+        + ((ANY, ANY) if sharing else (long(away, 0), long(away, 0))),
         scratch_shapes=[
             pltpu.VMEM((DH, rows + away), BF),
             pltpu.VMEM((rows + away, DH), F32),
             pltpu.VMEM((rows + away, DH), F32),
         ]
-        + (meanwhile_scratch(pieces) if sharing else []),
+        + (
+            [
+                pltpu.VMEM((2, heads, rows, DH), BF),
+                pltpu.SemaphoreType.DMA((2, heads)),
+                pltpu.SemaphoreType.DMA((2, heads)),
+            ]
+            + meanwhile_scratch(pieces)
+            if sharing
+            else []
+        ),
         compiler_params=pltpu.CompilerParams(
             vmem_limit_bytes=52 * MIB,
             **(dict(collective_id=ident, has_side_effects=True) if sharing else {}),
@@ -1188,7 +1257,7 @@
 
 
 def last_kernel(
-    per, turned_hbm, query_ref, key_ref, value_ref, key_in_ref, value_in_ref, proj_hbm, layer_hbm, layer_more_hbm,
+    per, turned_hbm, query_ref, key_ref, value_ref, in_ref, proj_hbm, layer_hbm, layer_more_hbm,
     grad_ref, sums_ref, part_ref, layer_ref, turned_ref, made, proj, layer, load_sem, put_sem,
 ):
     rows, cols = query_ref.shape
@@ -1215,10 +1284,13 @@
         puts.append(copy)
 
     for index, (own, far) in enumerate(
-        ((query_ref, None), (key_ref, key_in_ref), (value_ref, value_in_ref))
+        ((query_ref, None), (key_ref, 0), (value_ref, 1))
     ):
         span = pl.ds(index * cols, cols)
-        grad = own[...] if far is None else (own[...] + far[...].astype(F32)).astype(BF)
+        grad = own[...]
+        if far is not None:
+            far = [in_ref[far, head] for head in range(cols // DH)]
+            grad = (grad + jnp.concatenate(far, axis=1).astype(F32)).astype(BF)
         grad_ref[:, span] = grad
         sums_ref[:, span] = jnp.sum(grad.astype(F32), axis=0, keepdims=True)
         for place in range(count):
@@ -1239,7 +1311,7 @@
         copy.wait()
 
 
-def last_gradients(turned, query, key, value, key_in, value_in, proj_part, layer, layer_more, per):
+def last_gradients(turned, query, key, value, arrived, proj_part, layer, layer_more, per):
     rows, cols = query.shape
     width = turned.shape[0]
     return pl.pallas_call(
@@ -1250,7 +1322,7 @@
             jax.ShapeDtypeStruct((width, 4 * cols), BF),
             jax.ShapeDtypeStruct((2 * layer.shape[0],) + layer.shape[1:], layer.dtype),
         ),
-        in_specs=[ANY] + [VMEM] * 5 + [ANY] * 3,
+        in_specs=[ANY] + [VMEM] * 4 + [ANY] * 3,
         out_specs=(VMEM, VMEM, ANY, ANY),
         scratch_shapes=[
             pltpu.VMEM(turned.shape, BF),
@@ -1265,7 +1337,7 @@
             flops=6 * rows * width * cols, bytes_accessed=32 * MIB, transcendentals=0
         ),
         name="last_gradients",
-    )(turned, query, key, value, key_in, value_in, proj_part, layer, layer_more)
+    )(turned, query, key, value, arrived, proj_part, layer, layer_more)
 
 
 def packed(vectors, lines):
@@ -1300,7 +1372,7 @@
     micro, seqs, length, width = tokens.shape
     groups = micro * seqs
     per = members // groups
-    assert per * groups == members
+    assert per * groups == members and (parts != 4 or per == 2)
     piece = length // parts
     rows = groups * length
     quarter = groups * piece
@@ -1311,7 +1383,21 @@
     heads = cols // DH
     first = jnp.concatenate([query_weight, key_weight, value_weight, proj_weight.T], axis=1)
     first = lax.all_gather(first, "seq", axis=0, tiled=True)
-    w_inner = lax.all_gather(inner_weight, "seq", axis=0, tiled=True)
+    hidden = inner_weight.shape[1]
+    fused = parts == 4 and per == 2
+    outer_turned = outer_weight.T
+    if fused:
+        part = depth // 2
+        folded = jnp.concatenate(
+            [outer_turned[:part, : hidden // 2], outer_turned[:part, hidden // 2 :]], axis=0
+        )
+        second = jnp.concatenate([inner_weight, folded], axis=1)
+        second = lax.all_gather(second, "seq", axis=0, tiled=True)
+        w_inner = second[:, :hidden]
+        w_outer = lax.all_gather(outer_turned[part:], "seq", axis=0, tiled=True)
+    else:
+        w_inner = second = lax.all_gather(inner_weight, "seq", axis=0, tiled=True)
+        w_outer = lax.all_gather(outer_turned, "seq", axis=0, tiled=True)
     w_qkv = first[:, : 3 * cols]
     w_proj = first[:, 3 * cols :]
     vectors = [
@@ -1377,13 +1463,21 @@
 
     inner_pre = matmul(first_low, w_inner) + b_inner
     active = gelu_tanh(inner_pre).astype(BF)
-    first_turned = first_low.T
-    second_low, second_grad, layer_back, sums, outer_w_part, w_outer = second_norm(
+    done, active_turned, w_outer_half = None, None, None
+    if fused:
+        done, active_turned, w_outer_half, first_turned = half_sum(
+            active, second, first_low, groups, piece, members, parts, 13
+        )
+    else:
+        first_turned = first_low.T
+    second_low, second_grad, layer_back, sums, outer_w_part = second_norm(
         active,
-        outer_weight,
+        w_outer,
+        active_turned,
+        done,
         normal_one,
         jnp.stack(to_blocks(cotangent)),
-        after(jnp.stack([gain_one, shift_one, b_outer, gain_two, shift_two]), first_turned),
+        jnp.stack([gain_one, shift_one, b_outer, gain_two, shift_two]),
         members,
         parts,
         3,
@@ -1391,23 +1485,31 @@
     second_low = second_low.reshape(rows, width)
 
     outer_w_grad = lax.psum_scatter(outer_w_part, "seq", scatter_dimension=1, tiled=True)
-    fused = parts == 4 and per == 2
     pieces = list(range(groups)) if fused else []
     early, late = pieces[: groups // 2], pieces[groups // 2 :]
     if fused:
         inner_grad, inner_b_grad, inner_w_part, layer_out = feed_back(
-            second_low, w_outer, inner_pre, first_turned, layer_back, early, parts, 7
+            second_low,
+            w_outer_half,
+            w_outer,
+            inner_pre,
+            first_turned,
+            layer_back,
+            early,
+            members,
+            parts,
+            7,
         )
     else:
         _, pull_gelu = jax.vjp(gelu_tanh, inner_pre)
-        inner_grad = pull_gelu(over_cols(second_low, w_outer))[0].astype(BF)
+        inner_grad = pull_gelu(matmul(second_low, w_outer))[0].astype(BF)
         inner_b_grad = jnp.sum(inner_grad.astype(F32), axis=0)
         inner_w_part = matmul(first_turned, inner_grad).astype(BF)
         layer_out = lax.all_gather(jnp.roll(layer_back, group, axis=0), "mp", axis=1)
     inner_w_grad = lax.psum_scatter(inner_w_part, "seq", scatter_dimension=0, tiled=True)
     attn_low, attn_grad, summed_rows = first_back(
         inner_grad,
-        w_inner,
+        second,
         second_grad,
         normal_one,
         inverse_one,
@@ -1421,7 +1523,7 @@
 
     proj_w_part = over_rows(attn_low, mixture_low).astype(BF)
     mixture_grad = matmul(after(attn_low, proj_w_part), w_proj).astype(BF)
-    query_grad, key_grad, value_grad, key_away, value_away, *layer_more = attend_back(
+    query_grad, key_grad, value_grad, *others = attend_back(
         qkv, kv_far, mixture_grad, mixture, logs, heads, layer_back, late, parts, 5
     )
 
@@ -1429,23 +1531,21 @@
         return [array[i * rows : (i + 1) * rows] for i in range(per - 1)]
 
     if fused:
-        pairs = [(index, index + 1 - 2 * (index % 2)) for index in range(members)]
         qkv_grad, bias_grad, last_w_part, layer_out = last_gradients(
             x_turned,
             query_grad,
             key_grad,
             value_grad,
-            lax.ppermute(key_away, "seq", pairs),
-            lax.ppermute(value_away, "seq", pairs),
+            others[0],
             proj_w_part,
             layer_out,
-            layer_more[0],
+            others[1],
             per,
         )
         bias_grad = bias_grad[0]
     else:
-        key_grad = to_group_members(key_grad, blocks_of(key_away), members, per)
-        value_grad = to_group_members(value_grad, blocks_of(value_away), members, per)
+        key_grad = to_group_members(key_grad, blocks_of(others[0]), members, per)
+        value_grad = to_group_members(value_grad, blocks_of(others[1]), members, per)
         qkv_grad = jnp.concatenate([query_grad, key_grad.astype(BF), value_grad.astype(BF)], axis=1)
         last_w_part = jnp.concatenate([matmul(x_turned, qkv_grad).astype(BF), proj_w_part], axis=1)
         bias_grad = jnp.sum(qkv_grad.astype(F32), axis=0)

time: 679 us -> 663 us (0.976)
  waiting for transfers between devices: 40.4 us -> 28.2 us
  Pallas kernels: 522 us -> 534 us
  starting transfers between devices: 10.5 us -> 1.54 us
  local copies, waits for them, and re-layouts: 19.3 us -> 12.4 us
    pallas_call x1, Pallas kernels: 29.7 us -> 44 us  [attend_back(): pl.pallas_call(functools.partial(attend_back_kernel, pieces, step), grid=...]
    ppermute x2 -> x0, starting transfers between devices: 8.88 us -> none  [the longest x1 8.8 us: on_device(): lax.ppermute(key_away, 'seq', pairs)]
    all_gather x3 -> x2, waiting for transfers between devices: 11.2 us -> 2.34 us  [the longest x1 2.32 us: on_device(): w_outer = lax.all_gather(outer_turned[part:], 'seq', axis=0, tiled=True)]
  transfers between devices with their start and end apart: 10 -> 7, of which waited for: 5 -> 3; matrix products, arithmetic and copies ran while one was open for 11% -> 10% of each run, Pallas kernels for 67% -> 71%
where the time goes in v5:
time: 663 us; the launch traced here: 655 us
  Pallas kernels  534 us (81%)
  matrix products  44.4 us (7%)
  waiting for transfers between devices  28.2 us (4%)
  other arithmetic  19.2 us (3%)
  between operations  15.2 us (2%)
  local copies, waits for them, and re-layouts  12.4 us (2%)
    pallas_call x5, Pallas kernels, exchange_call(): pl.pallas_call(kernel, out_shape=tuple((jax.ShapeDtypeStruct(shape, dtype...  327 us
    pallas_call x1, Pallas kernels, swap_groups(): pl.pallas_call(functools.partial(swap_kernel, groups, per, sign), out_sha...  59.3 us
    pallas_call x1, Pallas kernels, attend_back(): pl.pallas_call(functools.partial(attend_back_kernel, pieces, step), grid=...  44 us
    pallas_call x1, Pallas kernels, share_over_mp(): pl.pallas_call(share_kernel, out_shape=jax.ShapeDtypeStruct((2, parts, ow...  36.9 us
    dot_general x3, matrix products, matmul(): return jnp.dot(left, right, preferred_element_type=F32)  32.3 us
    pallas_call x1, Pallas kernels, feed_back(): pl.pallas_call(functools.partial(feed_back_kernel, pieces, members), grid...  30.5 us
    reduce_scatter x1, waiting for transfers between devices, on_device(): lax.psum_scatter(last_w_part, 'seq', scatter_dimension=0, tiled=True)  24.5 us
    pallas_call x1, Pallas kernels, attend(): pl.pallas_call(attend_kernel, grid=(heads, rows // block), out_shape=(jax...  20.9 us
  transfers between devices with their start and end apart: 7, of which 3 were waited for; matrix products, arithmetic and copies ran while one was open for 10% of the time, Pallas kernels for 71%

profile of v5, /device:TPU:9, one launch (start us, length us, event | category | flops | bytes accessed | tf_op | source)
XLA Modules:
  0.0 654.8 jit_solution(11226593873653016065)
XLA Ops:
  7.3 1.2 copy.34
  8.5 2.2 pad_maximum_fusion.1
  11.6 1.3 maximum_maximum_fusion
  14.1 1.7 constant_dynamic-slice_fusion.3
  15.8 1.1 pad_maximum_fusion.block_ref
  17.5 59.3 %swap_groups_1.1 = (bf16[4,64,2048]{2,1,0:T(8,128)(2,1)}, bf16[8,16,128]{2,1,0:T(8,128)(2,1)}) custom-call(bf16[4,64,2048]{2,1,0:T(8,128)(2,1)} %pad_maximum_fusion.block_ref, bf16[8,16,128]{2,1,0:T(8,128)(2,1)} %broadcast_in_dim.12.small_ref), custom_call_target="tpu_custom_call" | custom-call | bytes 62914560 | tf_op jit(solution)/shard_map/swap_groups_1/pallas_call | solution.py:864
  77.8 36.9 %share_over_mp_8.1 = bf16[2,4,128,2048]{3,2,1,0:T(8,128)(2,1)} custom-call(bf16[256,2048]{1,0:T(8,128)(2,1)} %bitcast.86), custom_call_target="tpu_custom_call" | custom-call | bytes 104857600 | tf_op jit(solution)/shard_map/share_over_mp_8/pallas_call | solution.py:799
  114.7 10.0 %add_convert_fusion.query_ref.key_ref.value_ref = bf16[1024,1536]{1,0:T(8,128)(2,1)S(1)} fusion(bf16[1024,2048]{1,0:T(8,128)(2,1)} %bitcast.78, bf16[2048,2048]{1,0:T(8,128)(2,1)} %all-gather.4.cloned.1.call-done.weight_ref, f32[1536]{0:T(1024)S(1)} %pad_maximum_fusion.4), kind=kOutput, calls=%fused_computation.13 | convolution fusion | flops 6445596672 | bytes 13637632 | tf_op jit(solution)/shard_map/dot_general | solution.py:22
  125.0 1.3 collective-permute-start
  127.9 1.2 pad_maximum_fusion.2.cotan_ref
  129.0 1.2 collective-permute-done.key_far_ref.value_far_ref
  130.2 20.9 %attend.1 = (f32[1024,512]{1,0:T(8,128)}, bf16[1024,512]{1,0:T(8,128)(2,1)S(1)}, f32[4,1,1024]{2,1,0:T(1,128)S(1)}) custom-call(bf16[1024,1536]{1,0:T(8,128)(2,1)} %copy-done.1, bf16[1024,1536]{1,0:T(8,128)(2,1)} %copy-done.1, bf16[1024,1536]{1,0:T(8,128)(2,1)} %copy-done.1, bf16[1024,1024]{1,0:T(8,128)(2,1)} %collective-permute-done.key_far_ref.value_far_ref, ...), custom_call_target="tpu_custom_call" | custom-call | flops 8589934592 | bytes 10485760 | tf_op jit(solution)/shard_map/attend/pallas_call | solution.py:925
  151.1 6.0 convolution_convert_fusion
  157.1 76.4 %exchange_2.1 = (bf16[2,4,2,64,2048]{4,3,2,1,0:T(8,128)(2,1)}, f32[4,64,2048]{2,1,0:T(8,128)}, f32[4,64,1]{2,1,0:T(8,128)}, bf16[2048,1024]{1,0:T(8,128)(2,1)}) custom-call(bf16[2,4,2,64,2048]{4,3,2,1,0:T(8,128)(2,1)} %bitcast.87, bf16[4,64,2048]{2,1,0:T(8,128)(2,1)} %get-tuple-element.57.x_ref, bf16[1024,2048]{1,0:T(8,128)(2,1)} %bitcast.79, ...), custom_call_target="tpu_custom_call" | custom-call | bytes 209715200 | tf_op jit(solution)/shard_map/exchange_2/pallas_call | solution.py:588
  233.6 17.3 %fusion.7 = (bf16[1024,2048]{1,0:T(8,128)(2,1)}, f32[1024,2048]{1,0:T(8,128)}) fusion(f32[2048]{0:T(1024)S(1)} %bitcast.107, bf16[1024,2048]{1,0:T(8,128)(2,1)} %bitcast.83, bf16[2048,3072]{1,0:T(8,128)(2,1)} %all-gather.6.cloned.1.call-done.weight_ref), kind=kOutput, calls=%fused_computation.8 | convolution fusion | flops 8610906112 | bytes 25174016 | tf_op jit(solution)/shard_map/dot_general | solution.py:22
  250.9 27.5 %exchange_13.1 = (f32[4,64,1024]{2,1,0:T(8,128)}, bf16[2048,1024]{1,0:T(8,128)(2,1)}, bf16[1024,2048]{1,0:T(8,128)(2,1)}, bf16[2048,1024]{1,0:T(8,128)(2,1)}) custom-call(bf16[2,4,2,64,2048]{4,3,2,1,0:T(8,128)(2,1)} %bitcast.80, bf16[2048,3072]{1,0:T(8,128)(2,1)} %all-gather.6.cloned.1.call-done.weight_ref, bf16[1024,2048]{1,0:T(8,128)(2,1)} %bitcast.84), custom_call_target="tpu_custom_call" | custom-call | bytes 209715200 | tf_op jit(solution)/shard_map/exchange_13/pallas_call | solution.py:588
  278.4 2.3 all-gather.8.cloned.1.call-done.weight_ref.more_ref
  280.7 68.0 %exchange_3.1 = (bf16[2,4,2,64,2048]{4,3,2,1,0:T(8,128)(2,1)}, f32[4,64,2048]{2,1,0:T(8,128)}, bf16[4,64,2048]{2,1,0:T(8,128)(2,1)}, f32[8,2048]{1,0:T(8,128)}, bf16[2048,2048]{1,0:T(8,128)(2,1)}) custom-call(bf16[2,4,2,64,2048]{4,3,2,1,0:T(8,128)(2,1)} %bitcast.81, bf16[1024,2048]{1,0:T(8,128)(2,1)} %all-gather.8.cloned.1.call-done.weight_ref.more_ref, ...), custom_call_target="tpu_custom_call" | custom-call | bytes 209715200 | tf_op jit(solution)/shard_map/exchange_3/pallas_call | solution.py:588
  348.8 30.5 %feed_back.1 = (bf16[1024,2048]{1,0:T(8,128)(2,1)}, f32[1,2048]{1,0:T(1,128)}, bf16[2048,2048]{1,0:T(8,128)(2,1)}, bf16[2,4,64,2048]{3,2,1,0:T(8,128)(2,1)}) custom-call(bf16[1024,2048]{1,0:T(8,128)(2,1)} %bitcast.108, bf16[1024,2048]{1,0:T(8,128)(2,1)} %get-tuple-element.66.weight_ref, bf16[1024,2048]{1,0:T(8,128)(2,1)} %all-gather.8.cloned.1.call-done.weight_ref.more_ref, ...), custom_call_target="tpu_custom_call" | custom-call | flops 17179869184 | bytes 41943040 | tf_op jit(solution)/shard_map/feed_back/pallas_call | solution.py:1034
  379.4 74.1 %exchange_4.1 = (bf16[2,4,2,64,2048]{4,3,2,1,0:T(8,128)(2,1)}, f32[4,64,2048]{2,1,0:T(8,128)}, f32[4,8,2048]{2,1,0:T(8,128)}) custom-call(bf16[2,4,2,64,2048]{4,3,2,1,0:T(8,128)(2,1)} %bitcast.82, bf16[2048,3072]{1,0:T(8,128)(2,1)} %all-gather.6.cloned.1.call-done.weight_ref, f32[4,64,2048]{2,1,0:T(8,128)} %get-tuple-element.70.grad_ref, ...), custom_call_target="tpu_custom_call" | custom-call | bytes 209715200 | tf_op jit(solution)/shard_map/exchange_4/pallas_call | solution.py:588
  453.6 6.1 convolution_convert_fusion.1.proj_hbm
  459.7 4.9 fusion.20.grad_ref
  464.6 44.0 %attend_back.1 = (bf16[1024,512]{1,0:T(8,128)(2,1)S(1)}, f32[1024,512]{1,0:T(8,128)}, f32[1024,512]{1,0:T(8,128)}, bf16[2,4,1024,128]{3,2,1,0:T(8,128)(2,1)}, bf16[2,4,64,2048]{3,2,1,0:T(8,128)(2,1)}) custom-call(bf16[1024,1536]{1,0:T(8,128)(2,1)} %copy-done.1, bf16[1024,1536]{1,0:T(8,128)(2,1)} %copy-done.1, bf16[1024,1536]{1,0:T(8,128)(2,1)} %copy-done.1, ...), custom_call_target="tpu_custom_call" | custom-call | flops 21474836480 | bytes 15728640 | tf_op jit(solution)/shard_map/attend_back/pallas_call | solution.py:1179
  508.6 15.1 %last_gradients.1 = (bf16[1024,1536]{1,0:T(8,128)(2,1)}, f32[1,1536]{1,0:T(1,128)S(1)}, bf16[2048,2048]{1,0:T(8,128)(2,1)}, bf16[4,4,64,2048]{3,2,1,0:T(8,128)(2,1)}) custom-call(bf16[2048,1024]{1,0:T(8,128)(2,1)} %get-tuple-element.60.turned_hbm, bf16[1024,512]{1,0:T(8,128)(2,1)S(1)} %get-tuple-element.81.query_ref, f32[1024,512]{1,0:T(8,128)} %get-tuple-element.82.key_ref, ...), custom_call_target="tpu_custom_call" | custom-call | flops 6442450944 | bytes 33554432 | tf_op jit(solution)/shard_map/last_gradients/pallas_call | solution.py:1317
  527.0 81.2 %exchange_6.1 = (bf16[4,4,64,2048]{3,2,1,0:T(8,128)(2,1)}, f32[8,16,128]{2,1,0:T(8,128)}) custom-call(bf16[2,4,2,64,1536]{4,3,2,1,0:T(8,128)(2,1)} %bitcast.90, bf16[2048,2048]{1,0:T(8,128)(2,1)} %all-gather.4.cloned.1.call-done.weight_ref, f32[4,64,2048]{2,1,0:T(8,128)} %get-tuple-element.89.grad_ref, f32[8,16,128]{2,1,0:T(8,128)} %bitcast.92), custom_call_target="tpu_custom_call" | custom-call | bytes 209715200 | tf_op jit(solution)/shard_map/exchange_6/pallas_call | solution.py:588
  608.2 6.8 %convert.2 = f32[2,2,256,2048]{3,2,1,0:T(8,128)} convert(bf16[2,2,256,2048]{3,2,1,0:T(8,128)(2,1)} %bitcast.85) | non-fusion elementwise | flops 2097152 | bytes 12582912 | tf_op jit(solution)/shard_map/reshape | solution.py:1572
  615.0 1.6 convert_element_type.43
  616.6 1.5 convert_element_type.44
  619.3 24.5 %reduce-scatter.8.cloned.1.call-done = bf16[256,2048]{1,0:T(8,128)(2,1)} async-done(((bf16[2048,2048]{1,0:T(8,128)(2,1)}), bf16[256,2048]{1,0:T(8,128)(2,1)}) %reduce-scatter.8.cloned.1.call-update) | async-done | bytes 1048592 | tf_op jit(solution)/shard_map/reduce_scatter | solution.py:1552
  643.7 1.5 convert_element_type.42
  645.3 1.0 copy.36
  646.3 1.2 fusion.23
  (101 shorter events, 9.9 us)
Async XLA Ops:
  7.2 3.6 copy-start.5
  7.2 4.4 copy-start.2
  7.2 107.5 %all-gather.4.cloned.1.call-start = ((), (), s32[]{:S(2)}) async-start(), calls=%async_computation.3 | async-start | bytes 9437184 | tf_op jit(solution)/shard_map/all_gather | solution.py:1385
  10.7 222.9 %all-gather.6.cloned.1.call-start = ((), (), s32[]{:S(2)}) async-start(), calls=%async_computation.4 | async-start | bytes 14155776 | tf_op jit(solution)/shard_map/all_gather | solution.py:1395
  11.4 2.5 copy-start.10
  11.4 2.5 copy-start.11
  11.5 2.5 copy-start.12
  11.5 2.5 copy-start.13
  11.5 2.5 copy-start.14
  11.5 2.5 copy-start.15
  11.5 2.5 copy-start.16
  11.5 2.5 copy-start.17
  11.5 2.5 copy-start.18
  12.9 267.9 %all-gather.8.cloned.1.call-start = ((), (), s32[]{:S(2)}) async-start(), calls=%async_computation.5 | async-start | bytes 4718592 | tf_op jit(solution)/shard_map/all_gather | solution.py:1397
  13.8 439.8 %reduce-scatter.4.cloned.1.call-start = ((), (), s32[]{:S(2)}) async-start(), calls=%async_computation.6 | async-start | bytes 9437184 | tf_op jit(solution)/shard_map/reduce_scatter | solution.py:1487
  124.8 1.6 copy-start.1
  125.0 5.2 collective-permute-start
  126.4 24.7 %copy-start.7 = (f32[1,1,8,256]{3,1,2,0:T(1,128)}, f32[1,1,8,256]{3,1,2,0:T(1,128)S(1)}, u32[]{:S(2)}) copy-start(f32[1,1,8,256]{3,1,2,0:T(1,128)S(1)} %copy.39) | copy-start | bytes 24580
  348.7 259.4 %reduce-scatter.6.cloned.1.call-start = ((), (), s32[]{:S(2)}) async-start(), calls=%async_computation.7 | async-start | bytes 9437184 | tf_op jit(solution)/shard_map/reduce_scatter | solution.py:1509
  379.4 264.4 %reduce-scatter.8.cloned.1.call-start = ((), (), s32[]{:S(2)}) async-start(), calls=%async_computation.8 | async-start | bytes 9437184 | tf_op jit(solution)/shard_map/reduce_scatter | solution.py:1552
  453.6 6.1 copy-start.19
  523.7 1.0 copy-start.6
  523.7 1.7 copy-start.9
  608.2 6.9 %copy-start.8 = (f32[8,16,128]{2,1,0:T(8,128)S(1)}, f32[8,16,128]{2,1,0:T(8,128)}, u32[]{:S(2)}) copy-start(f32[8,16,128]{2,1,0:T(8,128)} %get-tuple-element.96) | copy-start | bytes 196612
  608.2 6.9 %copy-start.4 = (bf16[256,2048]{1,0:T(8,128)(2,1)S(1)}, bf16[256,2048]{1,0:T(8,128)(2,1)}, u32[]{:S(2)}) copy-start(bf16[256,2048]{1,0:T(8,128)(2,1)} %reduce-scatter.6.cloned.1.call-done) | copy-start | bytes 3145732
  608.2 8.4 %copy-start.3 = (bf16[2048,256]{1,0:T(8,128)(2,1)S(1)}, bf16[2048,256]{1,0:T(8,128)(2,1)}, u32[]{:S(2)}) copy-start(bf16[2048,256]{1,0:T(8,128)(2,1)} %reduce-scatter.4.cloned.1.call-done) | copy-start | bytes 3145732
  643.7 2.6 copy-start
Sparse Core Ops, SparseCore 0:
  10.8 101.0 all-gather.3
  114.2 117.4 all-gather.5
  233.9 46.8 all-gather.7
  348.9 91.9 reduce-scatter.3
  443.0 87.7 reduce-scatter.5
  533.0 110.7 reduce-scatter.7

commit v6 on v5

--- a/solution.py
+++ b/solution.py
@@ -169,6 +169,7 @@
     def __init__(self, exchange, turned, left_ref, weight_ref, weight, rows, load_sem, blocks=None):
         self.exchange, self.turned = exchange, turned
         self.left, self.weight, self.rows = left_ref, weight, rows
+        self.left_loads = {}
         width = exchange.parts.shape[-1]
         self.step = min(512, width)
         self.count = width // self.step
@@ -188,6 +189,9 @@
 
     def make(self, batch, first=False):
         _, _, half, piece_rows, _ = self.left.shape
+        for _, piece in batch:
+            if piece // half in self.left_loads:
+                self.left_loads.pop(piece // half).wait()
         for place, (owner, piece) in enumerate(batch):
             self.rows[place * piece_rows : (place + 1) * piece_rows] = self.left[
                 row_place(owner, piece, 2 * half)
@@ -330,19 +334,34 @@
 
 
 def second_norm_kernel(
-    groups, per, left_ref, weight_ref, turned_hbm, done_ref,
-    normal_ref, cotan_ref, rows_ref,
-    low_ref, grad_ref, back_ref, sums_ref, weight_grad_ref,
+    groups, per, left_hbm, weight_ref, turned_hbm, done_hbm,
+    normal_hbm, cotan_ref, rows_ref,
+    low_hbm, grad_hbm, back_ref, sums_ref, weight_grad_ref,
     landed, relay, part_ref, weight, rows, load_sem,
-    ready, layer, cotan_in, turned_ref, whole, put_sem, turned_sem,
+    ready, layer, cotan_in, turned_ref, whole, left_ref, done_ref, normal_ref, low_ref, grad_ref,
+    put_sem, in_sem, out_sem,
     send_sem, recv_sem, local_sem,
 ):
     exchange = Exchange(part_ref, landed, relay, send_sem, recv_sem)
+
+    def moved(source, target, sem):
+        copy = pltpu.make_async_copy(source, target, sem)
+        copy.start()
+        return copy
+
+    left_loads = {0: moved(left_hbm.at[0], left_ref.at[0], in_sem.at[0])}
     product = Product(exchange, True, left_ref, weight_ref, weight, rows, load_sem)
     members = groups * per
     narrow = weight.shape[0] // members
-    load_turned = pltpu.make_async_copy(turned_hbm, turned_ref, turned_sem)
-    load_turned.start()
+    left_loads[1] = moved(left_hbm.at[1], left_ref.at[1], in_sem.at[1])
+    product.left_loads = left_loads
+    early = [
+        moved(cotan_ref.at[0], cotan_in.at[0], in_sem.at[2]),
+        moved(normal_hbm, normal_ref, in_sem.at[3]),
+        moved(done_hbm, done_ref, in_sem.at[4]),
+    ]
+    load_turned = moved(turned_hbm, turned_ref, in_sem.at[5])
+    outward = []
     peers = planes(groups, per)
     greet([{"mp": exchange.along_x}, {"mp": exchange.along_y}] + peers[1:])
     base = 6 * groups
@@ -362,6 +381,8 @@
         local.append(copy)
 
     def work(index, piece, total):
+        while early:
+            early.pop().wait()
         gain_one, shift_one, bias = rows_ref[0:1], rows_ref[1:2], rows_ref[2:3]
         gain, shift = rows_ref[3:4], rows_ref[4:5]
         done = done_ref[piece]
@@ -378,7 +399,7 @@
         layer[index] = (normal * gain + shift).astype(BF)
         if piece == 0:
             keep(layer.at[index], back_ref.at[0], groups)
-            cotan = cotan_ref[0].astype(F32)
+            cotan = cotan_in[0].astype(F32)
         else:
             leaving.append(
                 exchange.send(
@@ -395,14 +416,13 @@
         sums_ref[0:1] += jnp.sum(grad, axis=0, keepdims=True)
         sums_ref[1:2] += jnp.sum(cotan * normal, axis=0, keepdims=True)
         sums_ref[2:3] += jnp.sum(cotan, axis=0, keepdims=True)
+        outward.append(moved(grad_ref.at[piece], grad_hbm.at[piece], out_sem.at[2 + index]))
 
     first, second = run_pieces(exchange, range(groups), work, product)
     for index, piece in first:
         exchange.forward(index, target(piece))
     for index, piece in second:
         work(index, piece, exchange.total(index, piece))
-    for index, piece in second:
-        exchange.forward(index, target(piece))
     step = 256
     count = whole.shape[1] // step
     depth = turned_ref.shape[1] // 2
@@ -424,15 +444,25 @@
     load_turned.wait()
     for copy in local[: len(first) + 1]:
         copy.wait()
-
-    @pl.loop(0, count)
-    def _(index):
-        span = columns(index)
-        whole[:, span] = product_of(0, span).astype(BF)
-
+    outward.append(moved(low_ref.at[0], low_hbm.at[0], out_sem.at[0]))
+
+    def first_product(start, stop):
+        @pl.loop(start, stop)
+        def _(index):
+            span = columns(index)
+            whole[:, span] = product_of(0, span).astype(BF)
+
+    share_out = count // (2 * len(second))
+    done = count // 2
+    first_product(0, done)
+    for index, piece in second:
+        exchange.forward(index, target(piece))
+        first_product(done, done + share_out)
+        done += share_out
     exchange.arrived([index for index, _ in second])
     for copy in local[len(first) + 1 :]:
         copy.wait()
+    outward.append(moved(low_ref.at[1], low_hbm.at[1], out_sem.at[1]))
 
     @pl.loop(0, count)
     def _(index):
@@ -441,6 +471,8 @@
         put(index).start()
 
     exchange.sent()
+    for copy in outward:
+        copy.wait()
     for copy in leaving:
         copy.wait()
     for copy in arriving.values():
@@ -681,8 +713,8 @@
             weight, turned, done, normal, cotan, rows,
         ),
         [
-            ((2, parts, half, piece, width), BF, VMEM),
-            ((groups, piece, width), F32, VMEM),
+            ((2, parts, half, piece, width), BF, ANY),
+            ((groups, piece, width), F32, ANY),
             ((groups, piece, width), BF, ANY),
             ((8, width), F32, VMEM),
             ((depth, width), BF, ANY),
@@ -695,11 +727,17 @@
             block,
             pltpu.VMEM(turned.shape, BF),
             pltpu.VMEM((depth, width), BF),
+            pltpu.VMEM((2, parts, half, piece, depth), BF),
+            pltpu.VMEM(done.shape, F32),
+            pltpu.VMEM(normal.shape, F32),
+            pltpu.VMEM((2, parts, half, piece, width), BF),
+            pltpu.VMEM((groups, piece, width), F32),
             pltpu.SemaphoreType.DMA((width // 256,)),
-            pltpu.SemaphoreType.DMA,
+            pltpu.SemaphoreType.DMA((6,)),
+            pltpu.SemaphoreType.DMA((2 + groups,)),
         ],
         2 * groups,
-        (1, 2),
+        (0, 1, 2, 3, 4, 5),
     )
 
 

time: 663 us -> 660 us (level)
  no operation moved by 1% of the time
where the time goes in v6:
time: 660 us; the launch traced here: 652 us
  Pallas kernels  532 us (81%)
  matrix products  44.4 us (7%)
  waiting for transfers between devices  27.1 us (4%)
  other arithmetic  19.3 us (3%)
  between operations  15.2 us (2%)
  local copies, waits for them, and re-layouts  12.4 us (2%)
    pallas_call x5, Pallas kernels, exchange_call(): pl.pallas_call(kernel, out_shape=tuple((jax.ShapeDtypeStruct(shape, dtype...  329 us
    pallas_call x1, Pallas kernels, swap_groups(): pl.pallas_call(functools.partial(swap_kernel, groups, per, sign), out_sha...  59.3 us
    pallas_call x1, Pallas kernels, attend_back(): pl.pallas_call(functools.partial(attend_back_kernel, pieces, step), grid=...  40.3 us
    pallas_call x1, Pallas kernels, share_over_mp(): pl.pallas_call(share_kernel, out_shape=jax.ShapeDtypeStruct((2, parts, ow...  36.9 us
    dot_general x3, matrix products, matmul(): return jnp.dot(left, right, preferred_element_type=F32)  32.3 us
    pallas_call x1, Pallas kernels, feed_back(): pl.pallas_call(functools.partial(feed_back_kernel, pieces, members), grid...  30 us
    reduce_scatter x1, waiting for transfers between devices, on_device(): lax.psum_scatter(last_w_part, 'seq', scatter_dimension=0, tiled=True)  23.3 us
    pallas_call x1, Pallas kernels, attend(): pl.pallas_call(attend_kernel, grid=(heads, rows // block), out_shape=(jax...  20.9 us
  transfers between devices with their start and end apart: 7, of which 3 were waited for; matrix products, arithmetic and copies ran while one was open for 10% of the time, Pallas kernels for 71%

profile of v6, /device:TPU:9, one launch (start us, length us, event | category | flops | bytes accessed | tf_op | source)
XLA Modules:
  0.0 651.6 jit_solution(4242265848014484826)
XLA Ops:
  7.3 1.2 copy.34
  8.5 2.2 pad_maximum_fusion.1
  11.6 1.3 maximum_maximum_fusion
  14.1 1.7 constant_dynamic-slice_fusion.3
  15.8 1.1 pad_maximum_fusion.block_ref
  17.5 59.3 %swap_groups_1.1 = (bf16[4,64,2048]{2,1,0:T(8,128)(2,1)}, bf16[8,16,128]{2,1,0:T(8,128)(2,1)}) custom-call(bf16[4,64,2048]{2,1,0:T(8,128)(2,1)} %pad_maximum_fusion.block_ref, bf16[8,16,128]{2,1,0:T(8,128)(2,1)} %broadcast_in_dim.12.small_ref), custom_call_target="tpu_custom_call" | custom-call | bytes 62914560 | tf_op jit(solution)/shard_map/swap_groups_1/pallas_call | solution.py:902
  77.8 36.9 %share_over_mp_8.1 = bf16[2,4,128,2048]{3,2,1,0:T(8,128)(2,1)} custom-call(bf16[256,2048]{1,0:T(8,128)(2,1)} %bitcast.86), custom_call_target="tpu_custom_call" | custom-call | bytes 104857600 | tf_op jit(solution)/shard_map/share_over_mp_8/pallas_call | solution.py:837
  114.7 10.0 %add_convert_fusion.query_ref.key_ref.value_ref = bf16[1024,1536]{1,0:T(8,128)(2,1)S(1)} fusion(bf16[1024,2048]{1,0:T(8,128)(2,1)} %bitcast.78, bf16[2048,2048]{1,0:T(8,128)(2,1)} %all-gather.4.cloned.1.call-done.weight_ref, f32[1536]{0:T(1024)S(1)} %pad_maximum_fusion.4), kind=kOutput, calls=%fused_computation.13 | convolution fusion | flops 6445596672 | bytes 13637632 | tf_op jit(solution)/shard_map/dot_general | solution.py:22
  125.0 1.3 collective-permute-start
  127.9 1.2 pad_maximum_fusion.2.cotan_ref
  129.0 1.2 collective-permute-done.key_far_ref.value_far_ref
  130.2 20.9 %attend.1 = (f32[1024,512]{1,0:T(8,128)}, bf16[1024,512]{1,0:T(8,128)(2,1)S(1)}, f32[4,1,1024]{2,1,0:T(1,128)S(1)}) custom-call(bf16[1024,1536]{1,0:T(8,128)(2,1)} %copy-done.1, bf16[1024,1536]{1,0:T(8,128)(2,1)} %copy-done.1, bf16[1024,1536]{1,0:T(8,128)(2,1)} %copy-done.1, bf16[1024,1024]{1,0:T(8,128)(2,1)} %collective-permute-done.key_far_ref.value_far_ref, ...), custom_call_target="tpu_custom_call" | custom-call | flops 8589934592 | bytes 10485760 | tf_op jit(solution)/shard_map/attend/pallas_call | solution.py:963
  151.1 6.0 convolution_convert_fusion
  157.1 76.4 %exchange_2.1 = (bf16[2,4,2,64,2048]{4,3,2,1,0:T(8,128)(2,1)}, f32[4,64,2048]{2,1,0:T(8,128)}, f32[4,64,1]{2,1,0:T(8,128)}, bf16[2048,1024]{1,0:T(8,128)(2,1)}) custom-call(bf16[2,4,2,64,2048]{4,3,2,1,0:T(8,128)(2,1)} %bitcast.87, bf16[4,64,2048]{2,1,0:T(8,128)(2,1)} %get-tuple-element.57.x_ref, bf16[1024,2048]{1,0:T(8,128)(2,1)} %bitcast.79, ...), custom_call_target="tpu_custom_call" | custom-call | bytes 209715200 | tf_op jit(solution)/shard_map/exchange_2/pallas_call | solution.py:620
  233.6 17.3 %fusion.7 = (bf16[1024,2048]{1,0:T(8,128)(2,1)}, f32[1024,2048]{1,0:T(8,128)}) fusion(f32[2048]{0:T(1024)S(1)} %bitcast.107, bf16[1024,2048]{1,0:T(8,128)(2,1)} %bitcast.83, bf16[2048,3072]{1,0:T(8,128)(2,1)} %all-gather.6.cloned.1.call-done.weight_ref), kind=kOutput, calls=%fused_computation.8 | convolution fusion | flops 8610906112 | bytes 25174016 | tf_op jit(solution)/shard_map/dot_general | solution.py:22
  250.9 27.5 %exchange_13.1 = (f32[4,64,1024]{2,1,0:T(8,128)}, bf16[2048,1024]{1,0:T(8,128)(2,1)}, bf16[1024,2048]{1,0:T(8,128)(2,1)}, bf16[2048,1024]{1,0:T(8,128)(2,1)}) custom-call(bf16[2,4,2,64,2048]{4,3,2,1,0:T(8,128)(2,1)} %bitcast.80, bf16[2048,3072]{1,0:T(8,128)(2,1)} %all-gather.6.cloned.1.call-done.weight_ref, bf16[1024,2048]{1,0:T(8,128)(2,1)} %bitcast.84), custom_call_target="tpu_custom_call" | custom-call | bytes 209715200 | tf_op jit(solution)/shard_map/exchange_13/pallas_call | solution.py:620
  278.4 2.3 all-gather.8.cloned.1.call-done.weight_ref.more_ref
  280.7 68.0 %exchange_3.1 = (bf16[2,4,2,64,2048]{4,3,2,1,0:T(8,128)(2,1)}, f32[4,64,2048]{2,1,0:T(8,128)}, bf16[4,64,2048]{2,1,0:T(8,128)(2,1)}, f32[8,2048]{1,0:T(8,128)}, bf16[2048,2048]{1,0:T(8,128)(2,1)}) custom-call(bf16[2,4,2,64,2048]{4,3,2,1,0:T(8,128)(2,1)} %bitcast.81, bf16[1024,2048]{1,0:T(8,128)(2,1)} %all-gather.8.cloned.1.call-done.weight_ref.more_ref, ...), custom_call_target="tpu_custom_call" | custom-call | bytes 209715200 | tf_op jit(solution)/shard_map/exchange_3/pallas_call | solution.py:620
  348.8 30.0 %feed_back.1 = (bf16[1024,2048]{1,0:T(8,128)(2,1)}, f32[1,2048]{1,0:T(1,128)}, bf16[2048,2048]{1,0:T(8,128)(2,1)}, bf16[2,4,64,2048]{3,2,1,0:T(8,128)(2,1)}) custom-call(bf16[1024,2048]{1,0:T(8,128)(2,1)} %bitcast.108, bf16[1024,2048]{1,0:T(8,128)(2,1)} %get-tuple-element.66.weight_ref, bf16[1024,2048]{1,0:T(8,128)(2,1)} %all-gather.8.cloned.1.call-done.weight_ref.more_ref, ...), custom_call_target="tpu_custom_call" | custom-call | flops 17179869184 | bytes 41943040 | tf_op jit(solution)/shard_map/feed_back/pallas_call | solution.py:1072
  378.9 77.7 %exchange_4.1 = (bf16[2,4,2,64,2048]{4,3,2,1,0:T(8,128)(2,1)}, f32[4,64,2048]{2,1,0:T(8,128)}, f32[4,8,2048]{2,1,0:T(8,128)}) custom-call(bf16[2,4,2,64,2048]{4,3,2,1,0:T(8,128)(2,1)} %bitcast.82, bf16[2048,3072]{1,0:T(8,128)(2,1)} %all-gather.6.cloned.1.call-done.weight_ref, f32[4,64,2048]{2,1,0:T(8,128)} %get-tuple-element.70.grad_ref, ...), custom_call_target="tpu_custom_call" | custom-call | bytes 209715200 | tf_op jit(solution)/shard_map/exchange_4/pallas_call | solution.py:620
  456.6 6.1 convolution_convert_fusion.1.proj_hbm
  462.8 5.0 fusion.20.grad_ref
  467.7 40.3 %attend_back.1 = (bf16[1024,512]{1,0:T(8,128)(2,1)S(1)}, f32[1024,512]{1,0:T(8,128)}, f32[1024,512]{1,0:T(8,128)}, bf16[2,4,1024,128]{3,2,1,0:T(8,128)(2,1)}, bf16[2,4,64,2048]{3,2,1,0:T(8,128)(2,1)}) custom-call(bf16[1024,1536]{1,0:T(8,128)(2,1)} %copy-done.1, bf16[1024,1536]{1,0:T(8,128)(2,1)} %copy-done.1, bf16[1024,1536]{1,0:T(8,128)(2,1)} %copy-done.1, ...), custom_call_target="tpu_custom_call" | custom-call | flops 21474836480 | bytes 15728640 | tf_op jit(solution)/shard_map/attend_back/pallas_call | solution.py:1217
  508.1 15.1 %last_gradients.1 = (bf16[1024,1536]{1,0:T(8,128)(2,1)}, f32[1,1536]{1,0:T(1,128)S(1)}, bf16[2048,2048]{1,0:T(8,128)(2,1)}, bf16[4,4,64,2048]{3,2,1,0:T(8,128)(2,1)}) custom-call(bf16[2048,1024]{1,0:T(8,128)(2,1)} %get-tuple-element.60.turned_hbm, bf16[1024,512]{1,0:T(8,128)(2,1)S(1)} %get-tuple-element.81.query_ref, f32[1024,512]{1,0:T(8,128)} %get-tuple-element.82.key_ref, ...), custom_call_target="tpu_custom_call" | custom-call | flops 6442450944 | bytes 33554432 | tf_op jit(solution)/shard_map/last_gradients/pallas_call | solution.py:1355
  526.4 79.5 %exchange_6.1 = (bf16[4,4,64,2048]{3,2,1,0:T(8,128)(2,1)}, f32[8,16,128]{2,1,0:T(8,128)}) custom-call(bf16[2,4,2,64,1536]{4,3,2,1,0:T(8,128)(2,1)} %bitcast.90, bf16[2048,2048]{1,0:T(8,128)(2,1)} %all-gather.4.cloned.1.call-done.weight_ref, f32[4,64,2048]{2,1,0:T(8,128)} %get-tuple-element.89.grad_ref, f32[8,16,128]{2,1,0:T(8,128)} %bitcast.92), custom_call_target="tpu_custom_call" | custom-call | bytes 209715200 | tf_op jit(solution)/shard_map/exchange_6/pallas_call | solution.py:620
  606.0 6.9 %convert.2 = f32[2,2,256,2048]{3,2,1,0:T(8,128)} convert(bf16[2,2,256,2048]{3,2,1,0:T(8,128)(2,1)} %bitcast.85) | non-fusion elementwise | flops 2097152 | bytes 12582912 | tf_op jit(solution)/shard_map/reshape | solution.py:1610
  612.9 1.6 convert_element_type.43
  614.5 1.5 convert_element_type.44
  617.1 23.3 %reduce-scatter.8.cloned.1.call-done = bf16[256,2048]{1,0:T(8,128)(2,1)} async-done(((bf16[2048,2048]{1,0:T(8,128)(2,1)}), bf16[256,2048]{1,0:T(8,128)(2,1)}) %reduce-scatter.8.cloned.1.call-update) | async-done | bytes 1048592 | tf_op jit(solution)/shard_map/reduce_scatter | solution.py:1590
  640.5 1.5 convert_element_type.42
  642.1 1.0 copy.36
  643.1 1.2 fusion.23
  (101 shorter events, 9.9 us)
Async XLA Ops:
  7.2 3.6 copy-start.5
  7.2 4.4 copy-start.2
  7.2 107.5 %all-gather.4.cloned.1.call-start = ((), (), s32[]{:S(2)}) async-start(), calls=%async_computation.3 | async-start | bytes 9437184 | tf_op jit(solution)/shard_map/all_gather | solution.py:1423
  10.7 222.9 %all-gather.6.cloned.1.call-start = ((), (), s32[]{:S(2)}) async-start(), calls=%async_computation.4 | async-start | bytes 14155776 | tf_op jit(solution)/shard_map/all_gather | solution.py:1433
  11.4 2.5 copy-start.10
  11.4 2.5 copy-start.11
  11.5 2.5 copy-start.12
  11.5 2.5 copy-start.13
  11.5 2.5 copy-start.14
  11.5 2.5 copy-start.15
  11.5 2.5 copy-start.16
  11.5 2.5 copy-start.17
  11.5 2.5 copy-start.18
  12.9 267.9 %all-gather.8.cloned.1.call-start = ((), (), s32[]{:S(2)}) async-start(), calls=%async_computation.5 | async-start | bytes 4718592 | tf_op jit(solution)/shard_map/all_gather | solution.py:1435
  13.8 442.8 %reduce-scatter.4.cloned.1.call-start = ((), (), s32[]{:S(2)}) async-start(), calls=%async_computation.6 | async-start | bytes 9437184 | tf_op jit(solution)/shard_map/reduce_scatter | solution.py:1525
  124.8 1.6 copy-start.1
  125.0 5.2 collective-permute-start
  126.4 24.7 %copy-start.7 = (f32[1,1,8,256]{3,1,2,0:T(1,128)}, f32[1,1,8,256]{3,1,2,0:T(1,128)S(1)}, u32[]{:S(2)}) copy-start(f32[1,1,8,256]{3,1,2,0:T(1,128)S(1)} %copy.39) | copy-start | bytes 24580
  348.8 257.2 %reduce-scatter.6.cloned.1.call-start = ((), (), s32[]{:S(2)}) async-start(), calls=%async_computation.7 | async-start | bytes 9437184 | tf_op jit(solution)/shard_map/reduce_scatter | solution.py:1547
  378.8 261.7 %reduce-scatter.8.cloned.1.call-start = ((), (), s32[]{:S(2)}) async-start(), calls=%async_computation.8 | async-start | bytes 9437184 | tf_op jit(solution)/shard_map/reduce_scatter | solution.py:1590
  456.6 6.1 copy-start.19
  523.1 1.0 copy-start.6
  523.1 1.7 copy-start.9
  606.0 6.9 %copy-start.8 = (f32[8,16,128]{2,1,0:T(8,128)S(1)}, f32[8,16,128]{2,1,0:T(8,128)}, u32[]{:S(2)}) copy-start(f32[8,16,128]{2,1,0:T(8,128)} %get-tuple-element.96) | copy-start | bytes 196612
  606.0 6.9 %copy-start.4 = (bf16[256,2048]{1,0:T(8,128)(2,1)S(1)}, bf16[256,2048]{1,0:T(8,128)(2,1)}, u32[]{:S(2)}) copy-start(bf16[256,2048]{1,0:T(8,128)(2,1)} %reduce-scatter.6.cloned.1.call-done) | copy-start | bytes 3145732
  606.0 8.5 %copy-start.3 = (bf16[2048,256]{1,0:T(8,128)(2,1)S(1)}, bf16[2048,256]{1,0:T(8,128)(2,1)}, u32[]{:S(2)}) copy-start(bf16[2048,256]{1,0:T(8,128)(2,1)} %reduce-scatter.4.cloned.1.call-done) | copy-start | bytes 3145732
  640.5 2.6 copy-start
Sparse Core Ops, SparseCore 0:
  10.8 101.0 all-gather.3
  114.2 117.4 all-gather.5
  233.9 46.8 all-gather.7
  348.9 88.6 reduce-scatter.3
  439.8 87.7 reduce-scatter.5
  529.7 110.7 reduce-scatter.7

commit v7 on v6

--- a/solution.py
+++ b/solution.py
@@ -423,7 +423,7 @@
         exchange.forward(index, target(piece))
     for index, piece in second:
         work(index, piece, exchange.total(index, piece))
-    step = 256
+    step = 512
     count = whole.shape[1] // step
     depth = turned_ref.shape[1] // 2
 
@@ -536,10 +536,119 @@
     return list(range(1, groups - 1)) + [0, groups - 1]
 
 
+class LineSum:
+    def __init__(
+        self, groups, per, blocks_ref, own, other, inbox, line_send, line_recv, pair_send, pair_recv, pair_local
+    ):
+        self.groups, self.per = groups, per
+        here = lax.axis_index("seq")
+        self.group, self.place = here // per, lax.rem(here, per)
+        self.own, self.other, self.inbox = own, other, inbox
+        self.line_send, self.line_recv = line_send, line_recv
+        sibling = {"seq": self.group * per + 1 - self.place}
+        send = sender(pair_send, pair_recv)
+        self.order = sorted(range(groups), key=lambda index: -abs(2 * index - groups + 1))
+        self.away, self.near = {}, {}
+        for index in self.order:
+            self.away[index] = send(
+                blocks_ref.at[index, 1 - self.place], other.at[index], index, sibling
+            )
+            copy = pltpu.make_async_copy(
+                blocks_ref.at[index, self.place], own.at[index], pair_local.at[index]
+            )
+            copy.start()
+            self.near[index] = copy
+
+    def seen(self, stream):
+        return self.group if stream == 0 else self.groups - 1 - self.group
+
+    def copy(self, stream, to):
+        group = to if stream == 0 else self.groups - 1 - to
+        ahead = self.group + (1 if stream == 0 else -1)
+        slot = stream * self.groups + to
+        return pltpu.make_async_remote_copy(
+            src_ref=self.own.at[group],
+            dst_ref=self.inbox.at[stream, to - 1],
+            send_sem=self.line_send.at[slot],
+            recv_sem=self.line_recv.at[slot],
+            device_id={"seq": ahead * self.per + self.place},
+            device_id_type=MESH,
+        )
+
+    def first_send(self, to):
+        for stream in range(2):
+
+            @pl.when(self.seen(stream) == 0)
+            def _(stream=stream):
+                self.copy(stream, to).start()
+
+    def pair_sums(self, indices):
+        for index in indices:
+            self.near[index].wait()
+            self.away[index].wait_recv()
+            self.own[index] = (
+                self.own[index].astype(F32) + self.other[index].astype(F32)
+            ).astype(BF)
+
+    def begin(self):
+        self.pair_sums(self.order[:2])
+        self.first_send(self.groups - 1)
+
+    def go_on(self):
+        self.pair_sums(self.order[2:])
+        self.first_send(self.groups - 2)
+
+    def hop(self, time):
+        if self.groups - 2 - time > 0:
+            for stream in range(2):
+
+                @pl.when(self.seen(stream) == 0)
+                def _(stream=stream):
+                    self.copy(stream, self.groups - time).wait_send()
+
+            self.first_send(self.groups - 2 - time)
+        for stream in range(2):
+            seen = self.seen(stream)
+
+            @pl.when((seen >= 1) & (seen <= time))
+            def _(stream=stream, seen=seen):
+                to = self.groups - 1 + seen - time
+                group = to if stream == 0 else self.groups - 1 - to
+                self.copy(stream, to).wait_recv()
+                self.own[group] = (
+                    self.own[group].astype(F32) + self.inbox[stream, to - 1].astype(F32)
+                ).astype(BF)
+                self.copy(stream, to).start()
+
+    def end(self, out_ref):
+        out_ref[...] = self.own[self.group].astype(F32)
+        for stream in range(2):
+            seen = self.seen(stream)
+
+            @pl.when(seen >= 1)
+            def _(stream=stream, seen=seen):
+                self.copy(stream, seen).wait_recv()
+                out_ref[...] += self.inbox[stream, seen - 1].astype(F32)
+
+        for stream in range(2):
+            for to in range(1, self.groups):
+
+                seen = self.seen(stream)
+                waited = (seen == 0) & (to > 2)
+
+                @pl.when((seen < to) & jnp.logical_not(waited))
+                def _(stream=stream, to=to):
+                    self.copy(stream, to).wait_send()
+
+        for copy in self.away.values():
+            copy.wait_send()
+
+
 def input_kernel(
-    groups, per, left_ref, weight_ref, grad_ref, small_ref,
-    all_ref, small_out,
+    groups, per, left_ref, weight_ref, grad_ref, small_ref, blocks_ref,
+    all_ref, small_out, block_out,
     landed, relay, ready, back, part_ref, weight, rows, load_sem,
+    own, other, inbox, line_send, line_recv, pair_send, pair_recv, pair_local,
     send_sem, recv_sem, local_sem,
 ):
     exchange = Exchange(part_ref, landed, relay, send_sem, recv_sem)
@@ -550,6 +659,10 @@
     group = here // per
     devices = [{"seq": lax.rem(here + step, members)} for step in range(1, members)]
     greet([{"mp": exchange.along_x}, {"mp": exchange.along_y}] + devices)
+    line = LineSum(
+        groups, per, blocks_ref, own, other, inbox,
+        line_send, line_recv, pair_send, pair_recv, pair_local,
+    )
     base = 6 * groups
     small = [
         exchange.send(
@@ -588,15 +701,29 @@
         exchange.share(index, source, target(piece))
         keep(source, target(piece)(exchange.me), index)
 
-    first, second = run_pieces(exchange, input_order(groups), work, product)
+    def fill(part):
+        if part == 0:
+            line.begin()
+        else:
+            line.go_on()
+
+    first, second = run_pieces(exchange, input_order(groups), work, product, fill)
     for index, piece in second:
         work(index, piece, exchange.total(index, piece))
-    outward = [place for place in second if place[1] == 0] + first
-    outward += [place for place in second if place[1] > 0]
-    for index, piece in outward:
+    here_first = [place for place in second if place[1] == 0]
+    late = [place for place in second if place[1] > 0]
+    line.hop(1)
+    for index, piece in here_first + first:
         share(index, piece)
-    for index, piece in outward:
+    for index, piece in here_first:
         exchange.forward(index, target(piece))
+    for time in range(2, groups - 1):
+        line.hop(time)
+    for index, piece in late:
+        share(index, piece)
+    for index, piece in first + late:
+        exchange.forward(index, target(piece))
+    line.end(block_out)
     exchange.finish(groups)
     for copy in small:
         copy.wait()
@@ -777,26 +904,40 @@
     )
 
 
-def input_gradient(left, weight, grad, small, members, parts, ident):
+def input_gradient(left, weight, grad, small, part, members, parts, ident):
     groups, piece, width = grad.shape
     depth = left.shape[-1]
     if parts != 4:
+        summed = lax.psum_scatter(part, "seq", scatter_dimension=0, tiled=True).astype(F32)
         part = over_cols(left, weight[:, :depth]).astype(BF)
         total = lax.psum_scatter(part, "mp", scatter_dimension=0, tiled=True).astype(F32)
         ready = (total.reshape(grad.shape) + grad).astype(BF)
         back = jnp.stack(swap_blocks(ready, members, -1))
         back = jnp.roll(back, lax.axis_index("seq") // (members // groups), axis=0)
-        return lax.all_gather(back, "mp", axis=1), lax.all_to_all(small, "seq", 0, 0)
+        return lax.all_gather(back, "mp", axis=1), lax.all_to_all(small, "seq", 0, 0), summed
+    per = members // groups
+    block = (part.shape[0] // members, part.shape[1])
     return exchange_call(
         functools.partial(input_kernel, groups, members // groups),
         ident,
-        (left.reshape(2, parts, groups // 2, piece, depth), weight, grad, small),
-        [((groups, parts, piece, width), BF, ANY), (small.shape, F32, VMEM)],
+        (left.reshape(2, parts, groups // 2, piece, depth), weight, grad, small, part.reshape(groups, per, *block)),
+        [
+            ((groups, parts, piece, width), BF, ANY),
+            (small.shape, F32, VMEM),
+            (block, F32, VMEM),
+        ],
         (groups, piece, width),
         [pltpu.VMEM((groups, piece, width), BF)] * 2
-        + product_scratch(parts, groups, piece, width, depth, True),
+        + product_scratch(parts, groups, piece, width, depth, True)
+        + [
+            pltpu.VMEM((groups, *block), BF),
+            pltpu.VMEM((groups, *block), BF),
+            pltpu.VMEM((2, groups - 1, *block), BF),
+        ]
+        + [pltpu.SemaphoreType.DMA((2 * groups,))] * 2
+        + [pltpu.SemaphoreType.DMA((groups,))] * 3,
         groups + members,
-        (1,),
+        (1, 4),
     )
 
 
@@ -1295,11 +1436,11 @@
 
 
 def last_kernel(
-    per, turned_hbm, query_ref, key_ref, value_ref, in_ref, proj_hbm, layer_hbm, layer_more_hbm,
-    grad_ref, sums_ref, part_ref, layer_ref, turned_ref, made, proj, layer, load_sem, put_sem,
+    per, turned_hbm, query_ref, key_ref, value_ref, in_ref, layer_hbm, layer_more_hbm,
+    grad_ref, sums_ref, part_ref, layer_ref, turned_ref, made, layer, load_sem, put_sem,
 ):
     rows, cols = query_ref.shape
-    count = load_sem.shape[0] - 3
+    count = load_sem.shape[0] - 2
     step = turned_ref.shape[0] // count
     loads = []
     for place in range(count):
@@ -1307,11 +1448,10 @@
         loads.append(
             pltpu.make_async_copy(turned_hbm.at[block], turned_ref.at[block], load_sem.at[place])
         )
-    loads.append(pltpu.make_async_copy(proj_hbm, proj, load_sem.at[count]))
     groups = layer.shape[0]
     for place, source in enumerate((layer_hbm, layer_more_hbm)):
         block = pl.ds(place * (groups // 2), groups // 2)
-        loads.append(pltpu.make_async_copy(source, layer.at[block], load_sem.at[count + 1 + place]))
+        loads.append(pltpu.make_async_copy(source, layer.at[block], load_sem.at[count + place]))
     for copy in loads:
         copy.start()
     puts = []
@@ -1338,9 +1478,7 @@
             made[index, block] = matmul(turned_ref[block], grad_ref[:, span]).astype(BF)
         put(made.at[index], part_ref.at[:, span])
         if index == 1:
-            loads[count].wait()
-            put(proj, part_ref.at[:, pl.ds(3 * cols, cols)])
-            for copy in loads[count + 1 :]:
+            for copy in loads[count:]:
                 copy.wait()
             group = lax.axis_index("seq") // per
             for piece in range(groups):
@@ -1349,7 +1487,7 @@
         copy.wait()
 
 
-def last_gradients(turned, query, key, value, arrived, proj_part, layer, layer_more, per):
+def last_gradients(turned, query, key, value, arrived, layer, layer_more, per):
     rows, cols = query.shape
     width = turned.shape[0]
     return pl.pallas_call(
@@ -1357,25 +1495,24 @@
         out_shape=(
             jax.ShapeDtypeStruct((rows, 3 * cols), BF),
             jax.ShapeDtypeStruct((1, 3 * cols), F32),
-            jax.ShapeDtypeStruct((width, 4 * cols), BF),
+            jax.ShapeDtypeStruct((width, 3 * cols), BF),
             jax.ShapeDtypeStruct((2 * layer.shape[0],) + layer.shape[1:], layer.dtype),
         ),
-        in_specs=[ANY] + [VMEM] * 4 + [ANY] * 3,
+        in_specs=[ANY] + [VMEM] * 4 + [ANY] * 2,
         out_specs=(VMEM, VMEM, ANY, ANY),
         scratch_shapes=[
             pltpu.VMEM(turned.shape, BF),
             pltpu.VMEM((3, width, cols), BF),
-            pltpu.VMEM(proj_part.shape, BF),
             pltpu.VMEM((2 * layer.shape[0],) + layer.shape[1:], BF),
-            pltpu.SemaphoreType.DMA((7,)),
-            pltpu.SemaphoreType.DMA((4 + 2 * layer.shape[0],)),
+            pltpu.SemaphoreType.DMA((6,)),
+            pltpu.SemaphoreType.DMA((3 + 2 * layer.shape[0],)),
         ],
         compiler_params=pltpu.CompilerParams(vmem_limit_bytes=52 * MIB),
         cost_estimate=pl.CostEstimate(
             flops=6 * rows * width * cols, bytes_accessed=32 * MIB, transcendentals=0
         ),
         name="last_gradients",
-    )(turned, query, key, value, arrived, proj_part, layer, layer_more)
+    )(turned, query, key, value, arrived, layer, layer_more)
 
 
 def packed(vectors, lines):
@@ -1575,7 +1712,6 @@
             key_grad,
             value_grad,
             others[0],
-            proj_w_part,
             layer_out,
             others[1],
             per,
@@ -1585,7 +1721,7 @@
         key_grad = to_group_members(key_grad, blocks_of(others[0]), members, per)
         value_grad = to_group_members(value_grad, blocks_of(others[1]), members, per)
         qkv_grad = jnp.concatenate([query_grad, key_grad.astype(BF), value_grad.astype(BF)], axis=1)
-        last_w_part = jnp.concatenate([matmul(x_turned, qkv_grad).astype(BF), proj_w_part], axis=1)
+        last_w_part = matmul(x_turned, qkv_grad).astype(BF)
         bias_grad = jnp.sum(qkv_grad.astype(F32), axis=0)
     last_w_grad = lax.psum_scatter(last_w_part, "seq", scatter_dimension=0, tiled=True).astype(F32)
     small = jnp.concatenate(
@@ -1598,11 +1734,12 @@
         axis=1,
     )
     small = jnp.pad(small, ((0, 0), (0, lines * 128 - small.shape[1])))
-    input_grad, small = input_gradient(
+    input_grad, small, proj_w_grad = input_gradient(
         qkv_grad,
         first,
         attn_grad,
         small.reshape(members, lines, 128),
+        proj_w_part,
         members,
         parts,
         6,
@@ -1623,7 +1760,7 @@
         last_w_grad[:, cols : 2 * cols],
         last_w_grad[:, 2 * cols : 3 * cols],
         pieces[1],
-        last_w_grad[:, 3 * cols :].T,
+        proj_w_grad.T,
         pieces[3],
         pieces[4],
         pieces[5],

time: 660 us -> 652 us (0.988)
  waiting for transfers between devices: 27.1 us -> 3.8 us
  Pallas kernels: 532 us -> 546 us
    reduce_scatter x1, waiting for transfers between devices: 23.3 us -> 0.08 us  [on_device(): lax.psum_scatter(last_w_part, 'seq', scatter_dimension=0, tiled=True)]
    pallas_call x5, Pallas kernels: 329 us -> 344 us  [exchange_call(): pl.pallas_call(kernel, out_shape=tuple((jax.ShapeDtypeStruct(shape, dtype...]
  transfers between devices with their start and end apart: 7 -> 7, of which waited for: 3 -> 3; matrix products, arithmetic and copies ran while one was open for 10% -> 11% of each run, Pallas kernels for 71% -> 75%
where the time goes in v7:
time: 652 us; the launch traced here: 642 us
  Pallas kernels  546 us (84%)
  matrix products  44.4 us (7%)
  other arithmetic  17.7 us (3%)
  between operations  14.9 us (2%)
  local copies, waits for them, and re-layouts  13.5 us (2%)
    pallas_call x5, Pallas kernels, exchange_call(): pl.pallas_call(kernel, out_shape=tuple((jax.ShapeDtypeStruct(shape, dtype...  344 us
    pallas_call x1, Pallas kernels, swap_groups(): pl.pallas_call(functools.partial(swap_kernel, groups, per, sign), out_sha...  59.3 us
    pallas_call x1, Pallas kernels, attend_back(): pl.pallas_call(functools.partial(attend_back_kernel, pieces, step), grid=...  40.3 us
    pallas_call x1, Pallas kernels, share_over_mp(): pl.pallas_call(share_kernel, out_shape=jax.ShapeDtypeStruct((2, parts, ow...  36.9 us
    dot_general x3, matrix products, matmul(): return jnp.dot(left, right, preferred_element_type=F32)  32.3 us
    pallas_call x1, Pallas kernels, feed_back(): pl.pallas_call(functools.partial(feed_back_kernel, pieces, members), grid...  30 us
    pallas_call x1, Pallas kernels, attend(): pl.pallas_call(attend_kernel, grid=(heads, rows // block), out_shape=(jax...  20.9 us
    pallas_call x1, Pallas kernels, last_gradients(): pl.pallas_call(functools.partial(last_kernel, per), out_shape=(jax.ShapeD...  14.7 us
  transfers between devices with their start and end apart: 7, of which 3 were waited for; matrix products, arithmetic and copies ran while one was open for 11% of the time, Pallas kernels for 75%

profile of v7, /device:TPU:9, one launch (start us, length us, event | category | flops | bytes accessed | tf_op | source)
XLA Modules:
  0.0 642.2 jit_solution(9976265346359354345)
XLA Ops:
  7.3 1.2 copy.34
  8.5 2.2 pad_maximum_fusion.1
  11.6 1.3 maximum_maximum_fusion
  12.9 0.8 slice.186
  14.1 1.7 constant_dynamic-slice_fusion.3
  15.8 1.1 pad_maximum_fusion.block_ref
  17.5 59.3 %swap_groups_1.1 = (bf16[4,64,2048]{2,1,0:T(8,128)(2,1)}, bf16[8,16,128]{2,1,0:T(8,128)(2,1)}) custom-call(bf16[4,64,2048]{2,1,0:T(8,128)(2,1)} %pad_maximum_fusion.block_ref, bf16[8,16,128]{2,1,0:T(8,128)(2,1)} %broadcast_in_dim.12.small_ref), custom_call_target="tpu_custom_call" | custom-call | bytes 62914560 | tf_op jit(solution)/shard_map/swap_groups_1/pallas_call | solution.py:1043
  77.8 36.9 %share_over_mp_8.1 = bf16[2,4,128,2048]{3,2,1,0:T(8,128)(2,1)} custom-call(bf16[256,2048]{1,0:T(8,128)(2,1)} %bitcast.86), custom_call_target="tpu_custom_call" | custom-call | bytes 104857600 | tf_op jit(solution)/shard_map/share_over_mp_8/pallas_call | solution.py:978
  114.7 10.0 %add_convert_fusion.query_ref.key_ref.value_ref = bf16[1024,1536]{1,0:T(8,128)(2,1)S(1)} fusion(bf16[1024,2048]{1,0:T(8,128)(2,1)} %bitcast.78, bf16[2048,2048]{1,0:T(8,128)(2,1)} %all-gather.4.cloned.1.call-done.weight_ref, f32[1536]{0:T(1024)S(1)} %pad_maximum_fusion.4), kind=kOutput, calls=%fused_computation.13 | convolution fusion | flops 6445596672 | bytes 13637632 | tf_op jit(solution)/shard_map/dot_general | solution.py:22
  125.0 1.3 collective-permute-start
  127.9 1.2 pad_maximum_fusion.2.cotan_ref
  129.0 1.2 collective-permute-done.key_far_ref.value_far_ref
  130.2 20.9 %attend.1 = (f32[1024,512]{1,0:T(8,128)}, bf16[1024,512]{1,0:T(8,128)(2,1)S(1)}, f32[4,1,1024]{2,1,0:T(1,128)S(1)}) custom-call(bf16[1024,1536]{1,0:T(8,128)(2,1)} %copy-done, bf16[1024,1536]{1,0:T(8,128)(2,1)} %copy-done, bf16[1024,1536]{1,0:T(8,128)(2,1)} %copy-done, bf16[1024,1024]{1,0:T(8,128)(2,1)} %collective-permute-done.key_far_ref.value_far_ref, ...), custom_call_target="tpu_custom_call" | custom-call | flops 8589934592 | bytes 10485760 | tf_op jit(solution)/shard_map/attend/pallas_call | solution.py:1104
  151.1 6.0 convolution_convert_fusion
  157.1 76.4 %exchange_2.1 = (bf16[2,4,2,64,2048]{4,3,2,1,0:T(8,128)(2,1)}, f32[4,64,2048]{2,1,0:T(8,128)}, f32[4,64,1]{2,1,0:T(8,128)}, bf16[2048,1024]{1,0:T(8,128)(2,1)}) custom-call(bf16[2,4,2,64,2048]{4,3,2,1,0:T(8,128)(2,1)} %bitcast.87, bf16[4,64,2048]{2,1,0:T(8,128)(2,1)} %get-tuple-element.58.x_ref, bf16[1024,2048]{1,0:T(8,128)(2,1)} %bitcast.79, ...), custom_call_target="tpu_custom_call" | custom-call | bytes 209715200 | tf_op jit(solution)/shard_map/exchange_2/pallas_call | solution.py:747
  233.6 17.3 %fusion.7 = (bf16[1024,2048]{1,0:T(8,128)(2,1)}, f32[1024,2048]{1,0:T(8,128)}) fusion(f32[2048]{0:T(1024)S(1)} %bitcast.109, bf16[1024,2048]{1,0:T(8,128)(2,1)} %bitcast.83, bf16[2048,3072]{1,0:T(8,128)(2,1)} %all-gather.6.cloned.1.call-done.weight_ref), kind=kOutput, calls=%fused_computation.8 | convolution fusion | flops 8610906112 | bytes 25174016 | tf_op jit(solution)/shard_map/dot_general | solution.py:22
  250.9 27.5 %exchange_13.1 = (f32[4,64,1024]{2,1,0:T(8,128)}, bf16[2048,1024]{1,0:T(8,128)(2,1)}, bf16[1024,2048]{1,0:T(8,128)(2,1)}, bf16[2048,1024]{1,0:T(8,128)(2,1)}) custom-call(bf16[2,4,2,64,2048]{4,3,2,1,0:T(8,128)(2,1)} %bitcast.80, bf16[2048,3072]{1,0:T(8,128)(2,1)} %all-gather.6.cloned.1.call-done.weight_ref, bf16[1024,2048]{1,0:T(8,128)(2,1)} %bitcast.84), custom_call_target="tpu_custom_call" | custom-call | bytes 209715200 | tf_op jit(solution)/shard_map/exchange_13/pallas_call | solution.py:747
  278.4 2.3 all-gather.8.cloned.1.call-done.weight_ref.more_ref
  280.7 67.7 %exchange_3.1 = (bf16[2,4,2,64,2048]{4,3,2,1,0:T(8,128)(2,1)}, f32[4,64,2048]{2,1,0:T(8,128)}, bf16[4,64,2048]{2,1,0:T(8,128)(2,1)}, f32[8,2048]{1,0:T(8,128)}, bf16[2048,2048]{1,0:T(8,128)(2,1)}) custom-call(bf16[2,4,2,64,2048]{4,3,2,1,0:T(8,128)(2,1)} %bitcast.81, bf16[1024,2048]{1,0:T(8,128)(2,1)} %all-gather.8.cloned.1.call-done.weight_ref.more_ref, ...), custom_call_target="tpu_custom_call" | custom-call | bytes 209715200 | tf_op jit(solution)/shard_map/exchange_3/pallas_call | solution.py:747
  348.5 30.0 %feed_back.1 = (bf16[1024,2048]{1,0:T(8,128)(2,1)}, f32[1,2048]{1,0:T(1,128)}, bf16[2048,2048]{1,0:T(8,128)(2,1)}, bf16[2,4,64,2048]{3,2,1,0:T(8,128)(2,1)}) custom-call(bf16[1024,2048]{1,0:T(8,128)(2,1)} %bitcast.110, bf16[1024,2048]{1,0:T(8,128)(2,1)} %get-tuple-element.67.weight_ref, bf16[1024,2048]{1,0:T(8,128)(2,1)} %all-gather.8.cloned.1.call-done.weight_ref.more_ref, ...), custom_call_target="tpu_custom_call" | custom-call | flops 17179869184 | bytes 41943040 | tf_op jit(solution)/shard_map/feed_back/pallas_call | solution.py:1213
  378.5 77.6 %exchange_4.1 = (bf16[2,4,2,64,2048]{4,3,2,1,0:T(8,128)(2,1)}, f32[4,64,2048]{2,1,0:T(8,128)}, f32[4,8,2048]{2,1,0:T(8,128)}) custom-call(bf16[2,4,2,64,2048]{4,3,2,1,0:T(8,128)(2,1)} %bitcast.82, bf16[2048,3072]{1,0:T(8,128)(2,1)} %all-gather.6.cloned.1.call-done.weight_ref, f32[4,64,2048]{2,1,0:T(8,128)} %get-tuple-element.71.grad_ref, ...), custom_call_target="tpu_custom_call" | custom-call | bytes 209715200 | tf_op jit(solution)/shard_map/exchange_4/pallas_call | solution.py:747
  456.2 6.1 convolution_convert_fusion.1
  462.4 5.0 fusion.20.grad_ref
  467.3 40.3 %attend_back.1 = (bf16[1024,512]{1,0:T(8,128)(2,1)S(1)}, f32[1024,512]{1,0:T(8,128)}, f32[1024,512]{1,0:T(8,128)}, bf16[2,4,1024,128]{3,2,1,0:T(8,128)(2,1)}, bf16[2,4,64,2048]{3,2,1,0:T(8,128)(2,1)}) custom-call(bf16[1024,1536]{1,0:T(8,128)(2,1)} %copy-done, bf16[1024,1536]{1,0:T(8,128)(2,1)} %copy-done, bf16[1024,1536]{1,0:T(8,128)(2,1)} %copy-done, ...), custom_call_target="tpu_custom_call" | custom-call | flops 21474836480 | bytes 15728640 | tf_op jit(solution)/shard_map/attend_back/pallas_call | solution.py:1358
  507.6 14.7 %last_gradients.1 = (bf16[1024,1536]{1,0:T(8,128)(2,1)}, f32[1,1536]{1,0:T(1,128)S(1)}, bf16[2048,1536]{1,0:T(8,128)(2,1)}, bf16[4,4,64,2048]{3,2,1,0:T(8,128)(2,1)}) custom-call(bf16[2048,1024]{1,0:T(8,128)(2,1)} %get-tuple-element.61.turned_hbm, bf16[1024,512]{1,0:T(8,128)(2,1)S(1)} %get-tuple-element.82.query_ref, f32[1024,512]{1,0:T(8,128)} %get-tuple-element.83.key_ref, ...), custom_call_target="tpu_custom_call" | custom-call | flops 6442450944 | bytes 33554432 | tf_op jit(solution)/shard_map/last_gradients/pallas_call | solution.py:1493
  522.4 0.9 copy-done.6
  525.6 95.0 %exchange_6.1 = (bf16[4,4,64,2048]{3,2,1,0:T(8,128)(2,1)}, f32[8,16,128]{2,1,0:T(8,128)}, f32[256,512]{1,0:T(8,128)}) custom-call(bf16[2,4,2,64,1536]{4,3,2,1,0:T(8,128)(2,1)} %bitcast.90, bf16[2048,2048]{1,0:T(8,128)(2,1)} %all-gather.4.cloned.1.call-done.weight_ref, f32[4,64,2048]{2,1,0:T(8,128)} %get-tuple-element.90.grad_ref, f32[8,16,128]{2,1,0:T(8,128)} %bitcast.94, ...), custom_call_target="tpu_custom_call" | custom-call | bytes 209715200 | tf_op jit(solution)/shard_map/exchange_6/pallas_call | solution.py:747
  620.7 6.8 %convert.2 = f32[2,2,256,2048]{3,2,1,0:T(8,128)} convert(bf16[2,2,256,2048]{3,2,1,0:T(8,128)(2,1)} %bitcast.85) | non-fusion elementwise | flops 2097152 | bytes 12582912 | tf_op jit(solution)/shard_map/reshape | solution.py:1747
  627.5 1.0 copy.36
  628.5 1.6 convert_element_type.43
  630.1 1.5 convert_element_type.44
  632.8 2.3 fusion.24
  (99 shorter events, 8.2 us)
Async XLA Ops:
  7.2 3.6 copy-start.4
  7.2 4.4 copy-start.1
  7.2 107.5 %all-gather.4.cloned.1.call-start = ((), (), s32[]{:S(2)}) async-start(), calls=%async_computation.3 | async-start | bytes 9437184 | tf_op jit(solution)/shard_map/all_gather | solution.py:1560
  10.7 222.9 %all-gather.6.cloned.1.call-start = ((), (), s32[]{:S(2)}) async-start(), calls=%async_computation.4 | async-start | bytes 14155776 | tf_op jit(solution)/shard_map/all_gather | solution.py:1570
  11.4 2.5 copy-start.10
  11.4 2.5 copy-start.11
  11.5 2.5 copy-start.12
  11.5 2.5 copy-start.13
  11.5 2.5 copy-start.14
  11.5 2.5 copy-start.15
  11.5 2.5 copy-start.16
  11.5 2.5 copy-start.17
  11.5 2.5 copy-start.18
  12.9 267.9 %all-gather.8.cloned.1.call-start = ((), (), s32[]{:S(2)}) async-start(), calls=%async_computation.5 | async-start | bytes 4718592 | tf_op jit(solution)/shard_map/all_gather | solution.py:1572
  13.8 442.4 %reduce-scatter.4.cloned.1.call-start = ((), (), s32[]{:S(2)}) async-start(), calls=%async_computation.6 | async-start | bytes 9437184 | tf_op jit(solution)/shard_map/reduce_scatter | solution.py:1662
  124.8 1.6 copy-start
  125.0 5.2 collective-permute-start
  126.4 24.7 %copy-start.7 = (f32[1,1,8,256]{3,1,2,0:T(1,128)}, f32[1,1,8,256]{3,1,2,0:T(1,128)S(1)}, u32[]{:S(2)}) copy-start(f32[1,1,8,256]{3,1,2,0:T(1,128)S(1)} %copy.39) | copy-start | bytes 24580
  348.5 272.2 %reduce-scatter.6.cloned.1.call-start = ((), (), s32[]{:S(2)}) async-start(), calls=%async_computation.7 | async-start | bytes 9437184 | tf_op jit(solution)/shard_map/reduce_scatter | solution.py:1684
  378.5 254.3 %reduce-scatter.8.cloned.1.call-start = ((), (), s32[]{:S(2)}) async-start(), calls=%async_computation.8 | async-start | bytes 7077888 | tf_op jit(solution)/shard_map/reduce_scatter | solution.py:1726
  456.2 6.1 copy-start.19
  522.3 1.0 copy-start.6
  522.4 1.7 copy-start.9
  620.6 6.9 %copy-start.5 = (f32[256,512]{1,0:T(8,128)S(1)}, f32[256,512]{1,0:T(8,128)}, u32[]{:S(2)}) copy-start(f32[256,512]{1,0:T(8,128)} %get-tuple-element.98) | copy-start | bytes 1572868
  620.6 7.9 %copy-start.8 = (f32[8,16,128]{2,1,0:T(8,128)S(1)}, f32[8,16,128]{2,1,0:T(8,128)}, u32[]{:S(2)}) copy-start(f32[8,16,128]{2,1,0:T(8,128)} %get-tuple-element.97) | copy-start | bytes 196612
  620.6 7.9 %copy-start.3 = (bf16[256,2048]{1,0:T(8,128)(2,1)S(1)}, bf16[256,2048]{1,0:T(8,128)(2,1)}, u32[]{:S(2)}) copy-start(bf16[256,2048]{1,0:T(8,128)(2,1)} %reduce-scatter.6.cloned.1.call-done) | copy-start | bytes 3145732
  627.5 2.6 copy-start.2
Sparse Core Ops, SparseCore 0:
  10.8 101.0 all-gather.3
  114.2 117.4 all-gather.5
  233.9 46.8 all-gather.7
  348.6 88.6 reduce-scatter.3
  439.4 87.7 reduce-scatter.5
  529.4 103.3 reduce-scatter.7

commit v8 on v7

--- a/solution.py
+++ b/solution.py
@@ -413,9 +413,7 @@
         ready[index] = grad.astype(BF)
         exchange.share(index, ready.at[index], target(piece))
         keep(ready.at[index], target(piece)(exchange.me), index)
-        sums_ref[0:1] += jnp.sum(grad, axis=0, keepdims=True)
-        sums_ref[1:2] += jnp.sum(cotan * normal, axis=0, keepdims=True)
-        sums_ref[2:3] += jnp.sum(cotan, axis=0, keepdims=True)
+        normal_ref[piece] = normal
         outward.append(moved(grad_ref.at[piece], grad_hbm.at[piece], out_sem.at[2 + index]))
 
     first, second = run_pieces(exchange, range(groups), work, product)
@@ -451,6 +449,12 @@
         def _(index):
             span = columns(index)
             whole[:, span] = product_of(0, span).astype(BF)
+
+    for _, piece in first + second:
+        cotan = cotan_in[piece].astype(F32)
+        sums_ref[0:1] += jnp.sum(grad_ref[piece], axis=0, keepdims=True)
+        sums_ref[1:2] += jnp.sum(cotan * normal_ref[piece], axis=0, keepdims=True)
+        sums_ref[2:3] += jnp.sum(cotan, axis=0, keepdims=True)
 
     share_out = count // (2 * len(second))
     done = count // 2

time: 652 us -> 652 us (level)
  no operation moved by 1% of the time
where the time goes in v8:
time: 652 us; the launch traced here: 642 us
  Pallas kernels  546 us (84%)
  matrix products  44.4 us (7%)
  other arithmetic  17.7 us (3%)
  between operations  14.9 us (2%)
  local copies, waits for them, and re-layouts  13.5 us (2%)
    pallas_call x5, Pallas kernels, exchange_call(): pl.pallas_call(kernel, out_shape=tuple((jax.ShapeDtypeStruct(shape, dtype...  344 us
    pallas_call x1, Pallas kernels, swap_groups(): pl.pallas_call(functools.partial(swap_kernel, groups, per, sign), out_sha...  59.3 us
    pallas_call x1, Pallas kernels, attend_back(): pl.pallas_call(functools.partial(attend_back_kernel, pieces, step), grid=...  40.3 us
    pallas_call x1, Pallas kernels, share_over_mp(): pl.pallas_call(share_kernel, out_shape=jax.ShapeDtypeStruct((2, parts, ow...  36.9 us
    dot_general x3, matrix products, matmul(): return jnp.dot(left, right, preferred_element_type=F32)  32.3 us
    pallas_call x1, Pallas kernels, feed_back(): pl.pallas_call(functools.partial(feed_back_kernel, pieces, members), grid...  30 us
    pallas_call x1, Pallas kernels, attend(): pl.pallas_call(attend_kernel, grid=(heads, rows // block), out_shape=(jax...  20.9 us
    pallas_call x1, Pallas kernels, last_gradients(): pl.pallas_call(functools.partial(last_kernel, per), out_shape=(jax.ShapeD...  14.7 us
  transfers between devices with their start and end apart: 7, of which 3 were waited for; matrix products, arithmetic and copies ran while one was open for 11% of the time, Pallas kernels for 75%

profile of v8, /device:TPU:9, one launch (start us, length us, event | category | flops | bytes accessed | tf_op | source)
XLA Modules:
  0.0 642.2 jit_solution(8828619411469060839)
XLA Ops:
  7.3 1.2 copy.34
  8.5 2.2 pad_maximum_fusion.1
  11.6 1.3 maximum_maximum_fusion
  12.9 0.8 slice.186
  14.1 1.7 constant_dynamic-slice_fusion.3
  15.8 1.1 pad_maximum_fusion.block_ref
  17.5 59.3 %swap_groups_1.1 = (bf16[4,64,2048]{2,1,0:T(8,128)(2,1)}, bf16[8,16,128]{2,1,0:T(8,128)(2,1)}) custom-call(bf16[4,64,2048]{2,1,0:T(8,128)(2,1)} %pad_maximum_fusion.block_ref, bf16[8,16,128]{2,1,0:T(8,128)(2,1)} %broadcast_in_dim.12.small_ref), custom_call_target="tpu_custom_call" | custom-call | bytes 62914560 | tf_op jit(solution)/shard_map/swap_groups_1/pallas_call | solution.py:1047
  77.8 36.9 %share_over_mp_8.1 = bf16[2,4,128,2048]{3,2,1,0:T(8,128)(2,1)} custom-call(bf16[256,2048]{1,0:T(8,128)(2,1)} %bitcast.86), custom_call_target="tpu_custom_call" | custom-call | bytes 104857600 | tf_op jit(solution)/shard_map/share_over_mp_8/pallas_call | solution.py:982
  114.7 10.0 %add_convert_fusion.query_ref.key_ref.value_ref = bf16[1024,1536]{1,0:T(8,128)(2,1)S(1)} fusion(bf16[1024,2048]{1,0:T(8,128)(2,1)} %bitcast.78, bf16[2048,2048]{1,0:T(8,128)(2,1)} %all-gather.4.cloned.1.call-done.weight_ref, f32[1536]{0:T(1024)S(1)} %pad_maximum_fusion.4), kind=kOutput, calls=%fused_computation.13 | convolution fusion | flops 6445596672 | bytes 13637632 | tf_op jit(solution)/shard_map/dot_general | solution.py:22
  125.0 1.3 collective-permute-start
  127.9 1.2 pad_maximum_fusion.2.cotan_ref
  129.0 1.2 collective-permute-done.key_far_ref.value_far_ref
  130.2 20.9 %attend.1 = (f32[1024,512]{1,0:T(8,128)}, bf16[1024,512]{1,0:T(8,128)(2,1)S(1)}, f32[4,1,1024]{2,1,0:T(1,128)S(1)}) custom-call(bf16[1024,1536]{1,0:T(8,128)(2,1)} %copy-done, bf16[1024,1536]{1,0:T(8,128)(2,1)} %copy-done, bf16[1024,1536]{1,0:T(8,128)(2,1)} %copy-done, bf16[1024,1024]{1,0:T(8,128)(2,1)} %collective-permute-done.key_far_ref.value_far_ref, ...), custom_call_target="tpu_custom_call" | custom-call | flops 8589934592 | bytes 10485760 | tf_op jit(solution)/shard_map/attend/pallas_call | solution.py:1108
  151.1 6.0 convolution_convert_fusion
  157.1 76.4 %exchange_2.1 = (bf16[2,4,2,64,2048]{4,3,2,1,0:T(8,128)(2,1)}, f32[4,64,2048]{2,1,0:T(8,128)}, f32[4,64,1]{2,1,0:T(8,128)}, bf16[2048,1024]{1,0:T(8,128)(2,1)}) custom-call(bf16[2,4,2,64,2048]{4,3,2,1,0:T(8,128)(2,1)} %bitcast.87, bf16[4,64,2048]{2,1,0:T(8,128)(2,1)} %get-tuple-element.58.x_ref, bf16[1024,2048]{1,0:T(8,128)(2,1)} %bitcast.79, ...), custom_call_target="tpu_custom_call" | custom-call | bytes 209715200 | tf_op jit(solution)/shard_map/exchange_2/pallas_call | solution.py:751
  233.6 17.3 %fusion.7 = (bf16[1024,2048]{1,0:T(8,128)(2,1)}, f32[1024,2048]{1,0:T(8,128)}) fusion(f32[2048]{0:T(1024)S(1)} %bitcast.109, bf16[1024,2048]{1,0:T(8,128)(2,1)} %bitcast.83, bf16[2048,3072]{1,0:T(8,128)(2,1)} %all-gather.6.cloned.1.call-done.weight_ref), kind=kOutput, calls=%fused_computation.8 | convolution fusion | flops 8610906112 | bytes 25174016 | tf_op jit(solution)/shard_map/dot_general | solution.py:22
  250.9 27.5 %exchange_13.1 = (f32[4,64,1024]{2,1,0:T(8,128)}, bf16[2048,1024]{1,0:T(8,128)(2,1)}, bf16[1024,2048]{1,0:T(8,128)(2,1)}, bf16[2048,1024]{1,0:T(8,128)(2,1)}) custom-call(bf16[2,4,2,64,2048]{4,3,2,1,0:T(8,128)(2,1)} %bitcast.80, bf16[2048,3072]{1,0:T(8,128)(2,1)} %all-gather.6.cloned.1.call-done.weight_ref, bf16[1024,2048]{1,0:T(8,128)(2,1)} %bitcast.84), custom_call_target="tpu_custom_call" | custom-call | bytes 209715200 | tf_op jit(solution)/shard_map/exchange_13/pallas_call | solution.py:751
  278.4 2.3 all-gather.8.cloned.1.call-done.weight_ref.more_ref
  280.7 67.7 %exchange_3.1 = (bf16[2,4,2,64,2048]{4,3,2,1,0:T(8,128)(2,1)}, f32[4,64,2048]{2,1,0:T(8,128)}, bf16[4,64,2048]{2,1,0:T(8,128)(2,1)}, f32[8,2048]{1,0:T(8,128)}, bf16[2048,2048]{1,0:T(8,128)(2,1)}) custom-call(bf16[2,4,2,64,2048]{4,3,2,1,0:T(8,128)(2,1)} %bitcast.81, bf16[1024,2048]{1,0:T(8,128)(2,1)} %all-gather.8.cloned.1.call-done.weight_ref.more_ref, ...), custom_call_target="tpu_custom_call" | custom-call | bytes 209715200 | tf_op jit(solution)/shard_map/exchange_3/pallas_call | solution.py:751
  348.5 30.0 %feed_back.1 = (bf16[1024,2048]{1,0:T(8,128)(2,1)}, f32[1,2048]{1,0:T(1,128)}, bf16[2048,2048]{1,0:T(8,128)(2,1)}, bf16[2,4,64,2048]{3,2,1,0:T(8,128)(2,1)}) custom-call(bf16[1024,2048]{1,0:T(8,128)(2,1)} %bitcast.110, bf16[1024,2048]{1,0:T(8,128)(2,1)} %get-tuple-element.67.weight_ref, bf16[1024,2048]{1,0:T(8,128)(2,1)} %all-gather.8.cloned.1.call-done.weight_ref.more_ref, ...), custom_call_target="tpu_custom_call" | custom-call | flops 17179869184 | bytes 41943040 | tf_op jit(solution)/shard_map/feed_back/pallas_call | solution.py:1217
  378.5 77.6 %exchange_4.1 = (bf16[2,4,2,64,2048]{4,3,2,1,0:T(8,128)(2,1)}, f32[4,64,2048]{2,1,0:T(8,128)}, f32[4,8,2048]{2,1,0:T(8,128)}) custom-call(bf16[2,4,2,64,2048]{4,3,2,1,0:T(8,128)(2,1)} %bitcast.82, bf16[2048,3072]{1,0:T(8,128)(2,1)} %all-gather.6.cloned.1.call-done.weight_ref, f32[4,64,2048]{2,1,0:T(8,128)} %get-tuple-element.71.grad_ref, ...), custom_call_target="tpu_custom_call" | custom-call | bytes 209715200 | tf_op jit(solution)/shard_map/exchange_4/pallas_call | solution.py:751
  456.2 6.1 convolution_convert_fusion.1
  462.4 5.0 fusion.20.grad_ref
  467.3 40.3 %attend_back.1 = (bf16[1024,512]{1,0:T(8,128)(2,1)S(1)}, f32[1024,512]{1,0:T(8,128)}, f32[1024,512]{1,0:T(8,128)}, bf16[2,4,1024,128]{3,2,1,0:T(8,128)(2,1)}, bf16[2,4,64,2048]{3,2,1,0:T(8,128)(2,1)}) custom-call(bf16[1024,1536]{1,0:T(8,128)(2,1)} %copy-done, bf16[1024,1536]{1,0:T(8,128)(2,1)} %copy-done, bf16[1024,1536]{1,0:T(8,128)(2,1)} %copy-done, ...), custom_call_target="tpu_custom_call" | custom-call | flops 21474836480 | bytes 15728640 | tf_op jit(solution)/shard_map/attend_back/pallas_call | solution.py:1362
  507.6 14.7 %last_gradients.1 = (bf16[1024,1536]{1,0:T(8,128)(2,1)}, f32[1,1536]{1,0:T(1,128)S(1)}, bf16[2048,1536]{1,0:T(8,128)(2,1)}, bf16[4,4,64,2048]{3,2,1,0:T(8,128)(2,1)}) custom-call(bf16[2048,1024]{1,0:T(8,128)(2,1)} %get-tuple-element.61.turned_hbm, bf16[1024,512]{1,0:T(8,128)(2,1)S(1)} %get-tuple-element.82.query_ref, f32[1024,512]{1,0:T(8,128)} %get-tuple-element.83.key_ref, ...), custom_call_target="tpu_custom_call" | custom-call | flops 6442450944 | bytes 33554432 | tf_op jit(solution)/shard_map/last_gradients/pallas_call | solution.py:1497
  522.4 0.9 copy-done.6
  525.6 95.0 %exchange_6.1 = (bf16[4,4,64,2048]{3,2,1,0:T(8,128)(2,1)}, f32[8,16,128]{2,1,0:T(8,128)}, f32[256,512]{1,0:T(8,128)}) custom-call(bf16[2,4,2,64,1536]{4,3,2,1,0:T(8,128)(2,1)} %bitcast.90, bf16[2048,2048]{1,0:T(8,128)(2,1)} %all-gather.4.cloned.1.call-done.weight_ref, f32[4,64,2048]{2,1,0:T(8,128)} %get-tuple-element.90.grad_ref, f32[8,16,128]{2,1,0:T(8,128)} %bitcast.94, ...), custom_call_target="tpu_custom_call" | custom-call | bytes 209715200 | tf_op jit(solution)/shard_map/exchange_6/pallas_call | solution.py:751
  620.7 6.8 %convert.2 = f32[2,2,256,2048]{3,2,1,0:T(8,128)} convert(bf16[2,2,256,2048]{3,2,1,0:T(8,128)(2,1)} %bitcast.85) | non-fusion elementwise | flops 2097152 | bytes 12582912 | tf_op jit(solution)/shard_map/reshape | solution.py:1751
  627.5 1.0 copy.36
  628.5 1.6 convert_element_type.43
  630.1 1.5 convert_element_type.44
  632.8 2.3 fusion.24
  (99 shorter events, 8.2 us)
Async XLA Ops:
  7.2 3.6 copy-start.4
  7.2 4.4 copy-start.1
  7.2 107.5 %all-gather.4.cloned.1.call-start = ((), (), s32[]{:S(2)}) async-start(), calls=%async_computation.3 | async-start | bytes 9437184 | tf_op jit(solution)/shard_map/all_gather | solution.py:1564
  10.7 222.9 %all-gather.6.cloned.1.call-start = ((), (), s32[]{:S(2)}) async-start(), calls=%async_computation.4 | async-start | bytes 14155776 | tf_op jit(solution)/shard_map/all_gather | solution.py:1574
  11.4 2.5 copy-start.10
  11.4 2.5 copy-start.11
  11.5 2.5 copy-start.12
  11.5 2.5 copy-start.13
  11.5 2.5 copy-start.14
  11.5 2.5 copy-start.15
  11.5 2.5 copy-start.16
  11.5 2.5 copy-start.17
  11.5 2.5 copy-start.18
  12.9 267.9 %all-gather.8.cloned.1.call-start = ((), (), s32[]{:S(2)}) async-start(), calls=%async_computation.5 | async-start | bytes 4718592 | tf_op jit(solution)/shard_map/all_gather | solution.py:1576
  13.8 442.4 %reduce-scatter.4.cloned.1.call-start = ((), (), s32[]{:S(2)}) async-start(), calls=%async_computation.6 | async-start | bytes 9437184 | tf_op jit(solution)/shard_map/reduce_scatter | solution.py:1666
  124.8 1.6 copy-start
  125.0 5.2 collective-permute-start
  126.4 24.7 %copy-start.7 = (f32[1,1,8,256]{3,1,2,0:T(1,128)}, f32[1,1,8,256]{3,1,2,0:T(1,128)S(1)}, u32[]{:S(2)}) copy-start(f32[1,1,8,256]{3,1,2,0:T(1,128)S(1)} %copy.39) | copy-start | bytes 24580
  348.5 272.2 %reduce-scatter.6.cloned.1.call-start = ((), (), s32[]{:S(2)}) async-start(), calls=%async_computation.7 | async-start | bytes 9437184 | tf_op jit(solution)/shard_map/reduce_scatter | solution.py:1688
  378.5 254.3 %reduce-scatter.8.cloned.1.call-start = ((), (), s32[]{:S(2)}) async-start(), calls=%async_computation.8 | async-start | bytes 7077888 | tf_op jit(solution)/shard_map/reduce_scatter | solution.py:1730
  456.2 6.1 copy-start.19
  522.3 1.0 copy-start.6
  522.4 1.7 copy-start.9
  620.6 6.9 %copy-start.5 = (f32[256,512]{1,0:T(8,128)S(1)}, f32[256,512]{1,0:T(8,128)}, u32[]{:S(2)}) copy-start(f32[256,512]{1,0:T(8,128)} %get-tuple-element.98) | copy-start | bytes 1572868
  620.6 7.9 %copy-start.8 = (f32[8,16,128]{2,1,0:T(8,128)S(1)}, f32[8,16,128]{2,1,0:T(8,128)}, u32[]{:S(2)}) copy-start(f32[8,16,128]{2,1,0:T(8,128)} %get-tuple-element.97) | copy-start | bytes 196612
  620.6 7.9 %copy-start.3 = (bf16[256,2048]{1,0:T(8,128)(2,1)S(1)}, bf16[256,2048]{1,0:T(8,128)(2,1)}, u32[]{:S(2)}) copy-start(bf16[256,2048]{1,0:T(8,128)(2,1)} %reduce-scatter.6.cloned.1.call-done) | copy-start | bytes 3145732
  627.5 2.6 copy-start.2
Sparse Core Ops, SparseCore 0:
  10.8 101.0 all-gather.3
  114.2 117.4 all-gather.5
  233.9 46.8 all-gather.7
  348.6 88.6 reduce-scatter.3
  439.4 87.7 reduce-scatter.5
  529.4 103.3 reduce-scatter.7
